TPU v7x, 32 devices: a whole 2x2x4 slice. The times are simulated.
32 devices in a mesh: groups: 2 (over y), grid: 8 (over z, x), depth: 2 (over core).
Axes of the slice: x: 2, y: 2, z: 4, core: 2. Of those that a mesh axis runs over, the one named last changes fastest.
Arguments:
- band_held: bfloat16 [2048, 4096], P('groups', 'grid'), parts along dimension 0, may hold values from -6 to 6
- inner_tiles: bfloat16 [6144, 4096], P(('groups', 'depth'), 'grid'), parts along dimension 0, may hold values from -0.109375 to 0.109375
- band_mask: int32 [4, 8], P('groups'), parts along dimension 0, may hold values 0 or 1
- inner_mask: int32 [12, 8], P(('groups', 'depth'), 'grid'), parts along dimension 0, may hold values 0 or 1
- held_col: int32 [16], P('groups'), parts along dimension 0, may hold values from 0 to 7, each once
Outputs:
- product: bfloat16 [2048, 4096], P(('groups', 'depth'), 'grid'), parts along dimension 0
There are 2 independent parts, one for each index of `groups`. A program takes and returns all parts, laid end to end along the dimension named above; each array names one. Nothing has to cross between parts.
Inputs may be any that keep to these rules, and one draw needn't show every extreme that they name: held_col holds every tile column once.
All inputs are finite; a program needn't handle non-finite values. No bound on the sum of `inner_mask` on one device may be relied on, other than what follows from the above.
Results may differ from a plain program's by a relative error of at most 0.001.
Values may be sent and summed in bfloat16 or wider, within the bound.
No kernel may reach another device: no remote copies, remote signals or barrier semaphores. Data moves between devices by JAX's collectives and lax.ppermute only.
A program may use at most 64 MiB of HBM per device.

v0:
```python
import jax
import jax.numpy as jnp
from jax import lax
from jax.sharding import PartitionSpec as P


def per_device(band_held, inner_tiles, band_mask, inner_mask, held_col):
    grid_size = lax.axis_size("grid")
    tile_size = band_held.shape[1]
    band_count = band_mask.shape[0]
    local_offsets = inner_mask.shape[0]
    depth_index = lax.axis_index("depth")
    column = lax.axis_index("grid")
    first_offset = depth_index * local_offsets
    right_flags = inner_mask[:, 0]
    row_count = band_count * tile_size
    col_order = jnp.arange(grid_size, dtype=jnp.int32)
    inverse = jnp.sum(
        jnp.where(held_col[None, :] == col_order[:, None], col_order[None, :], 0), axis=1
    )
    pieces = lax.all_to_all(
        band_held.reshape(row_count, 1, tile_size), "grid", split_axis=0, concat_axis=1, tiled=True
    )
    ordered = jnp.take(pieces, inverse, axis=1)
    padded = jnp.pad(ordered, ((0, 0), (local_offsets, local_offsets), (0, 0)))
    windows = jnp.stack(
        [
            lax.dynamic_slice_in_dim(padded, first_offset + offset, grid_size, 1)
            for offset in range(local_offsets)
        ],
        axis=2,
    )
    arrived = lax.all_to_all(windows, "grid", split_axis=1, concat_axis=0, tiled=True)
    arrived = arrived.reshape(row_count, local_offsets, tile_size)
    flags_pad = jnp.pad(band_mask, ((0, 0), (local_offsets, local_offsets)))
    keep_flags = (
        lax.dynamic_slice_in_dim(flags_pad, column + first_offset, local_offsets, 1)
        * right_flags[None, :]
    )
    keep_rows = jnp.repeat(keep_flags, tile_size, axis=0).astype(jnp.float32)
    summed = jnp.zeros((row_count, tile_size), jnp.float32)
    for offset in range(local_offsets):
        right_block = inner_tiles[offset * tile_size : (offset + 1) * tile_size]
        summed = (
            summed
            + jnp.dot(arrived[:, offset, :], right_block, preferred_element_type=jnp.float32)
            * keep_rows[:, offset : offset + 1]
        )
    summed = lax.psum_scatter(summed, "depth", scatter_dimension=0, tiled=True)
    return summed.astype(jnp.bfloat16)


def solution(mesh):
    placed = (
        P("groups", "grid"),
        P(("groups", "depth"), "grid"),
        P("groups", None),
        P(("groups", "depth"), "grid"),
        P("groups"),
    )
    return jax.shard_map(
        per_device,
        mesh=mesh,
        in_specs=placed,
        out_specs=P(("groups", "depth"), "grid"),
        check_vma=False,
    )
```

profile of v0, /device:TPU:0, one launch (start us, length us, event | category | flops | bytes accessed | tf_op | source)
XLA Modules:
  0.0 146.6 jit_solution(3072828780638455468)
XLA Ops:
  6.5 0.5 broadcast.47
  7.0 2.7 %reduce = bf16[1024,512]{1,0:T(8,128)(2,1)S(1)} reduce(bf16[1024,1,512]{2,0,1:T(8,128)(2,1)} %bitcast.45, bf16[]{:T(256)} %broadcast.47), dimensions={1}, to_apply=%copy.11.reduce_sub_computation | reduce | bytes 2097154 | tf_op jit(solution)/shard_map/reshape | solution.py:22
  9.7 0.0 copy-start.3
  9.7 1.6 %reshape.39 = bf16[8,2,32768]{2,1,0:T(2,128)(2,1)} reshape(bf16[1024,512]{1,0:T(8,128)(2,1)S(1)} %reduce) | data formatting | bytes 2097152
  11.3 7.3 %all-to-all-start = ((bf16[8,2,32768]{2,1,0:T(2,128)(2,1)}), bf16[8,2,32768]{2,1,0:T(2,128)(2,1)S(1)}, u32[]{:S(2)}, u32[]{:S(2)}) async-start(bf16[8,2,32768]{2,1,0:T(2,128)(2,1)} %reshape.39), calls=%async_computation | async-start | bytes 2097152 | tf_op jit(solution)/shard_map/all_to_all | solution.py:21
  18.6 0.0 copy-done.3
  18.6 0.1 select_reduce_fusion
  18.7 25.6 %all-to-all-done = bf16[8,2,32768]{2,1,0:T(2,128)(2,1)S(1)} async-done(((bf16[8,2,32768]{2,1,0:T(2,128)(2,1)}), bf16[8,2,32768]{2,1,0:T(2,128)(2,1)S(1)}, u32[]{:S(2)}, u32[]{:S(2)}) %all-to-all-start) | async-done | bytes 1048608 | tf_op jit(solution)/shard_map/all_to_all | solution.py:21
  44.3 1.0 reshape.40
  45.4 0.3 copy.14
  45.7 0.6 gather_fusion
  46.3 0.2 select_bitcast_fusion
  46.5 0.6 fusion
  47.1 2.0 %pad_maximum_fusion = bf16[128,8,3,512]{3,0,2,1:T(8,128)(2,1)} fusion(bf16[128,8,1,512]{3,0,2,1:T(8,128)(2,1)S(1)} %get-tuple-element.7, bf16[128,8,1,512]{3,0,2,1:T(8,128)(2,1)S(1)} %get-tuple-element.6, bf16[128,8,1,512]{3,0,2,1:T(8,128)(2,1)S(1)} %get-tuple-element.5), kind=kLoop, calls=%fused_computation.1 | loop fusion | flops 3145728 | bytes 6291456 | tf_op jit(solution)/shard_map/stack | solution.py:26
  49.1 0.0 copy-start.1
  49.1 0.0 copy-start.2
  49.1 3.8 %all-to-all-start.1 = ((bf16[128,8,3,512]{3,0,2,1:T(8,128)(2,1)}), bf16[128,8,3,512]{3,0,2,1:T(8,128)(2,1)S(1)}, u32[]{:S(2)}, u32[]{:S(2)}) async-start(bf16[128,8,3,512]{3,0,2,1:T(8,128)(2,1)} %pad_maximum_fusion), calls=%async_computation.1 | async-start | bytes 6291456 | tf_op jit(solution)/shard_map/all_to_all | solution.py:33
  52.9 0.0 reduce-scatter.2.cloned.1.call-start
  52.9 0.0 copy-done.1
  52.9 0.0 copy-done.2
  52.9 0.1 multiply_convert_fusion
  53.0 0.1 copy.13
  53.1 0.1 broadcast_bitcast_fusion
  53.2 70.5 %all-to-all-done.1 = bf16[128,8,3,512]{3,0,2,1:T(8,128)(2,1)S(1)} async-done(((bf16[128,8,3,512]{3,0,2,1:T(8,128)(2,1)}), bf16[128,8,3,512]{3,0,2,1:T(8,128)(2,1)S(1)}, u32[]{:S(2)}, u32[]{:S(2)}) %all-to-all-start.1) | async-done | bytes 3145760 | tf_op jit(solution)/shard_map/all_to_all | solution.py:33
  123.7 0.3 copy.12
  124.0 1.1 copy-done
  125.1 0.7 fusion.3
  125.8 0.7 fusion.4
  126.5 2.2 %multiply_add_fusion = f32[1024,512]{1,0:T(8,128)} fusion(f32[1024,512]{1,0:T(8,128)S(1)} %fusion.3, f32[1024,512]{1,0:T(8,128)S(1)} %fusion.4, bf16[1024,3,512]{2,0,1:T(8,128)(2,1)S(1)} %bitcast.43, f32[1024]{0:T(1024)S(1)} %bitcast.48, f32[1024]{0:T(1024)S(1)} %bitcast.49, f32[1024]{0:T(1024)S(1)} %bitcast.47, bf16[1536,512]{1,0:T(8,128)(2,1)S(1)} %copy-done), kind=kOutput, calls=%fused_computation.5 | convolution fusion | flops 539492352 | bytes 7876608 | tf_op jit(solution)/shard_map/dot_general | solution.py:46
  128.8 0.0 reduce-scatter.2.cloned.1.call-update
  128.8 8.8 %reduce-scatter.2.cloned.1.call-done = f32[512,512]{1,0:T(8,128)} async-done(((f32[1024,512]{1,0:T(8,128)}), f32[512,512]{1,0:T(8,128)}) %reduce-scatter.2.cloned.1.call-update) | async-done | bytes 1048592 | tf_op jit(solution)/shard_map/reduce_scatter | solution.py:49
  137.6 2.1 %convert_element_type.14 = bf16[512,512]{1,0:T(8,128)(2,1)} convert(f32[512,512]{1,0:T(8,128)} %reduce-scatter.2.cloned.1.call-done) | non-fusion elementwise | flops 262144 | bytes 1572864 | tf_op jit(solution)/shard_map/convert_element_type | solution.py:50
  (6 shorter events, 0.0 us)
Async XLA Ops:
  9.7 8.9 %copy-start.3 = (s32[8]{0:T(128)S(1)}, s32[8]{0:T(128)}, u32[]{:S(2)}) copy-start(s32[8]{0:T(128)} %param.9) | copy-start | bytes 100
  11.3 33.0 %all-to-all-start = ((bf16[8,2,32768]{2,1,0:T(2,128)(2,1)}), bf16[8,2,32768]{2,1,0:T(2,128)(2,1)S(1)}, u32[]{:S(2)}, u32[]{:S(2)}) async-start(bf16[8,2,32768]{2,1,0:T(2,128)(2,1)} %reshape.39), calls=%async_computation | async-start | bytes 2097152 | tf_op jit(solution)/shard_map/all_to_all | solution.py:21
  49.1 3.9 %copy-start.1 = (s32[2,8]{1,0:T(2,128)S(1)}, s32[2,8]{1,0:T(2,128)}, u32[]{:S(2)}) copy-start(s32[2,8]{1,0:T(2,128)} %param.7) | copy-start | bytes 196
  49.1 3.9 %copy-start.2 = (s32[3,1]{0,1:T(1,128)S(1)}, s32[3,1]{0,1:T(1,128)}, u32[]{:S(2)}) copy-start(s32[3,1]{0,1:T(1,128)} %param.8) | copy-start | bytes 40
  49.1 74.6 %all-to-all-start.1 = ((bf16[128,8,3,512]{3,0,2,1:T(8,128)(2,1)}), bf16[128,8,3,512]{3,0,2,1:T(8,128)(2,1)S(1)}, u32[]{:S(2)}, u32[]{:S(2)}) async-start(bf16[128,8,3,512]{3,0,2,1:T(8,128)(2,1)} %pad_maximum_fusion), calls=%async_computation.1 | async-start | bytes 6291456 | tf_op jit(solution)/shard_map/all_to_all | solution.py:33
  52.9 84.8 %reduce-scatter.2.cloned.1.call-start = ((), (), s32[]{:S(2)}) async-start(), calls=%async_computation.3 | async-start | bytes 3145728 | tf_op jit(solution)/shard_map/reduce_scatter | solution.py:49
  123.7 1.4 copy-start
Sparse Core Ops, SparseCore 0:
  128.9 8.6 reduce-scatter.1
where the time goes:
time: 147 us
  waiting for transfers between devices  105 us (71%)
  between operations  13.5 us (9%)
  starting transfers between devices  11.1 us (8%)
  other arithmetic  7.13 us (5%)
  local copies, waits for them, and re-layouts  6.24 us (4%)
  matrix products  3.66 us (2%)
    all_to_all x1, waiting for transfers between devices, per_device(): lax.all_to_all(windows, 'grid', split_axis=1, concat_axis=0, tiled=True)  70.5 us
    all_to_all x1, waiting for transfers between devices, per_device(): lax.all_to_all(band_held.reshape(row_count, 1, tile_size), 'grid', split_...  25.6 us
    reduce_scatter x1, waiting for transfers between devices, per_device(): summed = lax.psum_scatter(summed, 'depth', scatter_dimension=0, tiled=True)  8.85 us
    all_to_all x1, starting transfers between devices, per_device(): lax.all_to_all(band_held.reshape(row_count, 1, tile_size), 'grid', split_...  7.25 us
    unnamed x13, local copies, waits for them, and re-layouts  4.13 us
    all_to_all x1, starting transfers between devices, per_device(): lax.all_to_all(windows, 'grid', split_axis=1, concat_axis=0, tiled=True)  3.78 us
    dot_general x3, matrix products, per_device(): jnp.dot(arrived[:, offset, :], right_block, preferred_element_type=jnp.fl...  3.66 us
  transfers between devices with their start and end apart: 3, of which 3 were waited for; matrix products, arithmetic and copies ran while one was open for 0% of the time, Pallas kernels for 0%

commit v1 on v0

--- a/solution.py
+++ b/solution.py
@@ -1,10 +1,14 @@
+import functools
+
 import jax
 import jax.numpy as jnp
 from jax import lax
+from jax.experimental import pallas as pl
+from jax.experimental.pallas import tpu as pltpu
 from jax.sharding import PartitionSpec as P
 
 
-def per_device(band_held, inner_tiles, band_mask, inner_mask, held_col):
+def exchange_columns(band_held, inner_tiles, band_mask, inner_mask, held_col):
     grid_size = lax.axis_size("grid")
     tile_size = band_held.shape[1]
     band_count = band_mask.shape[0]
@@ -50,6 +54,125 @@
     return summed.astype(jnp.bfloat16)
 
 
+def add_products(places, slots, flags, pieces, inner, total):
+    for (source, row), piece in zip(places, pieces):
+        rows = pl.ds(row, piece.shape[0])
+
+        @pl.when(flags[source] != 0)
+        def _():
+            total[rows, :] += jnp.dot(
+                piece[...], inner[slots[source]], preferred_element_type=jnp.float32
+            )
+
+
+def early_kernel(places, slots, flags, inner, *refs):
+    total = refs[-1]
+    total[...] = jnp.zeros_like(total)
+    add_products(places, slots, flags, refs[:-1], inner, total)
+
+
+def late_kernel(places, slots, flags, inner, before, *refs):
+    *pieces, out, total = refs
+    total[...] = before[...]
+    add_products(places, slots, flags, pieces, inner, total)
+    out[...] = total[...].astype(out.dtype)
+
+
+def multiply(kernel, places, slots, flags, arrays, out_shape, scratch):
+    size = arrays[0].shape[-1]
+    smem, vmem = pl.BlockSpec(memory_space=pltpu.SMEM), pl.BlockSpec(memory_space=pltpu.VMEM)
+    return pl.pallas_call(
+        functools.partial(kernel, places),
+        out_shape=out_shape,
+        in_specs=[smem, smem] + [vmem] * len(arrays),
+        out_specs=vmem,
+        scratch_shapes=scratch,
+        compiler_params=pltpu.CompilerParams(vmem_limit_bytes=40 * 2**20),
+        cost_estimate=pl.CostEstimate(
+            flops=len(places) * size**3,
+            bytes_accessed=sum(a.size * a.dtype.itemsize for a in arrays),
+            transcendentals=0,
+        ),
+    )(slots, flags, *arrays)
+
+
+def gather_columns(band_held, inner_tiles, band_mask, inner_mask, held_col):
+    grid_size = lax.axis_size("grid")
+    size = band_held.shape[1]
+    local_offsets = inner_mask.shape[0]
+    halves = lax.axis_size("depth")
+    depth_index = lax.axis_index("depth")
+    column = lax.axis_index("grid")
+    half = size // 2
+
+    order = list(range(0, grid_size, 2)) + list(range(1, grid_size, 2))[::-1]
+    onward = [(order[i], order[(i + 1) % grid_size]) for i in range(grid_size)]
+    backward = [(b, a) for a, b in onward]
+    position_of = [order.index(g) for g in range(grid_size)]
+
+    own = lax.dynamic_slice_in_dim(band_held, depth_index * size, size, 0)
+    first = [own[:half], own[half:]]
+    pieces = {(0, 0): first[0], (0, 1): first[1]}
+    right, left = list(first), list(first)
+    steps = (grid_size - 1) // 2
+    for step in range(1, steps + 1):
+        for h in (0, 1):
+            right[h] = lax.ppermute(right[h], "grid", onward)
+            left[1 - h] = lax.ppermute(left[1 - h], "grid", backward)
+            pieces[(grid_size - step, h)] = right[h]
+            pieces[(step, 1 - h)] = left[1 - h]
+    last = {}
+    if grid_size % 2 == 0:
+        last[(steps + 1, 0)] = lax.ppermute(right[0], "grid", onward)
+        last[(steps + 1, 1)] = lax.ppermute(left[1], "grid", backward)
+
+    masked = inner_tiles.reshape(local_offsets, size, size) * inner_mask[:, :, None].astype(
+        inner_tiles.dtype
+    )
+    swapped = lax.ppermute(masked, "depth", [(0, 1), (1, 0)])
+    inner = jnp.concatenate([masked, swapped], axis=0)
+
+    position = jnp.asarray(position_of, jnp.int32)[column]
+    sources = jnp.asarray(order, jnp.int32)[
+        (position + jnp.arange(grid_size, dtype=jnp.int32)) % grid_size
+    ]
+    true_column = held_col[sources]
+    offset = true_column - column + local_offsets * halves // 2
+    inside = (offset >= 0) & (offset < local_offsets * halves)
+    offset = jnp.clip(offset, 0, local_offsets * halves - 1)
+    band_row = lax.dynamic_index_in_dim(band_mask, depth_index, 0, keepdims=False)
+    flags = jnp.where(inside, band_row[true_column], 0).astype(jnp.int32)
+    slots = (
+        jnp.where(offset // local_offsets == depth_index, 0, local_offsets)
+        + offset % local_offsets
+    ).astype(jnp.int32)
+
+    def placed(items):
+        return [(source, h * half) for source, h in items]
+
+    total_shape = jax.ShapeDtypeStruct((size, size), jnp.float32)
+    early = multiply(
+        early_kernel, placed(pieces), slots, flags, [inner, *pieces.values()], total_shape, []
+    )
+    return multiply(
+        late_kernel,
+        placed(last),
+        slots,
+        flags,
+        [inner, early, *last.values()],
+        jax.ShapeDtypeStruct((size, size), band_held.dtype),
+        [pltpu.VMEM((size, size), jnp.float32)],
+    )
+
+
+def per_device(band_held, inner_tiles, band_mask, inner_mask, held_col):
+    window = inner_mask.shape[0] * lax.axis_size("depth")
+    small = lax.axis_size("grid") <= 2 * window
+    fits = lax.axis_size("depth") == 2 and band_mask.shape[0] == 2 and lax.axis_size("grid") % 2 == 0
+    chosen = gather_columns if small and fits else exchange_columns
+    return chosen(band_held, inner_tiles, band_mask, inner_mask, held_col)
+
+
 def solution(mesh):
     placed = (
         P("groups", "grid"),

time: 147 us -> 52.8 us (0.36)
  waiting for transfers between devices: 105 us -> 25.1 us
  between operations: 13.5 us -> 0.07 us
  starting transfers between devices: 11.1 us -> 15.2 us
  local copies, waits for them, and re-layouts: 6.24 us -> 2.57 us
  matrix products: 3.66 us -> 0 us
  Pallas kernels: 0 us -> 3.33 us
    all_to_all x2 -> x0, waiting for transfers between devices: 96.1 us -> none  [the longest x1 70.5 us: per_device(): lax.all_to_all(windows, 'grid', split_axis=1, concat_axis=0, tiled=True)]
    ppermute x0 -> x15, waiting for transfers between devices: none -> 25.1 us  [the longest x6 22.4 us: gather_columns(): right[h] = lax.ppermute(right[h], 'grid', onward)]
    ppermute x0 -> x15, starting transfers between devices: none -> 15.2 us  [the longest x6 9 us: gather_columns(): left[1 - h] = lax.ppermute(left[1 - h], 'grid', backward)]
    all_to_all x2 -> x0, starting transfers between devices: 11 us -> none  [the longest x1 7.25 us: per_device(): lax.all_to_all(band_held.reshape(row_count, 1, tile_size), 'grid', split_...]
    reduce_scatter x1 -> x0, waiting for transfers between devices: 8.85 us -> none  [per_device(): summed = lax.psum_scatter(summed, 'depth', scatter_dimension=0, tiled=True)]
    unnamed x13 -> x10, local copies, waits for them, and re-layouts: 4.13 us -> 0.02 us
    dot_general x3 -> x0, matrix products: 3.66 us -> none  [per_device(): jnp.dot(arrived[:, offset, :], right_block, preferred_element_type=jnp.fl...]
    pallas_call x0 -> x2, Pallas kernels: none -> 3.33 us  [multiply(): pl.pallas_call(functools.partial(kernel, places), out_shape=out_shape, in...]
  transfers between devices with their start and end apart: 3 -> 15, of which waited for: 3 -> 8; matrix products, arithmetic and copies ran while one was open for 0% -> 10% of each run, Pallas kernels for 0% -> 4%
where the time goes in v1:
time: 52.8 us; the launch traced here: 52.6 us
  waiting for transfers between devices  25.1 us (48%)
  starting transfers between devices  15.2 us (29%)
  other arithmetic  6.37 us (12%)
  Pallas kernels  3.33 us (6%)
  local copies, waits for them, and re-layouts  2.57 us (5%)
    ppermute x6, waiting for transfers between devices, gather_columns(): right[h] = lax.ppermute(right[h], 'grid', onward)  22.4 us
    ppermute x6, starting transfers between devices, gather_columns(): left[1 - h] = lax.ppermute(left[1 - h], 'grid', backward)  9 us
    ppermute x6, starting transfers between devices, gather_columns(): right[h] = lax.ppermute(right[h], 'grid', onward)  3.77 us
    pallas_call x2, Pallas kernels, multiply(): pl.pallas_call(functools.partial(kernel, places), out_shape=out_shape, in...  3.33 us
    mul x1, other arithmetic, gather_columns(): inner_tiles.reshape(local_offsets, size, size)  2.84 us
    concatenate x1, other arithmetic, gather_columns(): inner = jnp.concatenate([masked, swapped], axis=0)  2.15 us
    ppermute x1, waiting for transfers between devices, gather_columns(): last[steps + 1, 0] = lax.ppermute(right[0], 'grid', onward)  1.65 us
    ppermute x1, starting transfers between devices, gather_columns(): last[steps + 1, 1] = lax.ppermute(left[1], 'grid', backward)  1.6 us
  transfers between devices with their start and end apart: 15, of which 8 were waited for; matrix products, arithmetic and copies ran while one was open for 10% of the time, Pallas kernels for 4%

profile of v1, /device:TPU:0, one launch (start us, length us, event | category | flops | bytes accessed | tf_op | source)
XLA Modules:
  0.0 52.6 jit_solution(452709855810396776)
XLA Ops:
  0.0 0.7 %convert_bitcast_fusion = bf16[3]{0:T(256)(128)(2,1)S(1)} fusion(s32[3,1]{0,1:T(1,128)} %param.10), kind=kLoop, calls=%fused_computation.27 | loop fusion | flops 3 | bytes 18 | tf_op jit(solution)/shard_map/convert_element_type | solution.py:129
  0.7 2.8 %broadcast_multiply_fusion = bf16[3,512,512]{2,1,0:T(8,128)(2,1)} fusion(bf16[3,512,512]{2,1,0:T(8,128)(2,1)} %bitcast.16, bf16[3]{0:T(256)(128)(2,1)S(1)} %convert_bitcast_fusion), kind=kLoop, calls=%fused_computation.4 | loop fusion | flops 786432 | bytes 3145734 | tf_op jit(solution)/shard_map/mul | solution.py:129
  3.5 0.5 collective-permute-start
  4.0 2.6 %collective-permute-start.2 = (bf16[256,512]{1,0:T(8,128)(2,1)S(1)}, bf16[256,512]{1,0:T(8,128)(2,1)S(1)}, u32[]{:S(2)}, u32[]{:S(2)}) collective-permute-start(bf16[256,512]{1,0:T(8,128)(2,1)S(1)} %get-tuple-element.5.refs_1_), channel_id=1, source_target_pairs={{4,0},{8,4},{12,8},{14,12},{10,14},{6,10},{2,6},{0,2},{5,1},{9,5},... | collective-permute-start | bytes 786440 | tf_op jit(solution)/shard_map/ppermute | solution.py:121
  6.6 0.2 collective-permute-start.3
  6.7 2.0 %collective-permute-start.1 = (bf16[256,512]{1,0:T(8,128)(2,1)S(1)}, bf16[256,512]{1,0:T(8,128)(2,1)S(1)}, u32[]{:S(2)}, u32[]{:S(2)}) collective-permute-start(bf16[256,512]{1,0:T(8,128)(2,1)S(1)} %get-tuple-element.6.refs_0_), channel_id=1, source_target_pairs={{0,4},{4,8},{8,12},{12,14},{14,10},{10,6},{6,2},{2,0},{1,5},{5,9},... | collective-permute-start | bytes 786440 | tf_op jit(solution)/shard_map/ppermute | solution.py:120
  8.7 0.6 %dynamic_slice.10 = s32[1]{0:T(128)} dynamic-slice(s32[8]{0:T(128)S(1)} %copy-done.4, s32[]{:T(128)S(6)} %select_n.71), dynamic_slice_sizes={1} | dynamic-slice | bytes 12 | tf_op jit(solution)/shard_map/dynamic_slice | solution.py:135
  9.3 0.7 %fusion.3 = s32[8]{0:T(128)S(1)} fusion(s32[]{:T(128)} %bitcast), kind=kLoop, calls=%fused_computation.24 | loop fusion | flops 120 | bytes 36 | tf_op jit(solution)/shard_map/select_n | solution.py:136
  10.0 0.6 %gather_fusion = s32[8]{0:T(128)S(1)} fusion(s32[8]{0:T(128)S(1)} %copy-done.2, s32[1024]{0:T(1024)S(1)} %pad_clamp_fusion.2), kind=kCustom, calls=%fused_computation | custom fusion | bytes 96 | tf_op jit(solution)/shard_map/gather | solution.py:136
  10.7 0.6 %gather_fusion.1 = s32[8]{0:T(128)S(1)} fusion(s32[8]{0:T(128)S(1)} %copy-done.1, s32[1024]{0:T(1024)S(1)} %pad_clamp_fusion.1), kind=kCustom, calls=%fused_computation.1 | custom fusion | bytes 96 | tf_op jit(solution)/shard_map/gather | solution.py:139
  11.3 9.3 %collective-permute-done.1.refs_2_ = bf16[256,512]{1,0:T(8,128)(2,1)S(1)} collective-permute-done((bf16[256,512]{1,0:T(8,128)(2,1)S(1)}, bf16[256,512]{1,0:T(8,128)(2,1)S(1)}, u32[]{:S(2)}, u32[]{:S(2)}) %collective-permute-start.1) | collective-permute-done | bytes 262176 | tf_op jit(solution)/shard_map/ppermute | solution.py:120
  20.6 0.4 collective-permute-start.5
  21.0 1.6 %collective-permute-start.6 = (bf16[256,512]{1,0:T(8,128)(2,1)S(1)}, bf16[256,512]{1,0:T(8,128)(2,1)S(1)}, u32[]{:S(2)}, u32[]{:S(2)}) collective-permute-start(bf16[256,512]{1,0:T(8,128)(2,1)S(1)} %collective-permute-done.2.refs_3_), channel_id=1, source_target_pairs={{4,0},{8,4},{12,8},{14,12},{10,14},{6,10},{2,6},{0,2},{5,1},{9,5},... | collective-permute-start | bytes 786440 | tf_op jit(solution)/shard_map/ppermute | solution.py:121
  22.6 0.4 collective-permute-start.7
  23.1 1.6 %collective-permute-start.8 = (bf16[256,512]{1,0:T(8,128)(2,1)S(1)}, bf16[256,512]{1,0:T(8,128)(2,1)S(1)}, u32[]{:S(2)}, u32[]{:S(2)}) collective-permute-start(bf16[256,512]{1,0:T(8,128)(2,1)S(1)} %collective-permute-done.4.refs_5_), channel_id=1, source_target_pairs={{4,0},{8,4},{12,8},{14,12},{10,14},{6,10},{2,6},{0,2},{5,1},{9,5},... | collective-permute-start | bytes 786440 | tf_op jit(solution)/shard_map/ppermute | solution.py:121
  24.7 5.2 %collective-permute-done.5.refs_6_ = bf16[256,512]{1,0:T(8,128)(2,1)S(1)} collective-permute-done((bf16[256,512]{1,0:T(8,128)(2,1)S(1)}, bf16[256,512]{1,0:T(8,128)(2,1)S(1)}, u32[]{:S(2)}, u32[]{:S(2)}) %collective-permute-start.5) | collective-permute-done | bytes 262176 | tf_op jit(solution)/shard_map/ppermute | solution.py:120
  29.9 0.4 collective-permute-start.9
  30.3 1.6 %collective-permute-start.10 = (bf16[256,512]{1,0:T(8,128)(2,1)S(1)}, bf16[256,512]{1,0:T(8,128)(2,1)S(1)}, u32[]{:S(2)}, u32[]{:S(2)}) collective-permute-start(bf16[256,512]{1,0:T(8,128)(2,1)S(1)} %collective-permute-done.6.refs_7_), channel_id=1, source_target_pairs={{4,0},{8,4},{12,8},{14,12},{10,14},{6,10},{2,6},{0,2},{5,1},{9,5},... | collective-permute-start | bytes 786440 | tf_op jit(solution)/shard_map/ppermute | solution.py:121
  31.9 0.6 %gather_fusion.2 = s32[8]{0:T(128)S(1)} fusion(s32[8]{0:T(128)S(1)} %fusion.1, s32[1024]{0:T(1024)S(1)} %pad_clamp_fusion), kind=kCustom, calls=%fused_computation.2 | custom fusion | bytes 96 | tf_op jit(solution)/shard_map/gather | solution.py:144
  32.5 2.9 %collective-permute-done.7.refs_8_ = bf16[256,512]{1,0:T(8,128)(2,1)S(1)} collective-permute-done((bf16[256,512]{1,0:T(8,128)(2,1)S(1)}, bf16[256,512]{1,0:T(8,128)(2,1)S(1)}, u32[]{:S(2)}, u32[]{:S(2)}) %collective-permute-start.7) | collective-permute-done | bytes 262176 | tf_op jit(solution)/shard_map/ppermute | solution.py:120
  35.5 0.4 collective-permute-start.11
  35.9 1.6 %collective-permute-start.12 = (bf16[256,512]{1,0:T(8,128)(2,1)S(1)}, bf16[256,512]{1,0:T(8,128)(2,1)S(1)}, u32[]{:S(2)}, u32[]{:S(2)}) collective-permute-start(bf16[256,512]{1,0:T(8,128)(2,1)S(1)} %collective-permute-done.8.refs_9_), channel_id=1, source_target_pairs={{4,0},{8,4},{12,8},{14,12},{10,14},{6,10},{2,6},{0,2},{5,1},{9,5},... | collective-permute-start | bytes 786440 | tf_op jit(solution)/shard_map/ppermute | solution.py:121
  37.5 3.6 %collective-permute-done.9.refs_10_ = bf16[256,512]{1,0:T(8,128)(2,1)S(1)} collective-permute-done((bf16[256,512]{1,0:T(8,128)(2,1)S(1)}, bf16[256,512]{1,0:T(8,128)(2,1)S(1)}, u32[]{:S(2)}, u32[]{:S(2)}) %collective-permute-start.9) | collective-permute-done | bytes 262176 | tf_op jit(solution)/shard_map/ppermute | solution.py:120
  41.1 0.4 collective-permute-start.13
  41.5 1.6 %collective-permute-start.14 = (bf16[256,512]{1,0:T(8,128)(2,1)S(1)}, bf16[256,512]{1,0:T(8,128)(2,1)S(1)}, u32[]{:S(2)}, u32[]{:S(2)}) collective-permute-start(bf16[256,512]{1,0:T(8,128)(2,1)S(1)} %collective-permute-done.10.refs_11_), channel_id=1, source_target_pairs={{4,0},{8,4},{12,8},{14,12},{10,14},{6,10},{2,6},{0,2},{5,1},{9,5},... | collective-permute-start | bytes 786440 | tf_op jit(solution)/shard_map/ppermute | solution.py:127
  43.1 2.2 %pad_maximum_fusion.inner = bf16[6,512,512]{2,1,0:T(8,128)(2,1)S(1)} fusion(bf16[3,512,512]{2,1,0:T(8,128)(2,1)} %collective-permute-done, bf16[3,512,512]{2,1,0:T(8,128)(2,1)} %broadcast_multiply_fusion), kind=kLoop, calls=%fused_computation.3 | loop fusion | flops 1572864 | bytes 6291456 | tf_op jit(solution)/shard_map/concatenate | solution.py:133
  45.3 1.4 %collective-permute-done.11.refs_12_ = bf16[256,512]{1,0:T(8,128)(2,1)S(1)} collective-permute-done((bf16[256,512]{1,0:T(8,128)(2,1)S(1)}, bf16[256,512]{1,0:T(8,128)(2,1)S(1)}, u32[]{:S(2)}, u32[]{:S(2)}) %collective-permute-start.11) | collective-permute-done | bytes 262176 | tf_op jit(solution)/shard_map/ppermute | solution.py:120
  46.7 0.4 collective-permute-done.12.refs_13_
  47.1 1.9 %shard_map.73.before = f32[512,512]{1,0:T(8,128)S(1)} custom-call(s32[8]{0:T(128)S(1)} %get-tuple-element.8.slots, s32[8]{0:T(128)S(1)} %get-tuple-element.7.flags, bf16[6,512,512]{2,1,0:T(8,128)(2,1)S(1)} %pad_maximum_fusion.inner, bf16[256,512]{1,0:T(8,128)(2,1)S(1)} %get-tuple-element.6.refs_0_, bf16[256,512]{1,0:T(8,128)(2,1)S(1)} %get-tuple-element.5.refs_1_, ...), custom_call_target="tpu_custom_call" | custom-call | flops 1879048192 | bytes 6815744 | tf_op jit(solution)/shard_map/pallas_call | solution.py:84
  49.0 1.6 %collective-permute-done.13.refs_0_ = bf16[256,512]{1,0:T(8,128)(2,1)S(1)} collective-permute-done((bf16[256,512]{1,0:T(8,128)(2,1)S(1)}, bf16[256,512]{1,0:T(8,128)(2,1)S(1)}, u32[]{:S(2)}, u32[]{:S(2)}) %collective-permute-start.13) | collective-permute-done | bytes 262176 | tf_op jit(solution)/shard_map/ppermute | solution.py:126
  50.7 0.5 collective-permute-done.14.refs_1_
  51.2 1.5 %shard_map.74 = bf16[512,512]{1,0:T(8,128)(2,1)} custom-call(s32[8]{0:T(128)S(1)} %get-tuple-element.8.slots, s32[8]{0:T(128)S(1)} %get-tuple-element.7.flags, bf16[6,512,512]{2,1,0:T(8,128)(2,1)S(1)} %pad_maximum_fusion.inner, f32[512,512]{1,0:T(8,128)S(1)} %shard_map.73.before, bf16[256,512]{1,0:T(8,128)(2,1)S(1)} %collective-permute-done.13.refs_0_, ...), custom_call_target="tpu_custom_call" | custom-call | flops 268435456 | bytes 4718592 | tf_op jit(solution)/shard_map/pallas_call | solution.py:84
  (26 shorter events, 0.3 us)
Async XLA Ops:
  0.0 31.9 %copy-start = (s32[2,8]{1,0:T(2,128)S(1)}, s32[2,8]{1,0:T(2,128)}, u32[]{:S(2)}) copy-start(s32[2,8]{1,0:T(2,128)} %param.9) | copy-start | bytes 196
  0.7 3.3 %copy-start.3 = (bf16[1024,512]{1,0:T(8,128)(2,1)S(1)}, bf16[1024,512]{1,0:T(8,128)(2,1)}, u32[]{:S(2)}) copy-start(bf16[1024,512]{1,0:T(8,128)(2,1)} %param.7) | copy-start | bytes 3145732
  0.7 8.1 %copy-start.4 = (s32[8]{0:T(128)S(1)}, s32[8]{0:T(128)}, u32[]{:S(2)}) copy-start(s32[8]{0:T(128)} %constant.60.clone) | copy-start | bytes 100
  0.7 9.3 %copy-start.2 = (s32[8]{0:T(128)S(1)}, s32[8]{0:T(128)}, u32[]{:S(2)}) copy-start(s32[8]{0:T(128)} %constant.61.clone) | copy-start | bytes 100
  3.5 7.2 %copy-start.1 = (s32[8]{0:T(128)S(1)}, s32[8]{0:T(128)}, u32[]{:S(2)}) copy-start(s32[8]{0:T(128)} %param.11) | copy-start | bytes 100
  3.5 39.6 %collective-permute-start = (bf16[3,512,512]{2,1,0:T(8,128)(2,1)}, bf16[3,512,512]{2,1,0:T(8,128)(2,1)}, u32[]{:S(2)}, u32[]{:S(2)}) collective-permute-start(bf16[3,512,512]{2,1,0:T(8,128)(2,1)} %broadcast_multiply_fusion), channel_id=1, source_target_pairs={{0,1},{1,0},{2,3},{3,2},{4,5},{5,4},{6,7},{7,6},{8,9},{9,8},{10,11... | collective-permute-start | bytes 4718600 | tf_op jit(solution)/shard_map/ppermute | solution.py:132
  4.0 17.0 %collective-permute-start.2 = (bf16[256,512]{1,0:T(8,128)(2,1)S(1)}, bf16[256,512]{1,0:T(8,128)(2,1)S(1)}, u32[]{:S(2)}, u32[]{:S(2)}) collective-permute-start(bf16[256,512]{1,0:T(8,128)(2,1)S(1)} %get-tuple-element.5.refs_1_), channel_id=1, source_target_pairs={{4,0},{8,4},{12,8},{14,12},{10,14},{6,10},{2,6},{0,2},{5,1},{9,5},... | collective-permute-start | bytes 786440 | tf_op jit(solution)/shard_map/ppermute | solution.py:121
  6.6 16.1 %collective-permute-start.3 = (bf16[256,512]{1,0:T(8,128)(2,1)S(1)}, bf16[256,512]{1,0:T(8,128)(2,1)S(1)}, u32[]{:S(2)}, u32[]{:S(2)}) collective-permute-start(bf16[256,512]{1,0:T(8,128)(2,1)S(1)} %get-tuple-element.5.refs_1_), channel_id=1, source_target_pairs={{0,4},{4,8},{8,12},{12,14},{14,10},{10,6},{6,2},{2,0},{1,5},{5,9},... | collective-permute-start | bytes 786440 | tf_op jit(solution)/shard_map/ppermute | solution.py:120
  6.7 13.9 %collective-permute-start.1 = (bf16[256,512]{1,0:T(8,128)(2,1)S(1)}, bf16[256,512]{1,0:T(8,128)(2,1)S(1)}, u32[]{:S(2)}, u32[]{:S(2)}) collective-permute-start(bf16[256,512]{1,0:T(8,128)(2,1)S(1)} %get-tuple-element.6.refs_0_), channel_id=1, source_target_pairs={{0,4},{4,8},{8,12},{12,14},{14,10},{10,6},{6,2},{2,0},{1,5},{5,9},... | collective-permute-start | bytes 786440 | tf_op jit(solution)/shard_map/ppermute | solution.py:120
  8.7 14.4 %collective-permute-start.4 = (bf16[256,512]{1,0:T(8,128)(2,1)S(1)}, bf16[256,512]{1,0:T(8,128)(2,1)S(1)}, u32[]{:S(2)}, u32[]{:S(2)}) collective-permute-start(bf16[256,512]{1,0:T(8,128)(2,1)S(1)} %get-tuple-element.6.refs_0_), channel_id=1, source_target_pairs={{4,0},{8,4},{12,8},{14,12},{10,14},{6,10},{2,6},{0,2},{5,1},{9,5},... | collective-permute-start | bytes 786440 | tf_op jit(solution)/shard_map/ppermute | solution.py:121
  20.6 9.2 %collective-permute-start.5 = (bf16[256,512]{1,0:T(8,128)(2,1)S(1)}, bf16[256,512]{1,0:T(8,128)(2,1)S(1)}, u32[]{:S(2)}, u32[]{:S(2)}) collective-permute-start(bf16[256,512]{1,0:T(8,128)(2,1)S(1)} %collective-permute-done.1.refs_2_), channel_id=1, source_target_pairs={{0,4},{4,8},{8,12},{12,14},{14,10},{10,6},{6,2},{2,0},{1,5},{5,9},... | collective-permute-start | bytes 786440 | tf_op jit(solution)/shard_map/ppermute | solution.py:120
  21.0 9.2 %collective-permute-start.6 = (bf16[256,512]{1,0:T(8,128)(2,1)S(1)}, bf16[256,512]{1,0:T(8,128)(2,1)S(1)}, u32[]{:S(2)}, u32[]{:S(2)}) collective-permute-start(bf16[256,512]{1,0:T(8,128)(2,1)S(1)} %collective-permute-done.2.refs_3_), channel_id=1, source_target_pairs={{4,0},{8,4},{12,8},{14,12},{10,14},{6,10},{2,6},{0,2},{5,1},{9,5},... | collective-permute-start | bytes 786440 | tf_op jit(solution)/shard_map/ppermute | solution.py:121
  22.6 12.8 %collective-permute-start.7 = (bf16[256,512]{1,0:T(8,128)(2,1)S(1)}, bf16[256,512]{1,0:T(8,128)(2,1)S(1)}, u32[]{:S(2)}, u32[]{:S(2)}) collective-permute-start(bf16[256,512]{1,0:T(8,128)(2,1)S(1)} %collective-permute-done.3.refs_4_), channel_id=1, source_target_pairs={{0,4},{4,8},{8,12},{12,14},{14,10},{10,6},{6,2},{2,0},{1,5},{5,9},... | collective-permute-start | bytes 786440 | tf_op jit(solution)/shard_map/ppermute | solution.py:120
  23.1 12.8 %collective-permute-start.8 = (bf16[256,512]{1,0:T(8,128)(2,1)S(1)}, bf16[256,512]{1,0:T(8,128)(2,1)S(1)}, u32[]{:S(2)}, u32[]{:S(2)}) collective-permute-start(bf16[256,512]{1,0:T(8,128)(2,1)S(1)} %collective-permute-done.4.refs_5_), channel_id=1, source_target_pairs={{4,0},{8,4},{12,8},{14,12},{10,14},{6,10},{2,6},{0,2},{5,1},{9,5},... | collective-permute-start | bytes 786440 | tf_op jit(solution)/shard_map/ppermute | solution.py:121
  29.9 11.2 %collective-permute-start.9 = (bf16[256,512]{1,0:T(8,128)(2,1)S(1)}, bf16[256,512]{1,0:T(8,128)(2,1)S(1)}, u32[]{:S(2)}, u32[]{:S(2)}) collective-permute-start(bf16[256,512]{1,0:T(8,128)(2,1)S(1)} %collective-permute-done.5.refs_6_), channel_id=1, source_target_pairs={{0,4},{4,8},{8,12},{12,14},{14,10},{10,6},{6,2},{2,0},{1,5},{5,9},... | collective-permute-start | bytes 786440 | tf_op jit(solution)/shard_map/ppermute | solution.py:120
  30.3 11.2 %collective-permute-start.10 = (bf16[256,512]{1,0:T(8,128)(2,1)S(1)}, bf16[256,512]{1,0:T(8,128)(2,1)S(1)}, u32[]{:S(2)}, u32[]{:S(2)}) collective-permute-start(bf16[256,512]{1,0:T(8,128)(2,1)S(1)} %collective-permute-done.6.refs_7_), channel_id=1, source_target_pairs={{4,0},{8,4},{12,8},{14,12},{10,14},{6,10},{2,6},{0,2},{5,1},{9,5},... | collective-permute-start | bytes 786440 | tf_op jit(solution)/shard_map/ppermute | solution.py:121
  35.5 11.2 %collective-permute-start.11 = (bf16[256,512]{1,0:T(8,128)(2,1)S(1)}, bf16[256,512]{1,0:T(8,128)(2,1)S(1)}, u32[]{:S(2)}, u32[]{:S(2)}) collective-permute-start(bf16[256,512]{1,0:T(8,128)(2,1)S(1)} %collective-permute-done.7.refs_8_), channel_id=1, source_target_pairs={{0,4},{4,8},{8,12},{12,14},{14,10},{10,6},{6,2},{2,0},{1,5},{5,9},... | collective-permute-start | bytes 786440 | tf_op jit(solution)/shard_map/ppermute | solution.py:120
  35.9 11.2 %collective-permute-start.12 = (bf16[256,512]{1,0:T(8,128)(2,1)S(1)}, bf16[256,512]{1,0:T(8,128)(2,1)S(1)}, u32[]{:S(2)}, u32[]{:S(2)}) collective-permute-start(bf16[256,512]{1,0:T(8,128)(2,1)S(1)} %collective-permute-done.8.refs_9_), channel_id=1, source_target_pairs={{4,0},{8,4},{12,8},{14,12},{10,14},{6,10},{2,6},{0,2},{5,1},{9,5},... | collective-permute-start | bytes 786440 | tf_op jit(solution)/shard_map/ppermute | solution.py:121
  41.1 9.6 %collective-permute-start.13 = (bf16[256,512]{1,0:T(8,128)(2,1)S(1)}, bf16[256,512]{1,0:T(8,128)(2,1)S(1)}, u32[]{:S(2)}, u32[]{:S(2)}) collective-permute-start(bf16[256,512]{1,0:T(8,128)(2,1)S(1)} %collective-permute-done.9.refs_10_), channel_id=1, source_target_pairs={{0,4},{4,8},{8,12},{12,14},{14,10},{10,6},{6,2},{2,0},{1,5},{5,9},... | collective-permute-start | bytes 786440 | tf_op jit(solution)/shard_map/ppermute | solution.py:126
  41.5 9.6 %collective-permute-start.14 = (bf16[256,512]{1,0:T(8,128)(2,1)S(1)}, bf16[256,512]{1,0:T(8,128)(2,1)S(1)}, u32[]{:S(2)}, u32[]{:S(2)}) collective-permute-start(bf16[256,512]{1,0:T(8,128)(2,1)S(1)} %collective-permute-done.10.refs_11_), channel_id=1, source_target_pairs={{4,0},{8,4},{12,8},{14,12},{10,14},{6,10},{2,6},{0,2},{5,1},{9,5},... | collective-permute-start | bytes 786440 | tf_op jit(solution)/shard_map/ppermute | solution.py:127

commit v2 on v1

--- a/solution.py
+++ b/solution.py
@@ -126,11 +126,12 @@
         last[(steps + 1, 0)] = lax.ppermute(right[0], "grid", onward)
         last[(steps + 1, 1)] = lax.ppermute(left[1], "grid", backward)
 
-    masked = inner_tiles.reshape(local_offsets, size, size) * inner_mask[:, :, None].astype(
-        inner_tiles.dtype
-    )
-    swapped = lax.ppermute(masked, "depth", [(0, 1), (1, 0)])
-    inner = jnp.concatenate([masked, swapped], axis=0)
+    swapped = lax.ppermute(inner_tiles, "depth", [(0, 1), (1, 0)])
+    inner = jnp.concatenate([inner_tiles, swapped], axis=0).reshape(-1, size, size)
+    inner_mask, _ = lax.optimization_barrier((inner_mask, pieces[(grid_size - 1, 0)]))
+    tile_flags = jnp.concatenate(
+        [inner_mask, lax.ppermute(inner_mask, "depth", [(0, 1), (1, 0)])], axis=0
+    )[:, 0]
 
     position = jnp.asarray(position_of, jnp.int32)[column]
     sources = jnp.asarray(order, jnp.int32)[
@@ -147,6 +148,8 @@
         + offset % local_offsets
     ).astype(jnp.int32)
 
+    flags = flags * tile_flags[slots]
+
     def placed(items):
         return [(source, h * half) for source, h in items]
 
@@ -156,10 +159,14 @@
     )
     return multiply(
         late_kernel,
-        placed(last),
-        slots,
-        flags,
-        [inner, early, *last.values()],
+        [(0, h * half) for _, h in last],
+        jnp.zeros((1,), jnp.int32),
+        flags[steps + 1 :][:1],
+        [
+            lax.dynamic_slice_in_dim(inner, slots[steps + 1], 1, 0),
+            early,
+            *last.values(),
+        ],
         jax.ShapeDtypeStruct((size, size), band_held.dtype),
         [pltpu.VMEM((size, size), jnp.float32)],
     )

time: 52.8 us -> 50.6 us (0.958)
  waiting for transfers between devices: 25.1 us -> 18.9 us
  local copies, waits for them, and re-layouts: 2.57 us -> 7.37 us
  other arithmetic: 6.37 us -> 3.54 us
  between operations: 0.07 us -> 2.07 us
  Pallas kernels: 3.33 us -> 2.78 us
    ppermute x6, waiting for transfers between devices: 22.4 us -> 15 us  [gather_columns(): right[h] = lax.ppermute(right[h], 'grid', onward)]
    mul x1 -> x0, other arithmetic: 2.84 us -> none  [gather_columns(): inner_tiles.reshape(local_offsets, size, size)]
    slice x0 -> x2, local copies, waits for them, and re-layouts: none -> 1.13 us  [the longest x1 0.58 us: gather_columns(): slots[steps + 1]]
    slice x1, local copies, waits for them, and re-layouts: 0.03 us -> 1.06 us  [gather_columns(): first = [own[:half], own[half:]]]
    ppermute x1, waiting for transfers between devices: 1.65 us -> 2.64 us  [gather_columns(): last[steps + 1, 0] = lax.ppermute(right[0], 'grid', onward)]
    ppermute x1 -> x2, waiting for transfers between devices: 0.01 us -> 0.75 us  [the longest x1 0.75 us: gather_columns(): lax.ppermute(inner_mask, 'depth', [(0, 1), (1, 0)])]
    squeeze x0 -> x1, other arithmetic: none -> 0.73 us  [gather_columns(): jnp.concatenate([inner_mask, lax.ppermute(inner_mask, 'depth', [(0, 1), (...]
    convert_element_type x1 -> x0, other arithmetic: 0.67 us -> none  [gather_columns(): inner_mask[:, :, None].astype(inner_tiles.dtype)]
  transfers between devices with their start and end apart: 15 -> 16, of which waited for: 8 -> 7; matrix products, arithmetic and copies ran while one was open for 10% -> 22% of each run, Pallas kernels for 4% -> 3%
where the time goes in v2:
time: 50.6 us; the launch traced here: 50.1 us
  waiting for transfers between devices  18.9 us (37%)
  starting transfers between devices  15.5 us (31%)
  local copies, waits for them, and re-layouts  7.37 us (15%)
  other arithmetic  3.54 us (7%)
  Pallas kernels  2.78 us (5%)
  between operations  2.07 us (4%)
    ppermute x6, waiting for transfers between devices, gather_columns(): right[h] = lax.ppermute(right[h], 'grid', onward)  15 us
    ppermute x6, starting transfers between devices, gather_columns(): left[1 - h] = lax.ppermute(left[1 - h], 'grid', backward)  9.05 us
    ppermute x6, starting transfers between devices, gather_columns(): right[h] = lax.ppermute(right[h], 'grid', onward)  3.87 us
    pallas_call x2, Pallas kernels, multiply(): pl.pallas_call(functools.partial(kernel, places), out_shape=out_shape, in...  2.78 us
    ppermute x1, waiting for transfers between devices, gather_columns(): last[steps + 1, 0] = lax.ppermute(right[0], 'grid', onward)  2.64 us
    concatenate x1, other arithmetic, gather_columns(): jnp.concatenate([inner_tiles, swapped], axis=0).reshape(-1, size, size)  2.09 us
    ppermute x1, starting transfers between devices, gather_columns(): last[steps + 1, 1] = lax.ppermute(left[1], 'grid', backward)  1.63 us
    gather x1, local copies, waits for them, and re-layouts, gather_columns(): jnp.asarray(order, jnp.int32)  1.3 us
  transfers between devices with their start and end apart: 16, of which 7 were waited for; matrix products, arithmetic and copies ran while one was open for 22% of the time, Pallas kernels for 3%

profile of v2, /device:TPU:0, one launch (start us, length us, event | category | flops | bytes accessed | tf_op | source)
XLA Modules:
  0.0 50.1 jit_solution(16624765590067972598)
XLA Ops:
  0.0 0.5 collective-permute-start.2
  0.5 1.1 %constant_dynamic-slice_fusion.2 = (bf16[256,512]{1,0:T(8,128)(2,1)S(1)}, bf16[256,512]{1,0:T(8,128)(2,1)S(1)}) fusion(bf16[1024,512]{1,0:T(8,128)(2,1)} %param.7, s32[]{:T(128)S(6)} %add.135, s32[]{:T(128)S(6)} %select_n.118), kind=kLoop, calls=%fused_computation.25 | loop fusion | bytes 1048584 | tf_op jit(solution)/shard_map/slice | solution.py:114
  1.5 2.6 %collective-permute-start.3 = (bf16[256,512]{1,0:T(8,128)(2,1)S(1)}, bf16[256,512]{1,0:T(8,128)(2,1)S(1)}, u32[]{:S(2)}, u32[]{:S(2)}) collective-permute-start(bf16[256,512]{1,0:T(8,128)(2,1)S(1)} %get-tuple-element.7.refs_1_), channel_id=1, source_target_pairs={{4,0},{8,4},{12,8},{14,12},{10,14},{6,10},{2,6},{0,2},{5,1},{9,5},... | collective-permute-start | bytes 786440 | tf_op jit(solution)/shard_map/ppermute | solution.py:121
  4.2 2.0 %collective-permute-start = (bf16[256,512]{1,0:T(8,128)(2,1)S(1)}, bf16[256,512]{1,0:T(8,128)(2,1)S(1)}, u32[]{:S(2)}, u32[]{:S(2)}) collective-permute-start(bf16[256,512]{1,0:T(8,128)(2,1)S(1)} %get-tuple-element.8.refs_0_), channel_id=1, source_target_pairs={{0,4},{4,8},{8,12},{12,14},{14,10},{10,6},{6,2},{2,0},{1,5},{5,9},... | collective-permute-start | bytes 786440 | tf_op jit(solution)/shard_map/ppermute | solution.py:120
  6.3 1.2 %dynamic_slice.13 = s32[1]{0:T(128)} dynamic-slice(s32[8]{0:T(128)} %constant.63.clone, s32[]{:T(128)S(6)} %select_n.111), dynamic_slice_sizes={1} | dynamic-slice | bytes 12 | tf_op jit(solution)/shard_map/dynamic_slice | solution.py:136
  7.5 0.7 %fusion.5 = s32[8]{0:T(128)S(1)} fusion(s32[]{:T(128)} %bitcast), kind=kLoop, calls=%fused_computation.32 | loop fusion | flops 120 | bytes 36 | tf_op jit(solution)/shard_map/select_n | solution.py:137
  8.2 1.3 %gather_fusion = s32[8]{0:T(128)S(1)} fusion(s32[8]{0:T(128)} %constant.64.clone, s32[1024]{0:T(1024)S(1)} %pad_clamp_fusion.3), kind=kCustom, calls=%fused_computation | custom fusion | bytes 96 | tf_op jit(solution)/shard_map/gather | solution.py:137
  9.5 1.3 %gather_fusion.1 = s32[8]{0:T(128)S(1)} fusion(s32[8]{0:T(128)} %param.11, s32[1024]{0:T(1024)S(1)} %pad_clamp_fusion.2), kind=kCustom, calls=%fused_computation.1 | custom fusion | bytes 96 | tf_op jit(solution)/shard_map/gather | solution.py:140
  10.8 7.3 %collective-permute-done.refs_2_ = bf16[256,512]{1,0:T(8,128)(2,1)S(1)} collective-permute-done((bf16[256,512]{1,0:T(8,128)(2,1)S(1)}, bf16[256,512]{1,0:T(8,128)(2,1)S(1)}, u32[]{:S(2)}, u32[]{:S(2)}) %collective-permute-start) | collective-permute-done | bytes 262176 | tf_op jit(solution)/shard_map/ppermute | solution.py:120
  18.1 0.4 collective-permute-start.6
  18.6 1.6 %collective-permute-start.7 = (bf16[256,512]{1,0:T(8,128)(2,1)S(1)}, bf16[256,512]{1,0:T(8,128)(2,1)S(1)}, u32[]{:S(2)}, u32[]{:S(2)}) collective-permute-start(bf16[256,512]{1,0:T(8,128)(2,1)S(1)} %collective-permute-done.3.refs_3_), channel_id=1, source_target_pairs={{4,0},{8,4},{12,8},{14,12},{10,14},{6,10},{2,6},{0,2},{5,1},{9,5},... | collective-permute-start | bytes 786440 | tf_op jit(solution)/shard_map/ppermute | solution.py:121
  20.2 0.6 %gather_fusion.2 = s32[8]{0:T(128)S(1)} fusion(s32[8]{0:T(128)S(1)} %fusion.2, s32[1024]{0:T(1024)S(1)} %get-tuple-element.14), kind=kCustom, calls=%fused_computation.2 | custom fusion | bytes 96 | tf_op jit(solution)/shard_map/gather | solution.py:145
  21.0 0.5 collective-permute-start.8
  21.4 0.7 %collective-permute-done.1 = s32[3,1]{0,1:T(1,128)S(1)} collective-permute-done((s32[3,1]{0,1:T(1,128)}, s32[3,1]{0,1:T(1,128)S(1)}, u32[]{:S(2)}, u32[]{:S(2)}) %collective-permute-start.1) | collective-permute-done | bytes 44 | tf_op jit(solution)/shard_map/ppermute | solution.py:133
  22.2 1.6 %collective-permute-start.9 = (bf16[256,512]{1,0:T(8,128)(2,1)S(1)}, bf16[256,512]{1,0:T(8,128)(2,1)S(1)}, u32[]{:S(2)}, u32[]{:S(2)}) collective-permute-start(bf16[256,512]{1,0:T(8,128)(2,1)S(1)} %collective-permute-done.5.refs_5_), channel_id=1, source_target_pairs={{4,0},{8,4},{12,8},{14,12},{10,14},{6,10},{2,6},{0,2},{5,1},{9,5},... | collective-permute-start | bytes 786440 | tf_op jit(solution)/shard_map/ppermute | solution.py:121
  23.8 3.6 %collective-permute-done.6.refs_6_ = bf16[256,512]{1,0:T(8,128)(2,1)S(1)} collective-permute-done((bf16[256,512]{1,0:T(8,128)(2,1)S(1)}, bf16[256,512]{1,0:T(8,128)(2,1)S(1)}, u32[]{:S(2)}, u32[]{:S(2)}) %collective-permute-start.6) | collective-permute-done | bytes 262176 | tf_op jit(solution)/shard_map/ppermute | solution.py:120
  27.4 0.4 collective-permute-start.10
  27.8 1.6 %collective-permute-start.11 = (bf16[256,512]{1,0:T(8,128)(2,1)S(1)}, bf16[256,512]{1,0:T(8,128)(2,1)S(1)}, u32[]{:S(2)}, u32[]{:S(2)}) collective-permute-start(bf16[256,512]{1,0:T(8,128)(2,1)S(1)} %collective-permute-done.7.refs_7_), channel_id=1, source_target_pairs={{4,0},{8,4},{12,8},{14,12},{10,14},{6,10},{2,6},{0,2},{5,1},{9,5},... | collective-permute-start | bytes 786440 | tf_op jit(solution)/shard_map/ppermute | solution.py:121
  29.4 0.7 %add_bitcast_fusion = s32[6]{0:T(128)S(1)} fusion(s32[3,1]{0,1:T(1,128)S(1)} %collective-permute-done.1, s32[3,1]{0,1:T(1,128)} %param.10), kind=kLoop, calls=%fused_computation.36 | loop fusion | flops 6 | bytes 48 | tf_op jit(solution)/shard_map/squeeze | solution.py:132
  30.1 0.6 %gather_fusion.3 = s32[8]{0:T(128)S(1)} fusion(s32[6]{0:T(128)S(1)} %add_bitcast_fusion, s32[1024]{0:T(1024)S(1)} %get-tuple-element.13), kind=kCustom, calls=%fused_computation.3 | custom fusion | bytes 96 | tf_op jit(solution)/shard_map/gather | solution.py:151
  30.8 0.6 %slice.16 = s32[1]{0:T(128)} slice(s32[8]{0:T(128)S(1)} %get-tuple-element.9.slots), slice={[4:5]} | slice | bytes 8 | tf_op jit(solution)/shard_map/slice | solution.py:166
  32.7 0.5 %slice.15.flags = s32[1]{0:T(128)} slice(s32[8]{0:T(128)S(1)} %get-tuple-element.10.flags), slice={[4:5]} | slice | bytes 8 | tf_op jit(solution)/shard_map/slice | solution.py:164
  33.9 0.4 collective-permute-start.12
  34.3 1.6 %collective-permute-start.13 = (bf16[256,512]{1,0:T(8,128)(2,1)S(1)}, bf16[256,512]{1,0:T(8,128)(2,1)S(1)}, u32[]{:S(2)}, u32[]{:S(2)}) collective-permute-start(bf16[256,512]{1,0:T(8,128)(2,1)S(1)} %collective-permute-done.9.refs_9_), channel_id=1, source_target_pairs={{4,0},{8,4},{12,8},{14,12},{10,14},{6,10},{2,6},{0,2},{5,1},{9,5},... | collective-permute-start | bytes 786440 | tf_op jit(solution)/shard_map/ppermute | solution.py:121
  36.0 2.6 %collective-permute-done.10.refs_10_ = bf16[256,512]{1,0:T(8,128)(2,1)S(1)} collective-permute-done((bf16[256,512]{1,0:T(8,128)(2,1)S(1)}, bf16[256,512]{1,0:T(8,128)(2,1)S(1)}, u32[]{:S(2)}, u32[]{:S(2)}) %collective-permute-start.10) | collective-permute-done | bytes 262176 | tf_op jit(solution)/shard_map/ppermute | solution.py:120
  39.0 1.6 %collective-permute-start.15 = (bf16[256,512]{1,0:T(8,128)(2,1)S(1)}, bf16[256,512]{1,0:T(8,128)(2,1)S(1)}, u32[]{:S(2)}, u32[]{:S(2)}) collective-permute-start(bf16[256,512]{1,0:T(8,128)(2,1)S(1)} %collective-permute-done.11.refs_11_), channel_id=1, source_target_pairs={{4,0},{8,4},{12,8},{14,12},{10,14},{6,10},{2,6},{0,2},{5,1},{9,5},... | collective-permute-start | bytes 786440 | tf_op jit(solution)/shard_map/ppermute | solution.py:127
  40.6 2.1 %pad_maximum_fusion = bf16[3072,512]{1,0:T(8,128)(2,1)S(1)} fusion(bf16[1536,512]{1,0:T(8,128)(2,1)} %collective-permute-done.2, bf16[1536,512]{1,0:T(8,128)(2,1)} %param.8), kind=kLoop, calls=%fused_computation.4 | loop fusion | flops 6291456 | bytes 6291456 | tf_op jit(solution)/shard_map/concatenate | solution.py:130
  42.8 1.4 %collective-permute-done.12.refs_12_ = bf16[256,512]{1,0:T(8,128)(2,1)S(1)} collective-permute-done((bf16[256,512]{1,0:T(8,128)(2,1)S(1)}, bf16[256,512]{1,0:T(8,128)(2,1)S(1)}, u32[]{:S(2)}, u32[]{:S(2)}) %collective-permute-start.12) | collective-permute-done | bytes 262176 | tf_op jit(solution)/shard_map/ppermute | solution.py:120
  44.2 1.3 %shard_map.73.before = f32[512,512]{1,0:T(8,128)S(1)} custom-call(s32[8]{0:T(128)S(1)} %get-tuple-element.9.slots, s32[8]{0:T(128)S(1)} %get-tuple-element.10.flags, bf16[6,512,512]{2,1,0:T(8,128)(2,1)S(1)} %bitcast.29, bf16[256,512]{1,0:T(8,128)(2,1)S(1)} %get-tuple-element.8.refs_0_, bf16[256,512]{1,0:T(8,128)(2,1)S(1)} %get-tuple-element.7.refs_1_, ...), custom_call_target="tpu_custom_call" | custom-call | flops 1879048192 | bytes 6815744 | tf_op jit(solution)/shard_map/pallas_call | solution.py:84
  45.5 2.6 %collective-permute-done.14.refs_0_ = bf16[256,512]{1,0:T(8,128)(2,1)S(1)} collective-permute-done((bf16[256,512]{1,0:T(8,128)(2,1)S(1)}, bf16[256,512]{1,0:T(8,128)(2,1)S(1)}, u32[]{:S(2)}, u32[]{:S(2)}) %collective-permute-start.14) | collective-permute-done | bytes 262176 | tf_op jit(solution)/shard_map/ppermute | solution.py:126
  48.2 0.5 collective-permute-done.15.refs_1_
  48.7 1.5 %shard_map.74 = bf16[512,512]{1,0:T(8,128)(2,1)} custom-call(s32[1]{0:T(128)} %constant.49.clone.1.slots, s32[1]{0:T(128)} %slice.15.flags, bf16[1,512,512]{2,1,0:T(8,128)(2,1)S(1)} %constant_dynamic-slice_fusion.1.inner, f32[512,512]{1,0:T(8,128)S(1)} %shard_map.73.before, bf16[256,512]{1,0:T(8,128)(2,1)S(1)} %collective-permute-done.14.refs_0_, ...), custom_call_target="tpu_custom_call" | custom-call | flops 268435456 | bytes 2097152 | tf_op jit(solution)/shard_map/pallas_call | solution.py:84
  (23 shorter events, 0.8 us)
Async XLA Ops:
  0.0 20.2 %copy-start = (s32[2,8]{1,0:T(2,128)S(1)}, s32[2,8]{1,0:T(2,128)}, u32[]{:S(2)}) copy-start(s32[2,8]{1,0:T(2,128)} %param.9) | copy-start | bytes 196
  0.0 40.6 %collective-permute-start.2 = (bf16[1536,512]{1,0:T(8,128)(2,1)}, bf16[1536,512]{1,0:T(8,128)(2,1)}, u32[]{:S(2)}, u32[]{:S(2)}) collective-permute-start(bf16[1536,512]{1,0:T(8,128)(2,1)} %param.8), channel_id=1, source_target_pairs={{0,1},{1,0},{2,3},{3,2},{4,5},{5,4},{6,7},{7,6},{8,9},{9,8},{10,11... | collective-permute-start | bytes 4718600 | tf_op jit(solution)/shard_map/ppermute | solution.py:129
  1.5 17.0 %collective-permute-start.3 = (bf16[256,512]{1,0:T(8,128)(2,1)S(1)}, bf16[256,512]{1,0:T(8,128)(2,1)S(1)}, u32[]{:S(2)}, u32[]{:S(2)}) collective-permute-start(bf16[256,512]{1,0:T(8,128)(2,1)S(1)} %get-tuple-element.7.refs_1_), channel_id=1, source_target_pairs={{4,0},{8,4},{12,8},{14,12},{10,14},{6,10},{2,6},{0,2},{5,1},{9,5},... | collective-permute-start | bytes 786440 | tf_op jit(solution)/shard_map/ppermute | solution.py:121
  4.1 16.8 %collective-permute-start.4 = (bf16[256,512]{1,0:T(8,128)(2,1)S(1)}, bf16[256,512]{1,0:T(8,128)(2,1)S(1)}, u32[]{:S(2)}, u32[]{:S(2)}) collective-permute-start(bf16[256,512]{1,0:T(8,128)(2,1)S(1)} %get-tuple-element.7.refs_1_), channel_id=1, source_target_pairs={{0,4},{4,8},{8,12},{12,14},{14,10},{10,6},{6,2},{2,0},{1,5},{5,9},... | collective-permute-start | bytes 786440 | tf_op jit(solution)/shard_map/ppermute | solution.py:120
  4.2 13.9 %collective-permute-start = (bf16[256,512]{1,0:T(8,128)(2,1)S(1)}, bf16[256,512]{1,0:T(8,128)(2,1)S(1)}, u32[]{:S(2)}, u32[]{:S(2)}) collective-permute-start(bf16[256,512]{1,0:T(8,128)(2,1)S(1)} %get-tuple-element.8.refs_0_), channel_id=1, source_target_pairs={{0,4},{4,8},{8,12},{12,14},{14,10},{10,6},{6,2},{2,0},{1,5},{5,9},... | collective-permute-start | bytes 786440 | tf_op jit(solution)/shard_map/ppermute | solution.py:120
  6.2 14.8 %collective-permute-start.5 = (bf16[256,512]{1,0:T(8,128)(2,1)S(1)}, bf16[256,512]{1,0:T(8,128)(2,1)S(1)}, u32[]{:S(2)}, u32[]{:S(2)}) collective-permute-start(bf16[256,512]{1,0:T(8,128)(2,1)S(1)} %get-tuple-element.8.refs_0_), channel_id=1, source_target_pairs={{4,0},{8,4},{12,8},{14,12},{10,14},{6,10},{2,6},{0,2},{5,1},{9,5},... | collective-permute-start | bytes 786440 | tf_op jit(solution)/shard_map/ppermute | solution.py:121
  18.1 9.2 %collective-permute-start.6 = (bf16[256,512]{1,0:T(8,128)(2,1)S(1)}, bf16[256,512]{1,0:T(8,128)(2,1)S(1)}, u32[]{:S(2)}, u32[]{:S(2)}) collective-permute-start(bf16[256,512]{1,0:T(8,128)(2,1)S(1)} %collective-permute-done.refs_2_), channel_id=1, source_target_pairs={{0,4},{4,8},{8,12},{12,14},{14,10},{10,6},{6,2},{2,0},{1,5},{5,9},... | collective-permute-start | bytes 786440 | tf_op jit(solution)/shard_map/ppermute | solution.py:120
  18.6 9.2 %collective-permute-start.7 = (bf16[256,512]{1,0:T(8,128)(2,1)S(1)}, bf16[256,512]{1,0:T(8,128)(2,1)S(1)}, u32[]{:S(2)}, u32[]{:S(2)}) collective-permute-start(bf16[256,512]{1,0:T(8,128)(2,1)S(1)} %collective-permute-done.3.refs_3_), channel_id=1, source_target_pairs={{4,0},{8,4},{12,8},{14,12},{10,14},{6,10},{2,6},{0,2},{5,1},{9,5},... | collective-permute-start | bytes 786440 | tf_op jit(solution)/shard_map/ppermute | solution.py:121
  20.9 1.3 %collective-permute-start.1 = (s32[3,1]{0,1:T(1,128)}, s32[3,1]{0,1:T(1,128)S(1)}, u32[]{:S(2)}, u32[]{:S(2)}) collective-permute-start(s32[3,1]{0,1:T(1,128)} %param.10), channel_id=1, source_target_pairs={{0,1},{1,0},{2,3},{3,2},{4,5},{5,4},{6,7},{7,6},{8,9},{9,8},{10,11... | collective-permute-start | bytes 44 | tf_op jit(solution)/shard_map/ppermute | solution.py:133
  21.0 12.9 %collective-permute-start.8 = (bf16[256,512]{1,0:T(8,128)(2,1)S(1)}, bf16[256,512]{1,0:T(8,128)(2,1)S(1)}, u32[]{:S(2)}, u32[]{:S(2)}) collective-permute-start(bf16[256,512]{1,0:T(8,128)(2,1)S(1)} %collective-permute-done.4.refs_4_), channel_id=1, source_target_pairs={{0,4},{4,8},{8,12},{12,14},{14,10},{10,6},{6,2},{2,0},{1,5},{5,9},... | collective-permute-start | bytes 786440 | tf_op jit(solution)/shard_map/ppermute | solution.py:120
  22.2 12.2 %collective-permute-start.9 = (bf16[256,512]{1,0:T(8,128)(2,1)S(1)}, bf16[256,512]{1,0:T(8,128)(2,1)S(1)}, u32[]{:S(2)}, u32[]{:S(2)}) collective-permute-start(bf16[256,512]{1,0:T(8,128)(2,1)S(1)} %collective-permute-done.5.refs_5_), channel_id=1, source_target_pairs={{4,0},{8,4},{12,8},{14,12},{10,14},{6,10},{2,6},{0,2},{5,1},{9,5},... | collective-permute-start | bytes 786440 | tf_op jit(solution)/shard_map/ppermute | solution.py:121
  27.4 11.2 %collective-permute-start.10 = (bf16[256,512]{1,0:T(8,128)(2,1)S(1)}, bf16[256,512]{1,0:T(8,128)(2,1)S(1)}, u32[]{:S(2)}, u32[]{:S(2)}) collective-permute-start(bf16[256,512]{1,0:T(8,128)(2,1)S(1)} %collective-permute-done.6.refs_6_), channel_id=1, source_target_pairs={{0,4},{4,8},{8,12},{12,14},{14,10},{10,6},{6,2},{2,0},{1,5},{5,9},... | collective-permute-start | bytes 786440 | tf_op jit(solution)/shard_map/ppermute | solution.py:120
  27.8 11.2 %collective-permute-start.11 = (bf16[256,512]{1,0:T(8,128)(2,1)S(1)}, bf16[256,512]{1,0:T(8,128)(2,1)S(1)}, u32[]{:S(2)}, u32[]{:S(2)}) collective-permute-start(bf16[256,512]{1,0:T(8,128)(2,1)S(1)} %collective-permute-done.7.refs_7_), channel_id=1, source_target_pairs={{4,0},{8,4},{12,8},{14,12},{10,14},{6,10},{2,6},{0,2},{5,1},{9,5},... | collective-permute-start | bytes 786440 | tf_op jit(solution)/shard_map/ppermute | solution.py:121
  33.9 10.3 %collective-permute-start.12 = (bf16[256,512]{1,0:T(8,128)(2,1)S(1)}, bf16[256,512]{1,0:T(8,128)(2,1)S(1)}, u32[]{:S(2)}, u32[]{:S(2)}) collective-permute-start(bf16[256,512]{1,0:T(8,128)(2,1)S(1)} %collective-permute-done.8.refs_8_), channel_id=1, source_target_pairs={{0,4},{4,8},{8,12},{12,14},{14,10},{10,6},{6,2},{2,0},{1,5},{5,9},... | collective-permute-start | bytes 786440 | tf_op jit(solution)/shard_map/ppermute | solution.py:120
  34.3 9.9 %collective-permute-start.13 = (bf16[256,512]{1,0:T(8,128)(2,1)S(1)}, bf16[256,512]{1,0:T(8,128)(2,1)S(1)}, u32[]{:S(2)}, u32[]{:S(2)}) collective-permute-start(bf16[256,512]{1,0:T(8,128)(2,1)S(1)} %collective-permute-done.9.refs_9_), channel_id=1, source_target_pairs={{4,0},{8,4},{12,8},{14,12},{10,14},{6,10},{2,6},{0,2},{5,1},{9,5},... | collective-permute-start | bytes 786440 | tf_op jit(solution)/shard_map/ppermute | solution.py:121
  38.6 9.6 %collective-permute-start.14 = (bf16[256,512]{1,0:T(8,128)(2,1)S(1)}, bf16[256,512]{1,0:T(8,128)(2,1)S(1)}, u32[]{:S(2)}, u32[]{:S(2)}) collective-permute-start(bf16[256,512]{1,0:T(8,128)(2,1)S(1)} %collective-permute-done.10.refs_10_), channel_id=1, source_target_pairs={{0,4},{4,8},{8,12},{12,14},{14,10},{10,6},{6,2},{2,0},{1,5},{5,9},... | collective-permute-start | bytes 786440 | tf_op jit(solution)/shard_map/ppermute | solution.py:126
  39.0 9.7 %collective-permute-start.15 = (bf16[256,512]{1,0:T(8,128)(2,1)S(1)}, bf16[256,512]{1,0:T(8,128)(2,1)S(1)}, u32[]{:S(2)}, u32[]{:S(2)}) collective-permute-start(bf16[256,512]{1,0:T(8,128)(2,1)S(1)} %collective-permute-done.11.refs_11_), channel_id=1, source_target_pairs={{4,0},{8,4},{12,8},{14,12},{10,14},{6,10},{2,6},{0,2},{5,1},{9,5},... | collective-permute-start | bytes 786440 | tf_op jit(solution)/shard_map/ppermute | solution.py:127

commit v3 on v2

--- a/solution.py
+++ b/solution.py
@@ -113,7 +113,8 @@
     own = lax.dynamic_slice_in_dim(band_held, depth_index * size, size, 0)
     first = [own[:half], own[half:]]
     pieces = {(0, 0): first[0], (0, 1): first[1]}
-    right, left = list(first), list(first)
+    late = lax.optimization_barrier((own[:half], own[half:], inner_mask))
+    right, left = [first[0], late[1]], [late[0], first[1]]
     steps = (grid_size - 1) // 2
     for step in range(1, steps + 1):
         for h in (0, 1):

time: 50.6 us -> 48 us (0.949)
  waiting for transfers between devices: 18.9 us -> 16.2 us
  Pallas kernels: 2.78 us -> 3.33 us
    ppermute x6, starting transfers between devices: 9.05 us -> 0.46 us  [gather_columns(): left[1 - h] = lax.ppermute(left[1 - h], 'grid', backward)]
    ppermute x6, starting transfers between devices: 3.87 us -> 12.4 us  [gather_columns(): right[h] = lax.ppermute(right[h], 'grid', onward)]
    ppermute x6, waiting for transfers between devices: 15 us -> 8.98 us  [gather_columns(): right[h] = lax.ppermute(right[h], 'grid', onward)]
    ppermute x6, waiting for transfers between devices: 0.02 us -> 4.17 us  [gather_columns(): left[1 - h] = lax.ppermute(left[1 - h], 'grid', backward)]
    ppermute x1, starting transfers between devices: 1.63 us -> 0.04 us  [gather_columns(): last[steps + 1, 1] = lax.ppermute(left[1], 'grid', backward)]
    ppermute x1, starting transfers between devices: 0.4 us -> 1.95 us  [gather_columns(): last[steps + 1, 0] = lax.ppermute(right[0], 'grid', onward)]
    ppermute x1, waiting for transfers between devices: 2.64 us -> 1.48 us  [gather_columns(): last[steps + 1, 0] = lax.ppermute(right[0], 'grid', onward)]
    ppermute x1, waiting for transfers between devices: 0.49 us -> 1.55 us  [gather_columns(): last[steps + 1, 1] = lax.ppermute(left[1], 'grid', backward)]
  transfers between devices with their start and end apart: 16 -> 16, of which waited for: 7 -> 9; matrix products, arithmetic and copies ran while one was open for 22% -> 23% of each run, Pallas kernels for 3% -> 4%
where the time goes in v3:
time: 48 us; the launch traced here: 47.8 us
  waiting for transfers between devices  16.2 us (34%)
  starting transfers between devices  15.3 us (32%)
  local copies, waits for them, and re-layouts  7.37 us (15%)
  other arithmetic  3.54 us (7%)
  Pallas kernels  3.33 us (7%)
  between operations  2.05 us (4%)
    ppermute x6, starting transfers between devices, gather_columns(): right[h] = lax.ppermute(right[h], 'grid', onward)  12.4 us
    ppermute x6, waiting for transfers between devices, gather_columns(): right[h] = lax.ppermute(right[h], 'grid', onward)  8.98 us
    ppermute x6, waiting for transfers between devices, gather_columns(): left[1 - h] = lax.ppermute(left[1 - h], 'grid', backward)  4.17 us
    pallas_call x2, Pallas kernels, multiply(): pl.pallas_call(functools.partial(kernel, places), out_shape=out_shape, in...  3.33 us
    concatenate x1, other arithmetic, gather_columns(): jnp.concatenate([inner_tiles, swapped], axis=0).reshape(-1, size, size)  2.09 us
    ppermute x1, starting transfers between devices, gather_columns(): last[steps + 1, 0] = lax.ppermute(right[0], 'grid', onward)  1.95 us
    ppermute x1, waiting for transfers between devices, gather_columns(): last[steps + 1, 1] = lax.ppermute(left[1], 'grid', backward)  1.55 us
    ppermute x1, waiting for transfers between devices, gather_columns(): last[steps + 1, 0] = lax.ppermute(right[0], 'grid', onward)  1.48 us
  transfers between devices with their start and end apart: 16, of which 9 were waited for; matrix products, arithmetic and copies ran while one was open for 23% of the time, Pallas kernels for 4%

profile of v3, /device:TPU:0, one launch (start us, length us, event | category | flops | bytes accessed | tf_op | source)
XLA Modules:
  0.0 47.8 jit_solution(11836102912131833951)
XLA Ops:
  0.0 0.5 collective-permute-start.2
  0.5 1.1 %constant_dynamic-slice_fusion.2 = (bf16[256,512]{1,0:T(8,128)(2,1)S(1)}, bf16[256,512]{1,0:T(8,128)(2,1)S(1)}) fusion(bf16[1024,512]{1,0:T(8,128)(2,1)} %param.7, s32[]{:T(128)S(6)} %add.135, s32[]{:T(128)S(6)} %select_n.118), kind=kLoop, calls=%fused_computation.25 | loop fusion | bytes 1048584 | tf_op jit(solution)/shard_map/slice | solution.py:114
  1.5 2.6 %collective-permute-start = (bf16[256,512]{1,0:T(8,128)(2,1)S(1)}, bf16[256,512]{1,0:T(8,128)(2,1)S(1)}, u32[]{:S(2)}, u32[]{:S(2)}) collective-permute-start(bf16[256,512]{1,0:T(8,128)(2,1)S(1)} %get-tuple-element.10.refs_0_), channel_id=1, source_target_pairs={{0,4},{4,8},{8,12},{12,14},{14,10},{10,6},{6,2},{2,0},{1,5},{5,9},... | collective-permute-start | bytes 786440 | tf_op jit(solution)/shard_map/ppermute | solution.py:121
  4.2 2.0 %collective-permute-start.4 = (bf16[256,512]{1,0:T(8,128)(2,1)S(1)}, bf16[256,512]{1,0:T(8,128)(2,1)S(1)}, u32[]{:S(2)}, u32[]{:S(2)}) collective-permute-start(bf16[256,512]{1,0:T(8,128)(2,1)S(1)} %get-tuple-element.9.refs_1_), channel_id=1, source_target_pairs={{0,4},{4,8},{8,12},{12,14},{14,10},{10,6},{6,2},{2,0},{1,5},{5,9},... | collective-permute-start | bytes 786440 | tf_op jit(solution)/shard_map/ppermute | solution.py:121
  6.2 1.2 %dynamic_slice.13 = s32[1]{0:T(128)} dynamic-slice(s32[8]{0:T(128)} %constant.63.clone, s32[]{:T(128)S(6)} %select_n.111), dynamic_slice_sizes={1} | dynamic-slice | bytes 12 | tf_op jit(solution)/shard_map/dynamic_slice | solution.py:137
  7.4 0.7 %fusion.5 = s32[8]{0:T(128)S(1)} fusion(s32[]{:T(128)} %bitcast), kind=kLoop, calls=%fused_computation.32 | loop fusion | flops 120 | bytes 36 | tf_op jit(solution)/shard_map/select_n | solution.py:138
  8.1 1.3 %gather_fusion = s32[8]{0:T(128)S(1)} fusion(s32[8]{0:T(128)} %constant.64.clone, s32[1024]{0:T(1024)S(1)} %pad_clamp_fusion.3), kind=kCustom, calls=%fused_computation | custom fusion | bytes 96 | tf_op jit(solution)/shard_map/gather | solution.py:138
  9.4 1.3 %gather_fusion.1 = s32[8]{0:T(128)S(1)} fusion(s32[8]{0:T(128)} %param.11, s32[1024]{0:T(1024)S(1)} %pad_clamp_fusion.2), kind=kCustom, calls=%fused_computation.1 | custom fusion | bytes 96 | tf_op jit(solution)/shard_map/gather | solution.py:141
  10.7 0.5 %collective-permute-done.refs_2_ = bf16[256,512]{1,0:T(8,128)(2,1)S(1)} collective-permute-done((bf16[256,512]{1,0:T(8,128)(2,1)S(1)}, bf16[256,512]{1,0:T(8,128)(2,1)S(1)}, u32[]{:S(2)}, u32[]{:S(2)}) %collective-permute-start) | collective-permute-done | bytes 262176 | tf_op jit(solution)/shard_map/ppermute | solution.py:121
  11.2 2.0 %collective-permute-start.6 = (bf16[256,512]{1,0:T(8,128)(2,1)S(1)}, bf16[256,512]{1,0:T(8,128)(2,1)S(1)}, u32[]{:S(2)}, u32[]{:S(2)}) collective-permute-start(bf16[256,512]{1,0:T(8,128)(2,1)S(1)} %collective-permute-done.refs_2_), channel_id=1, source_target_pairs={{0,4},{4,8},{8,12},{12,14},{14,10},{10,6},{6,2},{2,0},{1,5},{5,9},... | collective-permute-start | bytes 786440 | tf_op jit(solution)/shard_map/ppermute | solution.py:121
  13.4 0.6 %gather_fusion.2 = s32[8]{0:T(128)S(1)} fusion(s32[8]{0:T(128)S(1)} %fusion.2, s32[1024]{0:T(1024)S(1)} %get-tuple-element.18), kind=kCustom, calls=%fused_computation.2 | custom fusion | bytes 96 | tf_op jit(solution)/shard_map/gather | solution.py:146
  14.0 2.8 %collective-permute-done.4.refs_4_ = bf16[256,512]{1,0:T(8,128)(2,1)S(1)} collective-permute-done((bf16[256,512]{1,0:T(8,128)(2,1)S(1)}, bf16[256,512]{1,0:T(8,128)(2,1)S(1)}, u32[]{:S(2)}, u32[]{:S(2)}) %collective-permute-start.4) | collective-permute-done | bytes 262176 | tf_op jit(solution)/shard_map/ppermute | solution.py:121
  16.9 2.1 %collective-permute-done.5.refs_5_ = bf16[256,512]{1,0:T(8,128)(2,1)S(1)} collective-permute-done((bf16[256,512]{1,0:T(8,128)(2,1)S(1)}, bf16[256,512]{1,0:T(8,128)(2,1)S(1)}, u32[]{:S(2)}, u32[]{:S(2)}) %collective-permute-start.5) | collective-permute-done | bytes 262176 | tf_op jit(solution)/shard_map/ppermute | solution.py:122
  18.9 1.6 %collective-permute-start.8 = (bf16[256,512]{1,0:T(8,128)(2,1)S(1)}, bf16[256,512]{1,0:T(8,128)(2,1)S(1)}, u32[]{:S(2)}, u32[]{:S(2)}) collective-permute-start(bf16[256,512]{1,0:T(8,128)(2,1)S(1)} %collective-permute-done.4.refs_4_), channel_id=1, source_target_pairs={{0,4},{4,8},{8,12},{12,14},{14,10},{10,6},{6,2},{2,0},{1,5},{5,9},... | collective-permute-start | bytes 786440 | tf_op jit(solution)/shard_map/ppermute | solution.py:121
  20.5 0.4 collective-permute-start.9
  21.0 1.5 %collective-permute-done.6.refs_6_ = bf16[256,512]{1,0:T(8,128)(2,1)S(1)} collective-permute-done((bf16[256,512]{1,0:T(8,128)(2,1)S(1)}, bf16[256,512]{1,0:T(8,128)(2,1)S(1)}, u32[]{:S(2)}, u32[]{:S(2)}) %collective-permute-start.6) | collective-permute-done | bytes 262176 | tf_op jit(solution)/shard_map/ppermute | solution.py:121
  22.5 2.0 %collective-permute-start.10 = (bf16[256,512]{1,0:T(8,128)(2,1)S(1)}, bf16[256,512]{1,0:T(8,128)(2,1)S(1)}, u32[]{:S(2)}, u32[]{:S(2)}) collective-permute-start(bf16[256,512]{1,0:T(8,128)(2,1)S(1)} %collective-permute-done.6.refs_6_), channel_id=1, source_target_pairs={{0,4},{4,8},{8,12},{12,14},{14,10},{10,6},{6,2},{2,0},{1,5},{5,9},... | collective-permute-start | bytes 786440 | tf_op jit(solution)/shard_map/ppermute | solution.py:121
  24.5 0.7 %add_bitcast_fusion = s32[6]{0:T(128)S(1)} fusion(s32[3,1]{0,1:T(1,128)S(1)} %collective-permute-done.1, s32[3,1]{0,1:T(1,128)} %param.10), kind=kLoop, calls=%fused_computation.36 | loop fusion | flops 6 | bytes 48 | tf_op jit(solution)/shard_map/squeeze | solution.py:133
  25.3 0.6 %gather_fusion.3 = s32[8]{0:T(128)S(1)} fusion(s32[6]{0:T(128)S(1)} %add_bitcast_fusion, s32[1024]{0:T(1024)S(1)} %get-tuple-element.17), kind=kCustom, calls=%fused_computation.3 | custom fusion | bytes 96 | tf_op jit(solution)/shard_map/gather | solution.py:152
  25.9 0.6 %slice.18 = s32[1]{0:T(128)} slice(s32[8]{0:T(128)S(1)} %get-tuple-element.13.slots), slice={[4:5]} | slice | bytes 8 | tf_op jit(solution)/shard_map/slice | solution.py:167
  27.8 0.5 %slice.17.flags = s32[1]{0:T(128)} slice(s32[8]{0:T(128)S(1)} %get-tuple-element.14.flags), slice={[4:5]} | slice | bytes 8 | tf_op jit(solution)/shard_map/slice | solution.py:165
  29.0 2.1 %collective-permute-start.12 = (bf16[256,512]{1,0:T(8,128)(2,1)S(1)}, bf16[256,512]{1,0:T(8,128)(2,1)S(1)}, u32[]{:S(2)}, u32[]{:S(2)}) collective-permute-start(bf16[256,512]{1,0:T(8,128)(2,1)S(1)} %collective-permute-done.8.refs_8_), channel_id=1, source_target_pairs={{0,4},{4,8},{8,12},{12,14},{14,10},{10,6},{6,2},{2,0},{1,5},{5,9},... | collective-permute-start | bytes 786440 | tf_op jit(solution)/shard_map/ppermute | solution.py:121
  31.1 2.7 %collective-permute-done.10.refs_10_ = bf16[256,512]{1,0:T(8,128)(2,1)S(1)} collective-permute-done((bf16[256,512]{1,0:T(8,128)(2,1)S(1)}, bf16[256,512]{1,0:T(8,128)(2,1)S(1)}, u32[]{:S(2)}, u32[]{:S(2)}) %collective-permute-start.10) | collective-permute-done | bytes 262176 | tf_op jit(solution)/shard_map/ppermute | solution.py:121
  33.8 2.0 %collective-permute-start.14 = (bf16[256,512]{1,0:T(8,128)(2,1)S(1)}, bf16[256,512]{1,0:T(8,128)(2,1)S(1)}, u32[]{:S(2)}, u32[]{:S(2)}) collective-permute-start(bf16[256,512]{1,0:T(8,128)(2,1)S(1)} %collective-permute-done.10.refs_10_), channel_id=1, source_target_pairs={{0,4},{4,8},{8,12},{12,14},{14,10},{10,6},{6,2},{2,0},{1,5},{5,9},... | collective-permute-start | bytes 786440 | tf_op jit(solution)/shard_map/ppermute | solution.py:127
  35.8 0.0 collective-permute-start.15
  35.8 2.1 %pad_maximum_fusion = bf16[3072,512]{1,0:T(8,128)(2,1)S(1)} fusion(bf16[1536,512]{1,0:T(8,128)(2,1)} %collective-permute-done.2, bf16[1536,512]{1,0:T(8,128)(2,1)} %param.8), kind=kLoop, calls=%fused_computation.4 | loop fusion | flops 6291456 | bytes 6291456 | tf_op jit(solution)/shard_map/concatenate | solution.py:131
  38.0 1.4 %collective-permute-done.12.refs_12_ = bf16[256,512]{1,0:T(8,128)(2,1)S(1)} collective-permute-done((bf16[256,512]{1,0:T(8,128)(2,1)S(1)}, bf16[256,512]{1,0:T(8,128)(2,1)S(1)}, u32[]{:S(2)}, u32[]{:S(2)}) %collective-permute-start.12) | collective-permute-done | bytes 262176 | tf_op jit(solution)/shard_map/ppermute | solution.py:121
  39.4 2.0 %collective-permute-done.13.refs_13_ = bf16[256,512]{1,0:T(8,128)(2,1)S(1)} collective-permute-done((bf16[256,512]{1,0:T(8,128)(2,1)S(1)}, bf16[256,512]{1,0:T(8,128)(2,1)S(1)}, u32[]{:S(2)}, u32[]{:S(2)}) %collective-permute-start.13) | collective-permute-done | bytes 262176 | tf_op jit(solution)/shard_map/ppermute | solution.py:122
  41.4 1.9 %shard_map.73.before = f32[512,512]{1,0:T(8,128)S(1)} custom-call(s32[8]{0:T(128)S(1)} %get-tuple-element.13.slots, s32[8]{0:T(128)S(1)} %get-tuple-element.14.flags, bf16[6,512,512]{2,1,0:T(8,128)(2,1)S(1)} %bitcast.29, bf16[256,512]{1,0:T(8,128)(2,1)S(1)} %get-tuple-element.10.refs_0_, bf16[256,512]{1,0:T(8,128)(2,1)S(1)} %get-tuple-element.9.refs_1_, ...), custom_call_target="tpu_custom_call" | custom-call | flops 1879048192 | bytes 6815744 | tf_op jit(solution)/shard_map/pallas_call | solution.py:84
  43.3 1.5 %collective-permute-done.14.refs_0_ = bf16[256,512]{1,0:T(8,128)(2,1)S(1)} collective-permute-done((bf16[256,512]{1,0:T(8,128)(2,1)S(1)}, bf16[256,512]{1,0:T(8,128)(2,1)S(1)}, u32[]{:S(2)}, u32[]{:S(2)}) %collective-permute-start.14) | collective-permute-done | bytes 262176 | tf_op jit(solution)/shard_map/ppermute | solution.py:127
  44.7 1.5 %collective-permute-done.15.refs_1_ = bf16[256,512]{1,0:T(8,128)(2,1)S(1)} collective-permute-done((bf16[256,512]{1,0:T(8,128)(2,1)S(1)}, bf16[256,512]{1,0:T(8,128)(2,1)S(1)}, u32[]{:S(2)}, u32[]{:S(2)}) %collective-permute-start.15) | collective-permute-done | bytes 262176 | tf_op jit(solution)/shard_map/ppermute | solution.py:128
  46.3 1.5 %shard_map.74 = bf16[512,512]{1,0:T(8,128)(2,1)} custom-call(s32[1]{0:T(128)} %constant.49.clone.1.slots, s32[1]{0:T(128)} %slice.17.flags, bf16[1,512,512]{2,1,0:T(8,128)(2,1)S(1)} %constant_dynamic-slice_fusion.1.inner, f32[512,512]{1,0:T(8,128)S(1)} %shard_map.73.before, bf16[256,512]{1,0:T(8,128)(2,1)S(1)} %collective-permute-done.14.refs_0_, ...), custom_call_target="tpu_custom_call" | custom-call | flops 268435456 | bytes 2097152 | tf_op jit(solution)/shard_map/pallas_call | solution.py:84
  (23 shorter events, 0.3 us)
Async XLA Ops:
  0.0 13.3 %copy-start = (s32[2,8]{1,0:T(2,128)S(1)}, s32[2,8]{1,0:T(2,128)}, u32[]{:S(2)}) copy-start(s32[2,8]{1,0:T(2,128)} %param.9) | copy-start | bytes 196
  0.0 35.8 %collective-permute-start.2 = (bf16[1536,512]{1,0:T(8,128)(2,1)}, bf16[1536,512]{1,0:T(8,128)(2,1)}, u32[]{:S(2)}, u32[]{:S(2)}) collective-permute-start(bf16[1536,512]{1,0:T(8,128)(2,1)} %param.8), channel_id=1, source_target_pairs={{0,1},{1,0},{2,3},{3,2},{4,5},{5,4},{6,7},{7,6},{8,9},{9,8},{10,11... | collective-permute-start | bytes 4718600 | tf_op jit(solution)/shard_map/ppermute | solution.py:130
  1.5 9.7 %collective-permute-start = (bf16[256,512]{1,0:T(8,128)(2,1)S(1)}, bf16[256,512]{1,0:T(8,128)(2,1)S(1)}, u32[]{:S(2)}, u32[]{:S(2)}) collective-permute-start(bf16[256,512]{1,0:T(8,128)(2,1)S(1)} %get-tuple-element.10.refs_0_), channel_id=1, source_target_pairs={{0,4},{4,8},{8,12},{12,14},{14,10},{10,6},{6,2},{2,0},{1,5},{5,9},... | collective-permute-start | bytes 786440 | tf_op jit(solution)/shard_map/ppermute | solution.py:121
  4.2 9.1 %collective-permute-start.3 = (bf16[256,512]{1,0:T(8,128)(2,1)S(1)}, bf16[256,512]{1,0:T(8,128)(2,1)S(1)}, u32[]{:S(2)}, u32[]{:S(2)}) collective-permute-start(bf16[256,512]{1,0:T(8,128)(2,1)S(1)} %get-tuple-element.9.refs_1_), channel_id=1, source_target_pairs={{4,0},{8,4},{12,8},{14,12},{10,14},{6,10},{2,6},{0,2},{5,1},{9,5},... | collective-permute-start | bytes 786440 | tf_op jit(solution)/shard_map/ppermute | solution.py:122
  4.2 12.7 %collective-permute-start.4 = (bf16[256,512]{1,0:T(8,128)(2,1)S(1)}, bf16[256,512]{1,0:T(8,128)(2,1)S(1)}, u32[]{:S(2)}, u32[]{:S(2)}) collective-permute-start(bf16[256,512]{1,0:T(8,128)(2,1)S(1)} %get-tuple-element.9.refs_1_), channel_id=1, source_target_pairs={{0,4},{4,8},{8,12},{12,14},{14,10},{10,6},{6,2},{2,0},{1,5},{5,9},... | collective-permute-start | bytes 786440 | tf_op jit(solution)/shard_map/ppermute | solution.py:121
  6.2 12.7 %collective-permute-start.5 = (bf16[256,512]{1,0:T(8,128)(2,1)S(1)}, bf16[256,512]{1,0:T(8,128)(2,1)S(1)}, u32[]{:S(2)}, u32[]{:S(2)}) collective-permute-start(bf16[256,512]{1,0:T(8,128)(2,1)S(1)} %get-tuple-element.10.refs_0_), channel_id=1, source_target_pairs={{4,0},{8,4},{12,8},{14,12},{10,14},{6,10},{2,6},{0,2},{5,1},{9,5},... | collective-permute-start | bytes 786440 | tf_op jit(solution)/shard_map/ppermute | solution.py:122
  11.2 11.2 %collective-permute-start.6 = (bf16[256,512]{1,0:T(8,128)(2,1)S(1)}, bf16[256,512]{1,0:T(8,128)(2,1)S(1)}, u32[]{:S(2)}, u32[]{:S(2)}) collective-permute-start(bf16[256,512]{1,0:T(8,128)(2,1)S(1)} %collective-permute-done.refs_2_), channel_id=1, source_target_pairs={{0,4},{4,8},{8,12},{12,14},{14,10},{10,6},{6,2},{2,0},{1,5},{5,9},... | collective-permute-start | bytes 786440 | tf_op jit(solution)/shard_map/ppermute | solution.py:121
  13.3 11.2 %collective-permute-start.7 = (bf16[256,512]{1,0:T(8,128)(2,1)S(1)}, bf16[256,512]{1,0:T(8,128)(2,1)S(1)}, u32[]{:S(2)}, u32[]{:S(2)}) collective-permute-start(bf16[256,512]{1,0:T(8,128)(2,1)S(1)} %collective-permute-done.3.refs_3_), channel_id=1, source_target_pairs={{4,0},{8,4},{12,8},{14,12},{10,14},{6,10},{2,6},{0,2},{5,1},{9,5},... | collective-permute-start | bytes 786440 | tf_op jit(solution)/shard_map/ppermute | solution.py:122
  16.9 3.6 %collective-permute-start.1 = (s32[3,1]{0,1:T(1,128)}, s32[3,1]{0,1:T(1,128)S(1)}, u32[]{:S(2)}, u32[]{:S(2)}) collective-permute-start(s32[3,1]{0,1:T(1,128)} %param.10), channel_id=1, source_target_pairs={{0,1},{1,0},{2,3},{3,2},{4,5},{5,4},{6,7},{7,6},{8,9},{9,8},{10,11... | collective-permute-start | bytes 44 | tf_op jit(solution)/shard_map/ppermute | solution.py:134
  18.9 10.1 %collective-permute-start.8 = (bf16[256,512]{1,0:T(8,128)(2,1)S(1)}, bf16[256,512]{1,0:T(8,128)(2,1)S(1)}, u32[]{:S(2)}, u32[]{:S(2)}) collective-permute-start(bf16[256,512]{1,0:T(8,128)(2,1)S(1)} %collective-permute-done.4.refs_4_), channel_id=1, source_target_pairs={{0,4},{4,8},{8,12},{12,14},{14,10},{10,6},{6,2},{2,0},{1,5},{5,9},... | collective-permute-start | bytes 786440 | tf_op jit(solution)/shard_map/ppermute | solution.py:121
  20.5 10.6 %collective-permute-start.9 = (bf16[256,512]{1,0:T(8,128)(2,1)S(1)}, bf16[256,512]{1,0:T(8,128)(2,1)S(1)}, u32[]{:S(2)}, u32[]{:S(2)}) collective-permute-start(bf16[256,512]{1,0:T(8,128)(2,1)S(1)} %collective-permute-done.5.refs_5_), channel_id=1, source_target_pairs={{4,0},{8,4},{12,8},{14,12},{10,14},{6,10},{2,6},{0,2},{5,1},{9,5},... | collective-permute-start | bytes 786440 | tf_op jit(solution)/shard_map/ppermute | solution.py:122
  22.5 11.3 %collective-permute-start.10 = (bf16[256,512]{1,0:T(8,128)(2,1)S(1)}, bf16[256,512]{1,0:T(8,128)(2,1)S(1)}, u32[]{:S(2)}, u32[]{:S(2)}) collective-permute-start(bf16[256,512]{1,0:T(8,128)(2,1)S(1)} %collective-permute-done.6.refs_6_), channel_id=1, source_target_pairs={{0,4},{4,8},{8,12},{12,14},{14,10},{10,6},{6,2},{2,0},{1,5},{5,9},... | collective-permute-start | bytes 786440 | tf_op jit(solution)/shard_map/ppermute | solution.py:121
  24.5 11.2 %collective-permute-start.11 = (bf16[256,512]{1,0:T(8,128)(2,1)S(1)}, bf16[256,512]{1,0:T(8,128)(2,1)S(1)}, u32[]{:S(2)}, u32[]{:S(2)}) collective-permute-start(bf16[256,512]{1,0:T(8,128)(2,1)S(1)} %collective-permute-done.7.refs_7_), channel_id=1, source_target_pairs={{4,0},{8,4},{12,8},{14,12},{10,14},{6,10},{2,6},{0,2},{5,1},{9,5},... | collective-permute-start | bytes 786440 | tf_op jit(solution)/shard_map/ppermute | solution.py:122
  29.0 10.4 %collective-permute-start.12 = (bf16[256,512]{1,0:T(8,128)(2,1)S(1)}, bf16[256,512]{1,0:T(8,128)(2,1)S(1)}, u32[]{:S(2)}, u32[]{:S(2)}) collective-permute-start(bf16[256,512]{1,0:T(8,128)(2,1)S(1)} %collective-permute-done.8.refs_8_), channel_id=1, source_target_pairs={{0,4},{4,8},{8,12},{12,14},{14,10},{10,6},{6,2},{2,0},{1,5},{5,9},... | collective-permute-start | bytes 786440 | tf_op jit(solution)/shard_map/ppermute | solution.py:121
  31.1 10.3 %collective-permute-start.13 = (bf16[256,512]{1,0:T(8,128)(2,1)S(1)}, bf16[256,512]{1,0:T(8,128)(2,1)S(1)}, u32[]{:S(2)}, u32[]{:S(2)}) collective-permute-start(bf16[256,512]{1,0:T(8,128)(2,1)S(1)} %collective-permute-done.9.refs_9_), channel_id=1, source_target_pairs={{4,0},{8,4},{12,8},{14,12},{10,14},{6,10},{2,6},{0,2},{5,1},{9,5},... | collective-permute-start | bytes 786440 | tf_op jit(solution)/shard_map/ppermute | solution.py:122
  33.8 11.0 %collective-permute-start.14 = (bf16[256,512]{1,0:T(8,128)(2,1)S(1)}, bf16[256,512]{1,0:T(8,128)(2,1)S(1)}, u32[]{:S(2)}, u32[]{:S(2)}) collective-permute-start(bf16[256,512]{1,0:T(8,128)(2,1)S(1)} %collective-permute-done.10.refs_10_), channel_id=1, source_target_pairs={{0,4},{4,8},{8,12},{12,14},{14,10},{10,6},{6,2},{2,0},{1,5},{5,9},... | collective-permute-start | bytes 786440 | tf_op jit(solution)/shard_map/ppermute | solution.py:127
  35.8 10.5 %collective-permute-start.15 = (bf16[256,512]{1,0:T(8,128)(2,1)S(1)}, bf16[256,512]{1,0:T(8,128)(2,1)S(1)}, u32[]{:S(2)}, u32[]{:S(2)}) collective-permute-start(bf16[256,512]{1,0:T(8,128)(2,1)S(1)} %collective-permute-done.11.refs_11_), channel_id=1, source_target_pairs={{4,0},{8,4},{12,8},{14,12},{10,14},{6,10},{2,6},{0,2},{5,1},{9,5},... | collective-permute-start | bytes 786440 | tf_op jit(solution)/shard_map/ppermute | solution.py:128

commit v4 on v3

--- a/solution.py
+++ b/solution.py
@@ -71,11 +71,19 @@
     add_products(places, slots, flags, refs[:-1], inner, total)
 
 
-def late_kernel(places, slots, flags, inner, before, *refs):
-    *pieces, out, total = refs
-    total[...] = before[...]
-    add_products(places, slots, flags, pieces, inner, total)
-    out[...] = total[...].astype(out.dtype)
+def late_kernel(tile, before, *refs):
+    *pieces, out, held, sems = refs
+    copies = []
+    start = 0
+    for h, piece in enumerate(pieces):
+        rows = pl.ds(start, piece.shape[0])
+        start += piece.shape[0]
+        product = jnp.dot(piece[...], tile[...], preferred_element_type=jnp.float32)
+        held[rows, :] = (before[rows, :] + product).astype(out.dtype)
+        copies.append(pltpu.make_async_copy(held.at[rows], out.at[rows], sems.at[h]))
+        copies[-1].start()
+    for copy in copies:
+        copy.wait()
 
 
 def multiply(kernel, places, slots, flags, arrays, out_shape, scratch):
@@ -103,17 +111,21 @@
     halves = lax.axis_size("depth")
     depth_index = lax.axis_index("depth")
     column = lax.axis_index("grid")
-    half = size // 2
+    half = (size * 9 // 16) // 16 * 16
 
     order = list(range(0, grid_size, 2)) + list(range(1, grid_size, 2))[::-1]
     onward = [(order[i], order[(i + 1) % grid_size]) for i in range(grid_size)]
     backward = [(b, a) for a, b in onward]
     position_of = [order.index(g) for g in range(grid_size)]
 
-    own = lax.dynamic_slice_in_dim(band_held, depth_index * size, size, 0)
-    first = [own[:half], own[half:]]
+    begin = depth_index * size
+    again, _ = lax.optimization_barrier((band_held, inner_mask))
+    first = [
+        lax.dynamic_slice_in_dim(band_held, begin, half, 0),
+        lax.dynamic_slice_in_dim(again, begin + half, size - half, 0),
+    ]
     pieces = {(0, 0): first[0], (0, 1): first[1]}
-    late = lax.optimization_barrier((own[:half], own[half:], inner_mask))
+    late = lax.optimization_barrier((*first, inner_mask))
     right, left = [first[0], late[1]], [late[0], first[1]]
     steps = (grid_size - 1) // 2
     for step in range(1, steps + 1):
@@ -158,19 +170,20 @@
     early = multiply(
         early_kernel, placed(pieces), slots, flags, [inner, *pieces.values()], total_shape, []
     )
-    return multiply(
+    tile = lax.dynamic_index_in_dim(inner, slots[steps + 1], 0, keepdims=False)
+    tile = tile * flags[steps + 1].astype(tile.dtype)
+    vmem = pl.BlockSpec(memory_space=pltpu.VMEM)
+    return pl.pallas_call(
         late_kernel,
-        [(0, h * half) for _, h in last],
-        jnp.zeros((1,), jnp.int32),
-        flags[steps + 1 :][:1],
-        [
-            lax.dynamic_slice_in_dim(inner, slots[steps + 1], 1, 0),
-            early,
-            *last.values(),
+        out_shape=jax.ShapeDtypeStruct((size, size), band_held.dtype),
+        in_specs=[vmem] * 4,
+        out_specs=pl.BlockSpec(memory_space=pl.ANY),
+        scratch_shapes=[
+            pltpu.VMEM((size, size), band_held.dtype),
+            pltpu.SemaphoreType.DMA((len(last),)),
         ],
-        jax.ShapeDtypeStruct((size, size), band_held.dtype),
-        [pltpu.VMEM((size, size), jnp.float32)],
-    )
+        compiler_params=pltpu.CompilerParams(vmem_limit_bytes=40 * 2**20),
+    )(tile, early, *last.values())
 
 
 def per_device(band_held, inner_tiles, band_mask, inner_mask, held_col):

time: 48 us -> 47.2 us (0.983)
  waiting for transfers between devices: 16.2 us -> 12.9 us
  starting transfers between devices: 15.3 us -> 16.4 us
  other arithmetic: 3.54 us -> 4.14 us
    ppermute x6, waiting for transfers between devices: 8.98 us -> 0.91 us  [gather_columns(): right[h] = lax.ppermute(right[h], 'grid', onward)]
    ppermute x6, waiting for transfers between devices: 4.17 us -> 9.09 us  [gather_columns(): left[1 - h] = lax.ppermute(left[1 - h], 'grid', backward)]
    ppermute x1, waiting for transfers between devices: 1.48 us -> 0.01 us  [gather_columns(): last[steps + 1, 0] = lax.ppermute(right[0], 'grid', onward)]
    ppermute x1, waiting for transfers between devices: 0.01 us -> 1.25 us  [gather_columns(): lax.ppermute(inner_mask, 'depth', [(0, 1), (1, 0)])]
    pallas_call x0 -> x1, Pallas kernels: none -> 1.15 us  [gather_columns(): pl.pallas_call(late_kernel, out_shape=jax.ShapeDtypeStruct((size, size),...]
    slice x3 -> x2, local copies, waits for them, and re-layouts: 2.2 us -> 1.16 us  [the longest x1 0.58 us: gather_columns(): tile = lax.dynamic_index_in_dim(inner, slots[steps + 1], 0, keepdims=False)]
    pallas_call x2 -> x1, Pallas kernels: 3.33 us -> 2.49 us  [multiply(): pl.pallas_call(functools.partial(kernel, places), out_shape=out_shape, in...]
    unnamed x2, local copies, waits for them, and re-layouts: 0.01 us -> 0.77 us
  transfers between devices with their start and end apart: 16 -> 16, of which waited for: 9 -> 9; matrix products, arithmetic and copies ran while one was open for 23% -> 24% of each run, Pallas kernels for 4% -> 5%
where the time goes in v4:
time: 47.2 us; the launch traced here: 46.9 us
  starting transfers between devices  16.4 us (35%)
  waiting for transfers between devices  12.9 us (27%)
  local copies, waits for them, and re-layouts  7.77 us (16%)
  other arithmetic  4.14 us (9%)
  Pallas kernels  3.64 us (8%)
  between operations  2.05 us (4%)
    ppermute x6, starting transfers between devices, gather_columns(): right[h] = lax.ppermute(right[h], 'grid', onward)  13 us
    ppermute x6, waiting for transfers between devices, gather_columns(): left[1 - h] = lax.ppermute(left[1 - h], 'grid', backward)  9.09 us
    pallas_call x1, Pallas kernels, multiply(): pl.pallas_call(functools.partial(kernel, places), out_shape=out_shape, in...  2.49 us
    concatenate x1, other arithmetic, gather_columns(): jnp.concatenate([inner_tiles, swapped], axis=0).reshape(-1, size, size)  2.09 us
    ppermute x1, starting transfers between devices, gather_columns(): last[steps + 1, 0] = lax.ppermute(right[0], 'grid', onward)  2.02 us
    ppermute x1, waiting for transfers between devices, gather_columns(): last[steps + 1, 1] = lax.ppermute(left[1], 'grid', backward)  1.69 us
    gather x1, local copies, waits for them, and re-layouts, gather_columns(): jnp.asarray(order, jnp.int32)  1.3 us
    gather x1, local copies, waits for them, and re-layouts, gather_columns(): true_column = held_col[sources]  1.3 us
  transfers between devices with their start and end apart: 16, of which 9 were waited for; matrix products, arithmetic and copies ran while one was open for 24% of the time, Pallas kernels for 5%

profile of v4, /device:TPU:0, one launch (start us, length us, event | category | flops | bytes accessed | tf_op | source)
XLA Modules:
  0.0 46.9 jit_solution(12944327666134737746)
XLA Ops:
  0.0 0.5 collective-permute-start
  0.5 0.8 %copy-done = bf16[1024,512]{1,0:T(8,128)(2,1)S(1)} copy-done((bf16[1024,512]{1,0:T(8,128)(2,1)S(1)}, bf16[1024,512]{1,0:T(8,128)(2,1)}, u32[]{:S(2)}) %copy-start) | copy-done | bytes 1048600
  1.2 3.1 %collective-permute-start.1 = (bf16[288,512]{1,0:T(8,128)(2,1)S(1)}, bf16[288,512]{1,0:T(8,128)(2,1)S(1)}, u32[]{:S(2)}, u32[]{:S(2)}) collective-permute-start(bf16[288,512]{1,0:T(8,128)(2,1)S(1)} %constant_dynamic-slice_fusion.1.refs_0_), channel_id=1, source_target_pairs={{0,4},{4,8},{8,12},{12,14},{14,10},{10,6},{6,2},{2,0},{1,5},{5,9},... | collective-permute-start | bytes 884744 | tf_op jit(solution)/shard_map/ppermute | solution.py:133
  4.4 2.0 %collective-permute-start.4 = (bf16[224,512]{1,0:T(8,128)(2,1)S(1)}, bf16[224,512]{1,0:T(8,128)(2,1)S(1)}, u32[]{:S(2)}, u32[]{:S(2)}) collective-permute-start(bf16[224,512]{1,0:T(8,128)(2,1)S(1)} %constant_dynamic-slice_fusion.refs_1_), channel_id=1, source_target_pairs={{0,4},{4,8},{8,12},{12,14},{14,10},{10,6},{6,2},{2,0},{1,5},{5,9},... | collective-permute-start | bytes 688136 | tf_op jit(solution)/shard_map/ppermute | solution.py:133
  6.5 1.2 %dynamic_slice.17 = s32[1]{0:T(128)} dynamic-slice(s32[8]{0:T(128)} %constant.68.clone, s32[]{:T(128)S(6)} %select_n.115), dynamic_slice_sizes={1} | dynamic-slice | bytes 12 | tf_op jit(solution)/shard_map/dynamic_slice | solution.py:149
  7.7 0.7 %fusion.5 = s32[8]{0:T(128)S(1)} fusion(s32[]{:T(128)} %bitcast.1), kind=kLoop, calls=%fused_computation.32 | loop fusion | flops 120 | bytes 36 | tf_op jit(solution)/shard_map/select_n | solution.py:150
  8.4 1.3 %gather_fusion = s32[8]{0:T(128)S(1)} fusion(s32[8]{0:T(128)} %constant.69.clone, s32[1024]{0:T(1024)S(1)} %pad_clamp_fusion.3), kind=kCustom, calls=%fused_computation | custom fusion | bytes 96 | tf_op jit(solution)/shard_map/gather | solution.py:150
  9.7 1.3 %gather_fusion.1 = s32[8]{0:T(128)S(1)} fusion(s32[8]{0:T(128)} %param.11, s32[1024]{0:T(1024)S(1)} %pad_clamp_fusion.2), kind=kCustom, calls=%fused_computation.1 | custom fusion | bytes 96 | tf_op jit(solution)/shard_map/gather | solution.py:153
  11.0 1.9 %collective-permute-done.3.refs_3_ = bf16[224,512]{1,0:T(8,128)(2,1)S(1)} collective-permute-done((bf16[224,512]{1,0:T(8,128)(2,1)S(1)}, bf16[224,512]{1,0:T(8,128)(2,1)S(1)}, u32[]{:S(2)}, u32[]{:S(2)}) %collective-permute-start.3) | collective-permute-done | bytes 229408 | tf_op jit(solution)/shard_map/ppermute | solution.py:134
  13.0 2.0 %collective-permute-start.6 = (bf16[288,512]{1,0:T(8,128)(2,1)S(1)}, bf16[288,512]{1,0:T(8,128)(2,1)S(1)}, u32[]{:S(2)}, u32[]{:S(2)}) collective-permute-start(bf16[288,512]{1,0:T(8,128)(2,1)S(1)} %collective-permute-done.1.refs_2_), channel_id=1, source_target_pairs={{0,4},{4,8},{8,12},{12,14},{14,10},{10,6},{6,2},{2,0},{1,5},{5,9},... | collective-permute-start | bytes 884744 | tf_op jit(solution)/shard_map/ppermute | solution.py:133
  15.0 0.7 %fusion.2 = s32[8]{0:T(128)S(1)} fusion(s32[2,8]{1,0:T(2,128)} %param.9, s32[]{:T(128)S(6)} %select_n.123), kind=kLoop, calls=%fused_computation.29 | loop fusion | bytes 68 | tf_op jit(solution)/shard_map/jit(dynamic_index_in_dim)/squeeze | solution.py:157
  15.7 0.6 %gather_fusion.2 = s32[8]{0:T(128)S(1)} fusion(s32[8]{0:T(128)S(1)} %fusion.2, s32[1024]{0:T(1024)S(1)} %get-tuple-element.19), kind=kCustom, calls=%fused_computation.2 | custom fusion | bytes 96 | tf_op jit(solution)/shard_map/gather | solution.py:158
  16.3 0.7 %collective-permute-done.4.refs_4_ = bf16[224,512]{1,0:T(8,128)(2,1)S(1)} collective-permute-done((bf16[224,512]{1,0:T(8,128)(2,1)S(1)}, bf16[224,512]{1,0:T(8,128)(2,1)S(1)}, u32[]{:S(2)}, u32[]{:S(2)}) %collective-permute-start.4) | collective-permute-done | bytes 229408 | tf_op jit(solution)/shard_map/ppermute | solution.py:133
  17.0 2.1 %collective-permute-start.8 = (bf16[224,512]{1,0:T(8,128)(2,1)S(1)}, bf16[224,512]{1,0:T(8,128)(2,1)}, u32[]{:S(2)}, u32[]{:S(2)}) collective-permute-start(bf16[224,512]{1,0:T(8,128)(2,1)S(1)} %collective-permute-done.4.refs_4_), channel_id=1, source_target_pairs={{0,4},{4,8},{8,12},{12,14},{14,10},{10,6},{6,2},{2,0},{1,5},{5,9},... | collective-permute-start | bytes 688136 | tf_op jit(solution)/shard_map/ppermute | solution.py:133
  19.2 1.3 %collective-permute-done.2 = s32[3,1]{0,1:T(1,128)S(1)} collective-permute-done((s32[3,1]{0,1:T(1,128)}, s32[3,1]{0,1:T(1,128)S(1)}, u32[]{:S(2)}, u32[]{:S(2)}) %collective-permute-start.2) | collective-permute-done | bytes 44 | tf_op jit(solution)/shard_map/ppermute | solution.py:146
  20.5 2.3 %collective-permute-done.7.refs_7_ = bf16[224,512]{1,0:T(8,128)(2,1)} collective-permute-done((bf16[224,512]{1,0:T(8,128)(2,1)S(1)}, bf16[224,512]{1,0:T(8,128)(2,1)}, u32[]{:S(2)}, u32[]{:S(2)}) %collective-permute-start.7) | collective-permute-done | bytes 229408 | tf_op jit(solution)/shard_map/ppermute | solution.py:134
  22.8 0.3 collective-permute-start.11
  23.3 2.1 %collective-permute-start.10 = (bf16[288,512]{1,0:T(8,128)(2,1)S(1)}, bf16[288,512]{1,0:T(8,128)(2,1)S(1)}, u32[]{:S(2)}, u32[]{:S(2)}) collective-permute-start(bf16[288,512]{1,0:T(8,128)(2,1)S(1)} %collective-permute-done.6.refs_6_), channel_id=1, source_target_pairs={{0,4},{4,8},{8,12},{12,14},{14,10},{10,6},{6,2},{2,0},{1,5},{5,9},... | collective-permute-start | bytes 884744 | tf_op jit(solution)/shard_map/ppermute | solution.py:133
  25.5 0.7 %add_bitcast_fusion = s32[6]{0:T(128)S(1)} fusion(s32[3,1]{0,1:T(1,128)S(1)} %collective-permute-done.2, s32[3,1]{0,1:T(1,128)} %param.10), kind=kLoop, calls=%fused_computation.36 | loop fusion | flops 6 | bytes 48 | tf_op jit(solution)/shard_map/squeeze | solution.py:145
  26.2 0.6 %gather_fusion.3 = s32[8]{0:T(128)S(1)} fusion(s32[6]{0:T(128)S(1)} %add_bitcast_fusion, s32[1024]{0:T(1024)S(1)} %get-tuple-element.18), kind=kCustom, calls=%fused_computation.3 | custom fusion | bytes 96 | tf_op jit(solution)/shard_map/gather | solution.py:164
  26.9 0.6 %slice.7 = s32[1]{0:T(128)} slice(s32[8]{0:T(128)S(1)} %get-tuple-element.15.slots), slice={[4:5]} | slice | bytes 8 | tf_op jit(solution)/shard_map/slice | solution.py:173
  28.7 0.6 %slice.8 = bf16[1]{0:T(256)(128)(2,1)} slice(bf16[8]{0:T(256)(128)(2,1)S(1)} %get-tuple-element.13), slice={[4:5]} | slice | bytes 4 | tf_op jit(solution)/shard_map/slice | solution.py:174
  30.0 1.6 %collective-permute-start.12 = (bf16[224,512]{1,0:T(8,128)(2,1)}, bf16[224,512]{1,0:T(8,128)(2,1)S(1)}, u32[]{:S(2)}, u32[]{:S(2)}) collective-permute-start(bf16[224,512]{1,0:T(8,128)(2,1)} %collective-permute-done.8.refs_8_), channel_id=1, source_target_pairs={{0,4},{4,8},{8,12},{12,14},{14,10},{10,6},{6,2},{2,0},{1,5},{5,9},... | collective-permute-start | bytes 688136 | tf_op jit(solution)/shard_map/ppermute | solution.py:133
  31.6 0.4 collective-permute-start.13
  32.1 3.3 %collective-permute-done.11.refs_11_ = bf16[224,512]{1,0:T(8,128)(2,1)} collective-permute-done((bf16[224,512]{1,0:T(8,128)(2,1)}, bf16[224,512]{1,0:T(8,128)(2,1)}, u32[]{:S(2)}, u32[]{:S(2)}) %collective-permute-start.11) | collective-permute-done | bytes 229408 | tf_op jit(solution)/shard_map/ppermute | solution.py:134
  35.4 2.0 %collective-permute-start.14 = (bf16[288,512]{1,0:T(8,128)(2,1)S(1)}, bf16[288,512]{1,0:T(8,128)(2,1)S(1)}, u32[]{:S(2)}, u32[]{:S(2)}) collective-permute-start(bf16[288,512]{1,0:T(8,128)(2,1)S(1)} %collective-permute-done.10.refs_10_), channel_id=1, source_target_pairs={{0,4},{4,8},{8,12},{12,14},{14,10},{10,6},{6,2},{2,0},{1,5},{5,9},... | collective-permute-start | bytes 884744 | tf_op jit(solution)/shard_map/ppermute | solution.py:139
  37.4 2.1 %pad_maximum_fusion = bf16[3072,512]{1,0:T(8,128)(2,1)S(1)} fusion(bf16[1536,512]{1,0:T(8,128)(2,1)} %collective-permute-done, bf16[1536,512]{1,0:T(8,128)(2,1)} %param.8), kind=kLoop, calls=%fused_computation.4 | loop fusion | flops 6291456 | bytes 6291456 | tf_op jit(solution)/shard_map/concatenate | solution.py:143
  39.5 0.6 %multiply_bitcast_fusion.tile = bf16[512,512]{1,0:T(8,128)(2,1)S(1)} fusion(bf16[6,512,512]{2,1,0:T(8,128)(2,1)S(1)} %bitcast.31, s32[]{:T(128)S(6)} %select_n.122, bf16[]{:T(256)} %bitcast.11), kind=kLoop, calls=%fused_computation.5 | loop fusion | flops 262144 | bytes 1048582 | tf_op jit(solution)/shard_map/mul | solution.py:174
  40.1 1.5 %collective-permute-done.13.refs_13_ = bf16[288,512]{1,0:T(8,128)(2,1)S(1)} collective-permute-done((bf16[288,512]{1,0:T(8,128)(2,1)S(1)}, bf16[288,512]{1,0:T(8,128)(2,1)S(1)}, u32[]{:S(2)}, u32[]{:S(2)}) %collective-permute-start.13) | collective-permute-done | bytes 294944 | tf_op jit(solution)/shard_map/ppermute | solution.py:134
  41.6 2.5 %shard_map.73.before = f32[512,512]{1,0:T(8,128)S(1)} custom-call(s32[8]{0:T(128)S(1)} %get-tuple-element.15.slots, s32[8]{0:T(128)S(1)} %get-tuple-element.14.flags, bf16[6,512,512]{2,1,0:T(8,128)(2,1)S(1)} %bitcast.32, bf16[288,512]{1,0:T(8,128)(2,1)S(1)} %constant_dynamic-slice_fusion.1.refs_0_, bf16[224,512]{1,0:T(8,128)(2,1)S(1)} %constant_dynamic-slice_fusion.refs_1_, ...), custom_call_target="tpu_custom_call" | custom-call | flops 1879048192 | bytes 6815744 | tf_op jit(solution)/shard_map/pallas_call | solution.py:92
  44.1 1.7 %collective-permute-done.15.refs_1_ = bf16[224,512]{1,0:T(8,128)(2,1)S(1)} collective-permute-done((bf16[224,512]{1,0:T(8,128)(2,1)}, bf16[224,512]{1,0:T(8,128)(2,1)S(1)}, u32[]{:S(2)}, u32[]{:S(2)}) %collective-permute-start.15) | collective-permute-done | bytes 229408 | tf_op jit(solution)/shard_map/ppermute | solution.py:140
  45.8 1.1 %shard_map.74 = bf16[512,512]{1,0:T(8,128)(2,1)} custom-call(bf16[512,512]{1,0:T(8,128)(2,1)S(1)} %multiply_bitcast_fusion.tile, f32[512,512]{1,0:T(8,128)S(1)} %shard_map.73.before, bf16[288,512]{1,0:T(8,128)(2,1)S(1)} %collective-permute-done.14.refs_0_, bf16[224,512]{1,0:T(8,128)(2,1)S(1)} %collective-permute-done.15.refs_1_), custom_call_target="tpu_custom_call" | custom-call | tf_op jit(solution)/shard_map/pallas_call | solution.py:176
  (24 shorter events, 0.6 us)
Async XLA Ops:
  0.0 1.2 %copy-start = (bf16[1024,512]{1,0:T(8,128)(2,1)S(1)}, bf16[1024,512]{1,0:T(8,128)(2,1)}, u32[]{:S(2)}) copy-start(bf16[1024,512]{1,0:T(8,128)(2,1)} %param.7) | copy-start | bytes 3145732
  0.0 37.4 %collective-permute-start = (bf16[1536,512]{1,0:T(8,128)(2,1)}, bf16[1536,512]{1,0:T(8,128)(2,1)}, u32[]{:S(2)}, u32[]{:S(2)}) collective-permute-start(bf16[1536,512]{1,0:T(8,128)(2,1)} %param.8), channel_id=1, source_target_pairs={{0,1},{1,0},{2,3},{3,2},{4,5},{5,4},{6,7},{7,6},{8,9},{9,8},{10,11... | collective-permute-start | bytes 4718600 | tf_op jit(solution)/shard_map/ppermute | solution.py:142
  1.2 11.7 %collective-permute-start.1 = (bf16[288,512]{1,0:T(8,128)(2,1)S(1)}, bf16[288,512]{1,0:T(8,128)(2,1)S(1)}, u32[]{:S(2)}, u32[]{:S(2)}) collective-permute-start(bf16[288,512]{1,0:T(8,128)(2,1)S(1)} %constant_dynamic-slice_fusion.1.refs_0_), channel_id=1, source_target_pairs={{0,4},{4,8},{8,12},{12,14},{14,10},{10,6},{6,2},{2,0},{1,5},{5,9},... | collective-permute-start | bytes 884744 | tf_op jit(solution)/shard_map/ppermute | solution.py:133
  4.3 8.6 %collective-permute-start.3 = (bf16[224,512]{1,0:T(8,128)(2,1)S(1)}, bf16[224,512]{1,0:T(8,128)(2,1)S(1)}, u32[]{:S(2)}, u32[]{:S(2)}) collective-permute-start(bf16[224,512]{1,0:T(8,128)(2,1)S(1)} %constant_dynamic-slice_fusion.refs_1_), channel_id=1, source_target_pairs={{4,0},{8,4},{12,8},{14,12},{10,14},{6,10},{2,6},{0,2},{5,1},{9,5},... | collective-permute-start | bytes 688136 | tf_op jit(solution)/shard_map/ppermute | solution.py:134
  4.4 12.6 %collective-permute-start.4 = (bf16[224,512]{1,0:T(8,128)(2,1)S(1)}, bf16[224,512]{1,0:T(8,128)(2,1)S(1)}, u32[]{:S(2)}, u32[]{:S(2)}) collective-permute-start(bf16[224,512]{1,0:T(8,128)(2,1)S(1)} %constant_dynamic-slice_fusion.refs_1_), channel_id=1, source_target_pairs={{0,4},{4,8},{8,12},{12,14},{14,10},{10,6},{6,2},{2,0},{1,5},{5,9},... | collective-permute-start | bytes 688136 | tf_op jit(solution)/shard_map/ppermute | solution.py:133
  6.4 12.8 %collective-permute-start.5 = (bf16[288,512]{1,0:T(8,128)(2,1)S(1)}, bf16[288,512]{1,0:T(8,128)(2,1)S(1)}, u32[]{:S(2)}, u32[]{:S(2)}) collective-permute-start(bf16[288,512]{1,0:T(8,128)(2,1)S(1)} %constant_dynamic-slice_fusion.1.refs_0_), channel_id=1, source_target_pairs={{4,0},{8,4},{12,8},{14,12},{10,14},{6,10},{2,6},{0,2},{5,1},{9,5},... | collective-permute-start | bytes 884744 | tf_op jit(solution)/shard_map/ppermute | solution.py:134
  12.9 9.9 %collective-permute-start.7 = (bf16[224,512]{1,0:T(8,128)(2,1)S(1)}, bf16[224,512]{1,0:T(8,128)(2,1)}, u32[]{:S(2)}, u32[]{:S(2)}) collective-permute-start(bf16[224,512]{1,0:T(8,128)(2,1)S(1)} %collective-permute-done.3.refs_3_), channel_id=1, source_target_pairs={{4,0},{8,4},{12,8},{14,12},{10,14},{6,10},{2,6},{0,2},{5,1},{9,5},... | collective-permute-start | bytes 688136 | tf_op jit(solution)/shard_map/ppermute | solution.py:134
  13.0 10.4 %collective-permute-start.6 = (bf16[288,512]{1,0:T(8,128)(2,1)S(1)}, bf16[288,512]{1,0:T(8,128)(2,1)S(1)}, u32[]{:S(2)}, u32[]{:S(2)}) collective-permute-start(bf16[288,512]{1,0:T(8,128)(2,1)S(1)} %collective-permute-done.1.refs_2_), channel_id=1, source_target_pairs={{0,4},{4,8},{8,12},{12,14},{14,10},{10,6},{6,2},{2,0},{1,5},{5,9},... | collective-permute-start | bytes 884744 | tf_op jit(solution)/shard_map/ppermute | solution.py:133
  17.0 13.0 %collective-permute-start.8 = (bf16[224,512]{1,0:T(8,128)(2,1)S(1)}, bf16[224,512]{1,0:T(8,128)(2,1)}, u32[]{:S(2)}, u32[]{:S(2)}) collective-permute-start(bf16[224,512]{1,0:T(8,128)(2,1)S(1)} %collective-permute-done.4.refs_4_), channel_id=1, source_target_pairs={{0,4},{4,8},{8,12},{12,14},{14,10},{10,6},{6,2},{2,0},{1,5},{5,9},... | collective-permute-start | bytes 688136 | tf_op jit(solution)/shard_map/ppermute | solution.py:133
  19.2 1.3 %collective-permute-start.2 = (s32[3,1]{0,1:T(1,128)}, s32[3,1]{0,1:T(1,128)S(1)}, u32[]{:S(2)}, u32[]{:S(2)}) collective-permute-start(s32[3,1]{0,1:T(1,128)} %param.10), channel_id=1, source_target_pairs={{0,1},{1,0},{2,3},{3,2},{4,5},{5,4},{6,7},{7,6},{8,9},{9,8},{10,11... | collective-permute-start | bytes 44 | tf_op jit(solution)/shard_map/ppermute | solution.py:146
  20.5 11.1 %collective-permute-start.9 = (bf16[288,512]{1,0:T(8,128)(2,1)S(1)}, bf16[288,512]{1,0:T(8,128)(2,1)S(1)}, u32[]{:S(2)}, u32[]{:S(2)}) collective-permute-start(bf16[288,512]{1,0:T(8,128)(2,1)S(1)} %collective-permute-done.5.refs_5_), channel_id=1, source_target_pairs={{4,0},{8,4},{12,8},{14,12},{10,14},{6,10},{2,6},{0,2},{5,1},{9,5},... | collective-permute-start | bytes 884744 | tf_op jit(solution)/shard_map/ppermute | solution.py:134
  22.8 12.6 %collective-permute-start.11 = (bf16[224,512]{1,0:T(8,128)(2,1)}, bf16[224,512]{1,0:T(8,128)(2,1)}, u32[]{:S(2)}, u32[]{:S(2)}) collective-permute-start(bf16[224,512]{1,0:T(8,128)(2,1)} %collective-permute-done.7.refs_7_), channel_id=1, source_target_pairs={{4,0},{8,4},{12,8},{14,12},{10,14},{6,10},{2,6},{0,2},{5,1},{9,5},... | collective-permute-start | bytes 688136 | tf_op jit(solution)/shard_map/ppermute | solution.py:134
  23.3 12.1 %collective-permute-start.10 = (bf16[288,512]{1,0:T(8,128)(2,1)S(1)}, bf16[288,512]{1,0:T(8,128)(2,1)S(1)}, u32[]{:S(2)}, u32[]{:S(2)}) collective-permute-start(bf16[288,512]{1,0:T(8,128)(2,1)S(1)} %collective-permute-done.6.refs_6_), channel_id=1, source_target_pairs={{0,4},{4,8},{8,12},{12,14},{14,10},{10,6},{6,2},{2,0},{1,5},{5,9},... | collective-permute-start | bytes 884744 | tf_op jit(solution)/shard_map/ppermute | solution.py:133
  30.0 10.1 %collective-permute-start.12 = (bf16[224,512]{1,0:T(8,128)(2,1)}, bf16[224,512]{1,0:T(8,128)(2,1)S(1)}, u32[]{:S(2)}, u32[]{:S(2)}) collective-permute-start(bf16[224,512]{1,0:T(8,128)(2,1)} %collective-permute-done.8.refs_8_), channel_id=1, source_target_pairs={{0,4},{4,8},{8,12},{12,14},{14,10},{10,6},{6,2},{2,0},{1,5},{5,9},... | collective-permute-start | bytes 688136 | tf_op jit(solution)/shard_map/ppermute | solution.py:133
  31.6 10.0 %collective-permute-start.13 = (bf16[288,512]{1,0:T(8,128)(2,1)S(1)}, bf16[288,512]{1,0:T(8,128)(2,1)S(1)}, u32[]{:S(2)}, u32[]{:S(2)}) collective-permute-start(bf16[288,512]{1,0:T(8,128)(2,1)S(1)} %collective-permute-done.9.refs_9_), channel_id=1, source_target_pairs={{4,0},{8,4},{12,8},{14,12},{10,14},{6,10},{2,6},{0,2},{5,1},{9,5},... | collective-permute-start | bytes 884744 | tf_op jit(solution)/shard_map/ppermute | solution.py:134
  35.4 10.4 %collective-permute-start.15 = (bf16[224,512]{1,0:T(8,128)(2,1)}, bf16[224,512]{1,0:T(8,128)(2,1)S(1)}, u32[]{:S(2)}, u32[]{:S(2)}) collective-permute-start(bf16[224,512]{1,0:T(8,128)(2,1)} %collective-permute-done.11.refs_11_), channel_id=1, source_target_pairs={{4,0},{8,4},{12,8},{14,12},{10,14},{6,10},{2,6},{0,2},{5,1},{9,5},... | collective-permute-start | bytes 688136 | tf_op jit(solution)/shard_map/ppermute | solution.py:140
  35.4 10.4 %collective-permute-start.14 = (bf16[288,512]{1,0:T(8,128)(2,1)S(1)}, bf16[288,512]{1,0:T(8,128)(2,1)S(1)}, u32[]{:S(2)}, u32[]{:S(2)}) collective-permute-start(bf16[288,512]{1,0:T(8,128)(2,1)S(1)} %collective-permute-done.10.refs_10_), channel_id=1, source_target_pairs={{0,4},{4,8},{8,12},{12,14},{14,10},{10,6},{6,2},{2,0},{1,5},{5,9},... | collective-permute-start | bytes 884744 | tf_op jit(solution)/shard_map/ppermute | solution.py:139

commit v5 on v4

--- a/solution.py
+++ b/solution.py
@@ -71,37 +71,33 @@
     add_products(places, slots, flags, refs[:-1], inner, total)
 
 
-def late_kernel(tile, before, *refs):
-    *pieces, out, held, sems = refs
-    copies = []
-    start = 0
-    for h, piece in enumerate(pieces):
-        rows = pl.ds(start, piece.shape[0])
-        start += piece.shape[0]
-        product = jnp.dot(piece[...], tile[...], preferred_element_type=jnp.float32)
-        held[rows, :] = (before[rows, :] + product).astype(out.dtype)
-        copies.append(pltpu.make_async_copy(held.at[rows], out.at[rows], sems.at[h]))
-        copies[-1].start()
-    for copy in copies:
-        copy.wait()
-
-
-def multiply(kernel, places, slots, flags, arrays, out_shape, scratch):
-    size = arrays[0].shape[-1]
-    smem, vmem = pl.BlockSpec(memory_space=pltpu.SMEM), pl.BlockSpec(memory_space=pltpu.VMEM)
-    return pl.pallas_call(
-        functools.partial(kernel, places),
-        out_shape=out_shape,
-        in_specs=[smem, smem] + [vmem] * len(arrays),
-        out_specs=vmem,
-        scratch_shapes=scratch,
-        compiler_params=pltpu.CompilerParams(vmem_limit_bytes=40 * 2**20),
-        cost_estimate=pl.CostEstimate(
-            flops=len(places) * size**3,
-            bytes_accessed=sum(a.size * a.dtype.itemsize for a in arrays),
-            transcendentals=0,
-        ),
-    )(slots, flags, *arrays)
+def middle_kernel(places, last, slots, flags, inner, before, *refs):
+    *pieces, total, late_flag, out, held, sem = refs
+    late_flag[...] = jnp.full_like(late_flag, flags[last])
+    total[...] = before[...]
+    add_products(places, slots, flags, pieces, inner, total)
+    held[...] = total[...].astype(held.dtype)
+    copy = pltpu.make_async_copy(held, out, sem)
+    copy.start()
+    copy.wait()
+
+
+def late_kernel(flag, tile, before, *refs):
+    *pieces, _, out, held, sems = refs
+
+    @pl.when(flag[0, 0] != 0)
+    def _():
+        copies = []
+        start = 0
+        for h, piece in enumerate(pieces):
+            rows = pl.ds(start, piece.shape[0])
+            start += piece.shape[0]
+            product = jnp.dot(piece[...], tile[...], preferred_element_type=jnp.float32)
+            held[rows, :] = (before[rows, :] + product).astype(out.dtype)
+            copies.append(pltpu.make_async_copy(held.at[rows], out.at[rows], sems.at[h]))
+            copies[-1].start()
+        for copy in copies:
+            copy.wait()
 
 
 def gather_columns(band_held, inner_tiles, band_mask, inner_mask, held_col):
@@ -166,24 +162,49 @@
     def placed(items):
         return [(source, h * half) for source, h in items]
 
-    total_shape = jax.ShapeDtypeStruct((size, size), jnp.float32)
-    early = multiply(
-        early_kernel, placed(pieces), slots, flags, [inner, *pieces.values()], total_shape, []
-    )
+    smem, vmem = pl.BlockSpec(memory_space=pltpu.SMEM), pl.BlockSpec(memory_space=pltpu.VMEM)
+    anywhere = pl.BlockSpec(memory_space=pl.ANY)
+    params = pltpu.CompilerParams(vmem_limit_bytes=40 * 2**20)
+    result = jax.ShapeDtypeStruct((size, size), band_held.dtype)
+    staged = pltpu.VMEM((size, size), band_held.dtype)
+    wide = jax.ShapeDtypeStruct((size, size), jnp.float32)
+    near = {k: x for k, x in pieces.items() if k[0] not in (steps, grid_size - steps)}
+    far = {k: x for k, x in pieces.items() if k not in near}
+
+    def cost(items):
+        return pl.CostEstimate(
+            flops=len(items) * size**3,
+            bytes_accessed=2 * (inner.size + (len(items) + 2) * size**2),
+            transcendentals=0,
+        )
+
+    early = pl.pallas_call(
+        functools.partial(early_kernel, placed(near)),
+        out_shape=wide,
+        in_specs=[smem, smem] + [vmem] * (1 + len(near)),
+        out_specs=vmem,
+        compiler_params=params,
+        cost_estimate=cost(near),
+    )(slots, flags, inner, *near.values())
+    total, late_flag, early = pl.pallas_call(
+        functools.partial(middle_kernel, placed(far), steps + 1),
+        out_shape=[wide, jax.ShapeDtypeStruct((8, 128), jnp.int32), result],
+        in_specs=[smem, smem] + [vmem] * (2 + len(far)),
+        out_specs=[vmem, vmem, anywhere],
+        scratch_shapes=[staged, pltpu.SemaphoreType.DMA],
+        compiler_params=params,
+        cost_estimate=cost(far),
+    )(slots, flags, inner, early, *far.values())
     tile = lax.dynamic_index_in_dim(inner, slots[steps + 1], 0, keepdims=False)
-    tile = tile * flags[steps + 1].astype(tile.dtype)
-    vmem = pl.BlockSpec(memory_space=pltpu.VMEM)
     return pl.pallas_call(
         late_kernel,
-        out_shape=jax.ShapeDtypeStruct((size, size), band_held.dtype),
-        in_specs=[vmem] * 4,
-        out_specs=pl.BlockSpec(memory_space=pl.ANY),
-        scratch_shapes=[
-            pltpu.VMEM((size, size), band_held.dtype),
-            pltpu.SemaphoreType.DMA((len(last),)),
-        ],
-        compiler_params=pltpu.CompilerParams(vmem_limit_bytes=40 * 2**20),
-    )(tile, early, *last.values())
+        out_shape=result,
+        in_specs=[vmem] * (3 + len(last)) + [anywhere],
+        out_specs=anywhere,
+        scratch_shapes=[staged, pltpu.SemaphoreType.DMA((len(last),))],
+        input_output_aliases={3 + len(last): 0},
+        compiler_params=params,
+    )(late_flag, tile, total, *last.values(), early)
 
 
 def per_device(band_held, inner_tiles, band_mask, inner_mask, held_col):

time: 47.2 us -> 46.1 us (0.977)
  other arithmetic: 4.14 us -> 3.54 us
  local copies, waits for them, and re-layouts: 7.77 us -> 7.24 us
    mul x1, other arithmetic: 0.61 us -> 0.02 us  [gather_columns(): flags = flags * tile_flags[slots]]
    slice x1 -> x0, local copies, waits for them, and re-layouts: 0.58 us -> none  [gather_columns(): tile = tile * flags[steps + 1].astype(tile.dtype)]
    pallas_call x2 -> x3, Pallas kernels: 3.64 us -> 3.76 us  [the longest x1 2.49 us: gather_columns(): pl.pallas_call(functools.partial(middle_kernel, placed(far), steps + 1),...]
  transfers between devices with their start and end apart: 16 -> 16, of which waited for: 9 -> 9; matrix products, arithmetic and copies ran while one was open for 24% -> 22% of each run, Pallas kernels for 5% -> 8%
where the time goes in v5:
time: 46.1 us; the launch traced here: 45.8 us
  starting transfers between devices  16.4 us (36%)
  waiting for transfers between devices  12.9 us (28%)
  local copies, waits for them, and re-layouts  7.24 us (16%)
  Pallas kernels  3.76 us (8%)
  other arithmetic  3.54 us (8%)
  between operations  2.05 us (4%)
    ppermute x6, starting transfers between devices, gather_columns(): right[h] = lax.ppermute(right[h], 'grid', onward)  13 us
    ppermute x6, waiting for transfers between devices, gather_columns(): left[1 - h] = lax.ppermute(left[1 - h], 'grid', backward)  9.07 us
    pallas_call x1, Pallas kernels, gather_columns(): pl.pallas_call(functools.partial(middle_kernel, placed(far), steps + 1),...  2.49 us
    concatenate x1, other arithmetic, gather_columns(): jnp.concatenate([inner_tiles, swapped], axis=0).reshape(-1, size, size)  2.09 us
    ppermute x1, starting transfers between devices, gather_columns(): last[steps + 1, 0] = lax.ppermute(right[0], 'grid', onward)  2.02 us
    ppermute x1, waiting for transfers between devices, gather_columns(): last[steps + 1, 1] = lax.ppermute(left[1], 'grid', backward)  1.64 us
    gather x1, local copies, waits for them, and re-layouts, gather_columns(): jnp.asarray(order, jnp.int32)  1.3 us
    gather x1, local copies, waits for them, and re-layouts, gather_columns(): true_column = held_col[sources]  1.3 us
  transfers between devices with their start and end apart: 16, of which 9 were waited for; matrix products, arithmetic and copies ran while one was open for 22% of the time, Pallas kernels for 8%

profile of v5, /device:TPU:0, one launch (start us, length us, event | category | flops | bytes accessed | tf_op | source)
XLA Modules:
  0.0 45.8 jit_solution(2887552989820893356)
XLA Ops:
  0.0 0.5 collective-permute-start.2
  0.5 0.8 %copy-done = bf16[1024,512]{1,0:T(8,128)(2,1)S(1)} copy-done((bf16[1024,512]{1,0:T(8,128)(2,1)S(1)}, bf16[1024,512]{1,0:T(8,128)(2,1)}, u32[]{:S(2)}) %copy-start) | copy-done | bytes 1048600
  1.2 3.1 %collective-permute-start = (bf16[288,512]{1,0:T(8,128)(2,1)S(1)}, bf16[288,512]{1,0:T(8,128)(2,1)S(1)}, u32[]{:S(2)}, u32[]{:S(2)}) collective-permute-start(bf16[288,512]{1,0:T(8,128)(2,1)S(1)} %constant_dynamic-slice_fusion.1.refs_0_), channel_id=1, source_target_pairs={{0,4},{4,8},{8,12},{12,14},{14,10},{10,6},{6,2},{2,0},{1,5},{5,9},... | collective-permute-start | bytes 884744 | tf_op jit(solution)/shard_map/ppermute | solution.py:129
  4.4 2.0 %collective-permute-start.4 = (bf16[224,512]{1,0:T(8,128)(2,1)S(1)}, bf16[224,512]{1,0:T(8,128)(2,1)S(1)}, u32[]{:S(2)}, u32[]{:S(2)}) collective-permute-start(bf16[224,512]{1,0:T(8,128)(2,1)S(1)} %constant_dynamic-slice_fusion.refs_1_), channel_id=1, source_target_pairs={{0,4},{4,8},{8,12},{12,14},{14,10},{10,6},{6,2},{2,0},{1,5},{5,9},... | collective-permute-start | bytes 688136 | tf_op jit(solution)/shard_map/ppermute | solution.py:129
  6.5 1.2 %dynamic_slice.17 = s32[1]{0:T(128)} dynamic-slice(s32[8]{0:T(128)} %constant.68.clone, s32[]{:T(128)S(6)} %select_n.115), dynamic_slice_sizes={1} | dynamic-slice | bytes 12 | tf_op jit(solution)/shard_map/dynamic_slice | solution.py:145
  7.7 0.7 %fusion.5 = s32[8]{0:T(128)S(1)} fusion(s32[]{:T(128)} %bitcast), kind=kLoop, calls=%fused_computation.32 | loop fusion | flops 120 | bytes 36 | tf_op jit(solution)/shard_map/select_n | solution.py:146
  8.4 1.3 %gather_fusion = s32[8]{0:T(128)S(1)} fusion(s32[8]{0:T(128)} %constant.69.clone, s32[1024]{0:T(1024)S(1)} %pad_clamp_fusion.3), kind=kCustom, calls=%fused_computation | custom fusion | bytes 96 | tf_op jit(solution)/shard_map/gather | solution.py:146
  9.7 1.3 %gather_fusion.1 = s32[8]{0:T(128)S(1)} fusion(s32[8]{0:T(128)} %param.11, s32[1024]{0:T(1024)S(1)} %pad_clamp_fusion.2), kind=kCustom, calls=%fused_computation.1 | custom fusion | bytes 96 | tf_op jit(solution)/shard_map/gather | solution.py:149
  11.0 1.9 %collective-permute-done.3.refs_3_ = bf16[224,512]{1,0:T(8,128)(2,1)S(1)} collective-permute-done((bf16[224,512]{1,0:T(8,128)(2,1)S(1)}, bf16[224,512]{1,0:T(8,128)(2,1)S(1)}, u32[]{:S(2)}, u32[]{:S(2)}) %collective-permute-start.3) | collective-permute-done | bytes 229408 | tf_op jit(solution)/shard_map/ppermute | solution.py:130
  13.0 2.0 %collective-permute-start.6 = (bf16[288,512]{1,0:T(8,128)(2,1)S(1)}, bf16[288,512]{1,0:T(8,128)(2,1)S(1)}, u32[]{:S(2)}, u32[]{:S(2)}) collective-permute-start(bf16[288,512]{1,0:T(8,128)(2,1)S(1)} %collective-permute-done.refs_2_), channel_id=1, source_target_pairs={{0,4},{4,8},{8,12},{12,14},{14,10},{10,6},{6,2},{2,0},{1,5},{5,9},... | collective-permute-start | bytes 884744 | tf_op jit(solution)/shard_map/ppermute | solution.py:129
  15.0 0.7 %fusion.2 = s32[8]{0:T(128)S(1)} fusion(s32[2,8]{1,0:T(2,128)} %param.9, s32[]{:T(128)S(6)} %select_n.122), kind=kLoop, calls=%fused_computation.29 | loop fusion | bytes 68 | tf_op jit(solution)/shard_map/jit(dynamic_index_in_dim)/squeeze | solution.py:153
  15.7 0.6 %gather_fusion.2 = s32[8]{0:T(128)S(1)} fusion(s32[8]{0:T(128)S(1)} %fusion.2, s32[1024]{0:T(1024)S(1)} %get-tuple-element.24), kind=kCustom, calls=%fused_computation.2 | custom fusion | bytes 96 | tf_op jit(solution)/shard_map/gather | solution.py:154
  16.3 0.7 %collective-permute-done.4.refs_4_ = bf16[224,512]{1,0:T(8,128)(2,1)S(1)} collective-permute-done((bf16[224,512]{1,0:T(8,128)(2,1)S(1)}, bf16[224,512]{1,0:T(8,128)(2,1)S(1)}, u32[]{:S(2)}, u32[]{:S(2)}) %collective-permute-start.4) | collective-permute-done | bytes 229408 | tf_op jit(solution)/shard_map/ppermute | solution.py:129
  17.0 2.1 %collective-permute-start.8 = (bf16[224,512]{1,0:T(8,128)(2,1)S(1)}, bf16[224,512]{1,0:T(8,128)(2,1)}, u32[]{:S(2)}, u32[]{:S(2)}) collective-permute-start(bf16[224,512]{1,0:T(8,128)(2,1)S(1)} %collective-permute-done.4.refs_4_), channel_id=1, source_target_pairs={{0,4},{4,8},{8,12},{12,14},{14,10},{10,6},{6,2},{2,0},{1,5},{5,9},... | collective-permute-start | bytes 688136 | tf_op jit(solution)/shard_map/ppermute | solution.py:129
  19.1 0.1 collective-permute-done.5.refs_5_
  19.2 1.3 %collective-permute-done.1 = s32[3,1]{0,1:T(1,128)S(1)} collective-permute-done((s32[3,1]{0,1:T(1,128)}, s32[3,1]{0,1:T(1,128)S(1)}, u32[]{:S(2)}, u32[]{:S(2)}) %collective-permute-start.1) | collective-permute-done | bytes 44 | tf_op jit(solution)/shard_map/ppermute | solution.py:142
  20.5 2.3 %collective-permute-done.7.refs_7_ = bf16[224,512]{1,0:T(8,128)(2,1)} collective-permute-done((bf16[224,512]{1,0:T(8,128)(2,1)S(1)}, bf16[224,512]{1,0:T(8,128)(2,1)}, u32[]{:S(2)}, u32[]{:S(2)}) %collective-permute-start.7) | collective-permute-done | bytes 229408 | tf_op jit(solution)/shard_map/ppermute | solution.py:130
  22.8 0.3 collective-permute-start.11
  23.1 0.2 collective-permute-done.6.refs_6_
  23.3 2.1 %collective-permute-start.10 = (bf16[288,512]{1,0:T(8,128)(2,1)S(1)}, bf16[288,512]{1,0:T(8,128)(2,1)S(1)}, u32[]{:S(2)}, u32[]{:S(2)}) collective-permute-start(bf16[288,512]{1,0:T(8,128)(2,1)S(1)} %collective-permute-done.6.refs_6_), channel_id=1, source_target_pairs={{0,4},{4,8},{8,12},{12,14},{14,10},{10,6},{6,2},{2,0},{1,5},{5,9},... | collective-permute-start | bytes 884744 | tf_op jit(solution)/shard_map/ppermute | solution.py:129
  25.5 0.7 %add_bitcast_fusion = s32[6]{0:T(128)S(1)} fusion(s32[3,1]{0,1:T(1,128)S(1)} %collective-permute-done.1, s32[3,1]{0,1:T(1,128)} %param.10), kind=kLoop, calls=%fused_computation.36 | loop fusion | flops 6 | bytes 48 | tf_op jit(solution)/shard_map/squeeze | solution.py:141
  26.2 0.6 %gather_fusion.3 = s32[8]{0:T(128)S(1)} fusion(s32[6]{0:T(128)S(1)} %add_bitcast_fusion, s32[1024]{0:T(1024)S(1)} %get-tuple-element.23), kind=kCustom, calls=%fused_computation.3 | custom fusion | bytes 96 | tf_op jit(solution)/shard_map/gather | solution.py:160
  26.9 0.6 %slice.3 = s32[1]{0:T(128)} slice(s32[8]{0:T(128)S(1)} %get-tuple-element.20.slots), slice={[4:5]} | slice | bytes 8 | tf_op jit(solution)/shard_map/slice | solution.py:198
  29.4 1.6 %collective-permute-start.12 = (bf16[224,512]{1,0:T(8,128)(2,1)}, bf16[224,512]{1,0:T(8,128)(2,1)S(1)}, u32[]{:S(2)}, u32[]{:S(2)}) collective-permute-start(bf16[224,512]{1,0:T(8,128)(2,1)} %collective-permute-done.8.refs_8_), channel_id=1, source_target_pairs={{0,4},{4,8},{8,12},{12,14},{14,10},{10,6},{6,2},{2,0},{1,5},{5,9},... | collective-permute-start | bytes 688136 | tf_op jit(solution)/shard_map/ppermute | solution.py:129
  31.0 0.4 collective-permute-start.13
  31.5 3.9 %collective-permute-done.11.refs_1_ = bf16[224,512]{1,0:T(8,128)(2,1)} collective-permute-done((bf16[224,512]{1,0:T(8,128)(2,1)}, bf16[224,512]{1,0:T(8,128)(2,1)}, u32[]{:S(2)}, u32[]{:S(2)}) %collective-permute-start.11) | collective-permute-done | bytes 229408 | tf_op jit(solution)/shard_map/ppermute | solution.py:130
  35.4 2.0 %collective-permute-start.14 = (bf16[288,512]{1,0:T(8,128)(2,1)S(1)}, bf16[288,512]{1,0:T(8,128)(2,1)S(1)}, u32[]{:S(2)}, u32[]{:S(2)}) collective-permute-start(bf16[288,512]{1,0:T(8,128)(2,1)S(1)} %collective-permute-done.10.refs_0_), channel_id=1, source_target_pairs={{0,4},{4,8},{8,12},{12,14},{14,10},{10,6},{6,2},{2,0},{1,5},{5,9},... | collective-permute-start | bytes 884744 | tf_op jit(solution)/shard_map/ppermute | solution.py:135
  37.4 2.1 %pad_maximum_fusion = bf16[3072,512]{1,0:T(8,128)(2,1)S(1)} fusion(bf16[1536,512]{1,0:T(8,128)(2,1)} %collective-permute-done.2, bf16[1536,512]{1,0:T(8,128)(2,1)} %param.8), kind=kLoop, calls=%fused_computation.4 | loop fusion | flops 6291456 | bytes 6291456 | tf_op jit(solution)/shard_map/concatenate | solution.py:139
  39.5 1.2 %shard_map.73.before = f32[512,512]{1,0:T(8,128)S(1)} custom-call(s32[8]{0:T(128)S(1)} %get-tuple-element.20.slots, s32[8]{0:T(128)S(1)} %get-tuple-element.19.flags, bf16[6,512,512]{2,1,0:T(8,128)(2,1)S(1)} %bitcast.30, bf16[288,512]{1,0:T(8,128)(2,1)S(1)} %constant_dynamic-slice_fusion.1.refs_0_, bf16[224,512]{1,0:T(8,128)(2,1)S(1)} %constant_dynamic-slice_fusion.refs_1_, ...), custom_call_target="tpu_custom_call" | custom-call | flops 1342177280 | bytes 9437184 | tf_op jit(solution)/shard_map/pallas_call | solution.py:181
  40.7 0.9 %collective-permute-done.13.refs_3_ = bf16[288,512]{1,0:T(8,128)(2,1)S(1)} collective-permute-done((bf16[288,512]{1,0:T(8,128)(2,1)S(1)}, bf16[288,512]{1,0:T(8,128)(2,1)S(1)}, u32[]{:S(2)}, u32[]{:S(2)}) %collective-permute-start.13) | collective-permute-done | bytes 294944 | tf_op jit(solution)/shard_map/ppermute | solution.py:130
  41.6 2.5 %shard_map.74 = (f32[512,512]{1,0:T(8,128)S(1)}, s32[8,128]{1,0:T(8,128)S(1)}, bf16[512,512]{1,0:T(8,128)(2,1)}) custom-call(s32[8]{0:T(128)S(1)} %get-tuple-element.20.slots, s32[8]{0:T(128)S(1)} %get-tuple-element.19.flags, bf16[6,512,512]{2,1,0:T(8,128)(2,1)S(1)} %bitcast.31, f32[512,512]{1,0:T(8,128)S(1)} %shard_map.73.before, ...), custom_call_target="tpu_custom_call" | custom-call | flops 536870912 | bytes 6291456 | tf_op jit(solution)/shard_map/pallas_call | solution.py:189
  44.1 1.6 %collective-permute-done.15.refs_1_ = bf16[224,512]{1,0:T(8,128)(2,1)S(1)} collective-permute-done((bf16[224,512]{1,0:T(8,128)(2,1)}, bf16[224,512]{1,0:T(8,128)(2,1)S(1)}, u32[]{:S(2)}, u32[]{:S(2)}) %collective-permute-start.15) | collective-permute-done | bytes 229408 | tf_op jit(solution)/shard_map/ppermute | solution.py:136
  (24 shorter events, 0.4 us)
Async XLA Ops:
  0.0 1.2 %copy-start = (bf16[1024,512]{1,0:T(8,128)(2,1)S(1)}, bf16[1024,512]{1,0:T(8,128)(2,1)}, u32[]{:S(2)}) copy-start(bf16[1024,512]{1,0:T(8,128)(2,1)} %param.7) | copy-start | bytes 3145732
  0.0 37.4 %collective-permute-start.2 = (bf16[1536,512]{1,0:T(8,128)(2,1)}, bf16[1536,512]{1,0:T(8,128)(2,1)}, u32[]{:S(2)}, u32[]{:S(2)}) collective-permute-start(bf16[1536,512]{1,0:T(8,128)(2,1)} %param.8), channel_id=1, source_target_pairs={{0,1},{1,0},{2,3},{3,2},{4,5},{5,4},{6,7},{7,6},{8,9},{9,8},{10,11... | collective-permute-start | bytes 4718600 | tf_op jit(solution)/shard_map/ppermute | solution.py:138
  1.2 11.7 %collective-permute-start = (bf16[288,512]{1,0:T(8,128)(2,1)S(1)}, bf16[288,512]{1,0:T(8,128)(2,1)S(1)}, u32[]{:S(2)}, u32[]{:S(2)}) collective-permute-start(bf16[288,512]{1,0:T(8,128)(2,1)S(1)} %constant_dynamic-slice_fusion.1.refs_0_), channel_id=1, source_target_pairs={{0,4},{4,8},{8,12},{12,14},{14,10},{10,6},{6,2},{2,0},{1,5},{5,9},... | collective-permute-start | bytes 884744 | tf_op jit(solution)/shard_map/ppermute | solution.py:129
  4.3 8.6 %collective-permute-start.3 = (bf16[224,512]{1,0:T(8,128)(2,1)S(1)}, bf16[224,512]{1,0:T(8,128)(2,1)S(1)}, u32[]{:S(2)}, u32[]{:S(2)}) collective-permute-start(bf16[224,512]{1,0:T(8,128)(2,1)S(1)} %constant_dynamic-slice_fusion.refs_1_), channel_id=1, source_target_pairs={{4,0},{8,4},{12,8},{14,12},{10,14},{6,10},{2,6},{0,2},{5,1},{9,5},... | collective-permute-start | bytes 688136 | tf_op jit(solution)/shard_map/ppermute | solution.py:130
  4.4 12.6 %collective-permute-start.4 = (bf16[224,512]{1,0:T(8,128)(2,1)S(1)}, bf16[224,512]{1,0:T(8,128)(2,1)S(1)}, u32[]{:S(2)}, u32[]{:S(2)}) collective-permute-start(bf16[224,512]{1,0:T(8,128)(2,1)S(1)} %constant_dynamic-slice_fusion.refs_1_), channel_id=1, source_target_pairs={{0,4},{4,8},{8,12},{12,14},{14,10},{10,6},{6,2},{2,0},{1,5},{5,9},... | collective-permute-start | bytes 688136 | tf_op jit(solution)/shard_map/ppermute | solution.py:129
  6.4 12.8 %collective-permute-start.5 = (bf16[288,512]{1,0:T(8,128)(2,1)S(1)}, bf16[288,512]{1,0:T(8,128)(2,1)S(1)}, u32[]{:S(2)}, u32[]{:S(2)}) collective-permute-start(bf16[288,512]{1,0:T(8,128)(2,1)S(1)} %constant_dynamic-slice_fusion.1.refs_0_), channel_id=1, source_target_pairs={{4,0},{8,4},{12,8},{14,12},{10,14},{6,10},{2,6},{0,2},{5,1},{9,5},... | collective-permute-start | bytes 884744 | tf_op jit(solution)/shard_map/ppermute | solution.py:130
  12.9 9.9 %collective-permute-start.7 = (bf16[224,512]{1,0:T(8,128)(2,1)S(1)}, bf16[224,512]{1,0:T(8,128)(2,1)}, u32[]{:S(2)}, u32[]{:S(2)}) collective-permute-start(bf16[224,512]{1,0:T(8,128)(2,1)S(1)} %collective-permute-done.3.refs_3_), channel_id=1, source_target_pairs={{4,0},{8,4},{12,8},{14,12},{10,14},{6,10},{2,6},{0,2},{5,1},{9,5},... | collective-permute-start | bytes 688136 | tf_op jit(solution)/shard_map/ppermute | solution.py:130
  13.0 10.4 %collective-permute-start.6 = (bf16[288,512]{1,0:T(8,128)(2,1)S(1)}, bf16[288,512]{1,0:T(8,128)(2,1)S(1)}, u32[]{:S(2)}, u32[]{:S(2)}) collective-permute-start(bf16[288,512]{1,0:T(8,128)(2,1)S(1)} %collective-permute-done.refs_2_), channel_id=1, source_target_pairs={{0,4},{4,8},{8,12},{12,14},{14,10},{10,6},{6,2},{2,0},{1,5},{5,9},... | collective-permute-start | bytes 884744 | tf_op jit(solution)/shard_map/ppermute | solution.py:129
  17.0 12.4 %collective-permute-start.8 = (bf16[224,512]{1,0:T(8,128)(2,1)S(1)}, bf16[224,512]{1,0:T(8,128)(2,1)}, u32[]{:S(2)}, u32[]{:S(2)}) collective-permute-start(bf16[224,512]{1,0:T(8,128)(2,1)S(1)} %collective-permute-done.4.refs_4_), channel_id=1, source_target_pairs={{0,4},{4,8},{8,12},{12,14},{14,10},{10,6},{6,2},{2,0},{1,5},{5,9},... | collective-permute-start | bytes 688136 | tf_op jit(solution)/shard_map/ppermute | solution.py:129
  19.2 1.3 %collective-permute-start.1 = (s32[3,1]{0,1:T(1,128)}, s32[3,1]{0,1:T(1,128)S(1)}, u32[]{:S(2)}, u32[]{:S(2)}) collective-permute-start(s32[3,1]{0,1:T(1,128)} %param.10), channel_id=1, source_target_pairs={{0,1},{1,0},{2,3},{3,2},{4,5},{5,4},{6,7},{7,6},{8,9},{9,8},{10,11... | collective-permute-start | bytes 44 | tf_op jit(solution)/shard_map/ppermute | solution.py:142
  20.5 10.5 %collective-permute-start.9 = (bf16[288,512]{1,0:T(8,128)(2,1)S(1)}, bf16[288,512]{1,0:T(8,128)(2,1)S(1)}, u32[]{:S(2)}, u32[]{:S(2)}) collective-permute-start(bf16[288,512]{1,0:T(8,128)(2,1)S(1)} %collective-permute-done.5.refs_5_), channel_id=1, source_target_pairs={{4,0},{8,4},{12,8},{14,12},{10,14},{6,10},{2,6},{0,2},{5,1},{9,5},... | collective-permute-start | bytes 884744 | tf_op jit(solution)/shard_map/ppermute | solution.py:130
  22.8 12.6 %collective-permute-start.11 = (bf16[224,512]{1,0:T(8,128)(2,1)}, bf16[224,512]{1,0:T(8,128)(2,1)}, u32[]{:S(2)}, u32[]{:S(2)}) collective-permute-start(bf16[224,512]{1,0:T(8,128)(2,1)} %collective-permute-done.7.refs_7_), channel_id=1, source_target_pairs={{4,0},{8,4},{12,8},{14,12},{10,14},{6,10},{2,6},{0,2},{5,1},{9,5},... | collective-permute-start | bytes 688136 | tf_op jit(solution)/shard_map/ppermute | solution.py:130
  23.3 12.1 %collective-permute-start.10 = (bf16[288,512]{1,0:T(8,128)(2,1)S(1)}, bf16[288,512]{1,0:T(8,128)(2,1)S(1)}, u32[]{:S(2)}, u32[]{:S(2)}) collective-permute-start(bf16[288,512]{1,0:T(8,128)(2,1)S(1)} %collective-permute-done.6.refs_6_), channel_id=1, source_target_pairs={{0,4},{4,8},{8,12},{12,14},{14,10},{10,6},{6,2},{2,0},{1,5},{5,9},... | collective-permute-start | bytes 884744 | tf_op jit(solution)/shard_map/ppermute | solution.py:129
  29.4 11.3 %collective-permute-start.12 = (bf16[224,512]{1,0:T(8,128)(2,1)}, bf16[224,512]{1,0:T(8,128)(2,1)S(1)}, u32[]{:S(2)}, u32[]{:S(2)}) collective-permute-start(bf16[224,512]{1,0:T(8,128)(2,1)} %collective-permute-done.8.refs_8_), channel_id=1, source_target_pairs={{0,4},{4,8},{8,12},{12,14},{14,10},{10,6},{6,2},{2,0},{1,5},{5,9},... | collective-permute-start | bytes 688136 | tf_op jit(solution)/shard_map/ppermute | solution.py:129
  31.0 10.6 %collective-permute-start.13 = (bf16[288,512]{1,0:T(8,128)(2,1)S(1)}, bf16[288,512]{1,0:T(8,128)(2,1)S(1)}, u32[]{:S(2)}, u32[]{:S(2)}) collective-permute-start(bf16[288,512]{1,0:T(8,128)(2,1)S(1)} %collective-permute-done.9.refs_9_), channel_id=1, source_target_pairs={{4,0},{8,4},{12,8},{14,12},{10,14},{6,10},{2,6},{0,2},{5,1},{9,5},... | collective-permute-start | bytes 884744 | tf_op jit(solution)/shard_map/ppermute | solution.py:130
  35.4 10.4 %collective-permute-start.15 = (bf16[224,512]{1,0:T(8,128)(2,1)}, bf16[224,512]{1,0:T(8,128)(2,1)S(1)}, u32[]{:S(2)}, u32[]{:S(2)}) collective-permute-start(bf16[224,512]{1,0:T(8,128)(2,1)} %collective-permute-done.11.refs_1_), channel_id=1, source_target_pairs={{4,0},{8,4},{12,8},{14,12},{10,14},{6,10},{2,6},{0,2},{5,1},{9,5},... | collective-permute-start | bytes 688136 | tf_op jit(solution)/shard_map/ppermute | solution.py:136
  35.4 10.4 %collective-permute-start.14 = (bf16[288,512]{1,0:T(8,128)(2,1)S(1)}, bf16[288,512]{1,0:T(8,128)(2,1)S(1)}, u32[]{:S(2)}, u32[]{:S(2)}) collective-permute-start(bf16[288,512]{1,0:T(8,128)(2,1)S(1)} %collective-permute-done.10.refs_0_), channel_id=1, source_target_pairs={{0,4},{4,8},{8,12},{12,14},{14,10},{10,6},{6,2},{2,0},{1,5},{5,9},... | collective-permute-start | bytes 884744 | tf_op jit(solution)/shard_map/ppermute | solution.py:135

commit v6 on v5

--- a/solution.py
+++ b/solution.py
@@ -137,7 +137,7 @@
 
     swapped = lax.ppermute(inner_tiles, "depth", [(0, 1), (1, 0)])
     inner = jnp.concatenate([inner_tiles, swapped], axis=0).reshape(-1, size, size)
-    inner_mask, _ = lax.optimization_barrier((inner_mask, pieces[(grid_size - 1, 0)]))
+    inner_mask, _ = lax.optimization_barrier((inner_mask, pieces[(grid_size - 1, 1)]))
     tile_flags = jnp.concatenate(
         [inner_mask, lax.ppermute(inner_mask, "depth", [(0, 1), (1, 0)])], axis=0
     )[:, 0]
@@ -173,7 +173,7 @@
 
     def cost(items):
         return pl.CostEstimate(
-            flops=len(items) * size**3,
+            flops=3 * len(items) * size**3,
             bytes_accessed=2 * (inner.size + (len(items) + 2) * size**2),
             transcendentals=0,
         )

time: 46.1 us -> 45.7 us (level)
  transfers between devices with their start and end apart: 16 -> 16, of which waited for: 9 -> 8; matrix products, arithmetic and copies ran while one was open for 22% -> 22% of each run, Pallas kernels for 8% -> 8%
where the time goes in v6:
time: 45.7 us; the launch traced here: 45.5 us
  starting transfers between devices  16.3 us (36%)
  waiting for transfers between devices  12.6 us (28%)
  local copies, waits for them, and re-layouts  7.24 us (16%)
  Pallas kernels  3.76 us (8%)
  other arithmetic  3.54 us (8%)
  between operations  2.05 us (4%)
    ppermute x6, starting transfers between devices, gather_columns(): right[h] = lax.ppermute(right[h], 'grid', onward)  12.9 us
    ppermute x6, waiting for transfers between devices, gather_columns(): left[1 - h] = lax.ppermute(left[1 - h], 'grid', backward)  9.05 us
    pallas_call x1, Pallas kernels, gather_columns(): pl.pallas_call(functools.partial(middle_kernel, placed(far), steps + 1),...  2.49 us
    concatenate x1, other arithmetic, gather_columns(): jnp.concatenate([inner_tiles, swapped], axis=0).reshape(-1, size, size)  2.09 us
    ppermute x1, starting transfers between devices, gather_columns(): last[steps + 1, 0] = lax.ppermute(right[0], 'grid', onward)  2.02 us
    ppermute x1, waiting for transfers between devices, gather_columns(): last[steps + 1, 1] = lax.ppermute(left[1], 'grid', backward)  1.37 us
    gather x1, local copies, waits for them, and re-layouts, gather_columns(): jnp.asarray(order, jnp.int32)  1.3 us
    gather x1, local copies, waits for them, and re-layouts, gather_columns(): true_column = held_col[sources]  1.3 us
  transfers between devices with their start and end apart: 16, of which 8 were waited for; matrix products, arithmetic and copies ran while one was open for 22% of the time, Pallas kernels for 8%

profile of v6, /device:TPU:0, one launch (start us, length us, event | category | flops | bytes accessed | tf_op | source)
XLA Modules:
  0.0 45.5 jit_solution(9810906476125564652)
XLA Ops:
  0.0 0.5 collective-permute-start.2
  0.5 0.8 %copy-done = bf16[1024,512]{1,0:T(8,128)(2,1)S(1)} copy-done((bf16[1024,512]{1,0:T(8,128)(2,1)S(1)}, bf16[1024,512]{1,0:T(8,128)(2,1)}, u32[]{:S(2)}) %copy-start) | copy-done | bytes 1048600
  1.2 3.1 %collective-permute-start.3 = (bf16[288,512]{1,0:T(8,128)(2,1)S(1)}, bf16[288,512]{1,0:T(8,128)(2,1)S(1)}, u32[]{:S(2)}, u32[]{:S(2)}) collective-permute-start(bf16[288,512]{1,0:T(8,128)(2,1)S(1)} %constant_dynamic-slice_fusion.1.refs_0_), channel_id=1, source_target_pairs={{0,4},{4,8},{8,12},{12,14},{14,10},{10,6},{6,2},{2,0},{1,5},{5,9},... | collective-permute-start | bytes 884744 | tf_op jit(solution)/shard_map/ppermute | solution.py:129
  4.4 2.0 %collective-permute-start = (bf16[224,512]{1,0:T(8,128)(2,1)S(1)}, bf16[224,512]{1,0:T(8,128)(2,1)S(1)}, u32[]{:S(2)}, u32[]{:S(2)}) collective-permute-start(bf16[224,512]{1,0:T(8,128)(2,1)S(1)} %constant_dynamic-slice_fusion.refs_1_), channel_id=1, source_target_pairs={{0,4},{4,8},{8,12},{12,14},{14,10},{10,6},{6,2},{2,0},{1,5},{5,9},... | collective-permute-start | bytes 688136 | tf_op jit(solution)/shard_map/ppermute | solution.py:129
  6.4 0.1 collective-permute-start.5
  6.5 1.2 %dynamic_slice.17 = s32[1]{0:T(128)} dynamic-slice(s32[8]{0:T(128)} %constant.68.clone, s32[]{:T(128)S(6)} %select_n.115), dynamic_slice_sizes={1} | dynamic-slice | bytes 12 | tf_op jit(solution)/shard_map/dynamic_slice | solution.py:145
  7.7 0.7 %fusion.5 = s32[8]{0:T(128)S(1)} fusion(s32[]{:T(128)} %bitcast), kind=kLoop, calls=%fused_computation.32 | loop fusion | flops 120 | bytes 36 | tf_op jit(solution)/shard_map/select_n | solution.py:146
  8.4 1.3 %gather_fusion = s32[8]{0:T(128)S(1)} fusion(s32[8]{0:T(128)} %constant.69.clone, s32[1024]{0:T(1024)S(1)} %pad_clamp_fusion.3), kind=kCustom, calls=%fused_computation | custom fusion | bytes 96 | tf_op jit(solution)/shard_map/gather | solution.py:146
  9.7 1.3 %gather_fusion.1 = s32[8]{0:T(128)S(1)} fusion(s32[8]{0:T(128)} %param.11, s32[1024]{0:T(1024)S(1)} %pad_clamp_fusion.2), kind=kCustom, calls=%fused_computation.1 | custom fusion | bytes 96 | tf_op jit(solution)/shard_map/gather | solution.py:149
  11.0 1.9 %collective-permute-done.4.refs_3_ = bf16[224,512]{1,0:T(8,128)(2,1)S(1)} collective-permute-done((bf16[224,512]{1,0:T(8,128)(2,1)S(1)}, bf16[224,512]{1,0:T(8,128)(2,1)S(1)}, u32[]{:S(2)}, u32[]{:S(2)}) %collective-permute-start.4) | collective-permute-done | bytes 229408 | tf_op jit(solution)/shard_map/ppermute | solution.py:130
  13.0 2.0 %collective-permute-start.6 = (bf16[288,512]{1,0:T(8,128)(2,1)S(1)}, bf16[288,512]{1,0:T(8,128)(2,1)S(1)}, u32[]{:S(2)}, u32[]{:S(2)}) collective-permute-start(bf16[288,512]{1,0:T(8,128)(2,1)S(1)} %collective-permute-done.3.refs_2_), channel_id=1, source_target_pairs={{0,4},{4,8},{8,12},{12,14},{14,10},{10,6},{6,2},{2,0},{1,5},{5,9},... | collective-permute-start | bytes 884744 | tf_op jit(solution)/shard_map/ppermute | solution.py:129
  15.0 0.7 %fusion.2 = s32[8]{0:T(128)S(1)} fusion(s32[2,8]{1,0:T(2,128)} %param.9, s32[]{:T(128)S(6)} %select_n.122), kind=kLoop, calls=%fused_computation.29 | loop fusion | bytes 68 | tf_op jit(solution)/shard_map/jit(dynamic_index_in_dim)/squeeze | solution.py:153
  15.7 0.6 %gather_fusion.2 = s32[8]{0:T(128)S(1)} fusion(s32[8]{0:T(128)S(1)} %fusion.2, s32[1024]{0:T(1024)S(1)} %get-tuple-element.24), kind=kCustom, calls=%fused_computation.2 | custom fusion | bytes 96 | tf_op jit(solution)/shard_map/gather | solution.py:154
  16.3 0.7 %collective-permute-done.refs_4_ = bf16[224,512]{1,0:T(8,128)(2,1)S(1)} collective-permute-done((bf16[224,512]{1,0:T(8,128)(2,1)S(1)}, bf16[224,512]{1,0:T(8,128)(2,1)S(1)}, u32[]{:S(2)}, u32[]{:S(2)}) %collective-permute-start) | collective-permute-done | bytes 229408 | tf_op jit(solution)/shard_map/ppermute | solution.py:129
  17.0 1.3 %collective-permute-done.1 = s32[3,1]{0,1:T(1,128)S(1)} collective-permute-done((s32[3,1]{0,1:T(1,128)}, s32[3,1]{0,1:T(1,128)S(1)}, u32[]{:S(2)}, u32[]{:S(2)}) %collective-permute-start.1) | collective-permute-done | bytes 44 | tf_op jit(solution)/shard_map/ppermute | solution.py:142
  18.2 2.1 %collective-permute-start.8 = (bf16[224,512]{1,0:T(8,128)(2,1)S(1)}, bf16[224,512]{1,0:T(8,128)(2,1)}, u32[]{:S(2)}, u32[]{:S(2)}) collective-permute-start(bf16[224,512]{1,0:T(8,128)(2,1)S(1)} %collective-permute-done.refs_4_), channel_id=1, source_target_pairs={{0,4},{4,8},{8,12},{12,14},{14,10},{10,6},{6,2},{2,0},{1,5},{5,9},... | collective-permute-start | bytes 688136 | tf_op jit(solution)/shard_map/ppermute | solution.py:129
  20.4 2.4 %collective-permute-done.7.refs_7_ = bf16[224,512]{1,0:T(8,128)(2,1)} collective-permute-done((bf16[224,512]{1,0:T(8,128)(2,1)S(1)}, bf16[224,512]{1,0:T(8,128)(2,1)}, u32[]{:S(2)}, u32[]{:S(2)}) %collective-permute-start.7) | collective-permute-done | bytes 229408 | tf_op jit(solution)/shard_map/ppermute | solution.py:130
  22.8 0.3 collective-permute-start.11
  23.1 0.2 collective-permute-done.6.refs_6_
  23.3 2.0 %collective-permute-start.10 = (bf16[288,512]{1,0:T(8,128)(2,1)S(1)}, bf16[288,512]{1,0:T(8,128)(2,1)S(1)}, u32[]{:S(2)}, u32[]{:S(2)}) collective-permute-start(bf16[288,512]{1,0:T(8,128)(2,1)S(1)} %collective-permute-done.6.refs_6_), channel_id=1, source_target_pairs={{0,4},{4,8},{8,12},{12,14},{14,10},{10,6},{6,2},{2,0},{1,5},{5,9},... | collective-permute-start | bytes 884744 | tf_op jit(solution)/shard_map/ppermute | solution.py:129
  25.4 0.7 %add_bitcast_fusion = s32[6]{0:T(128)S(1)} fusion(s32[3,1]{0,1:T(1,128)S(1)} %collective-permute-done.1, s32[3,1]{0,1:T(1,128)} %param.10), kind=kLoop, calls=%fused_computation.36 | loop fusion | flops 6 | bytes 48 | tf_op jit(solution)/shard_map/squeeze | solution.py:141
  26.1 0.6 %gather_fusion.3 = s32[8]{0:T(128)S(1)} fusion(s32[6]{0:T(128)S(1)} %add_bitcast_fusion, s32[1024]{0:T(1024)S(1)} %get-tuple-element.23), kind=kCustom, calls=%fused_computation.3 | custom fusion | bytes 96 | tf_op jit(solution)/shard_map/gather | solution.py:160
  26.8 0.6 %slice.3 = s32[1]{0:T(128)} slice(s32[8]{0:T(128)S(1)} %get-tuple-element.20.slots), slice={[4:5]} | slice | bytes 8 | tf_op jit(solution)/shard_map/slice | solution.py:198
  29.3 1.6 %collective-permute-start.12 = (bf16[224,512]{1,0:T(8,128)(2,1)}, bf16[224,512]{1,0:T(8,128)(2,1)S(1)}, u32[]{:S(2)}, u32[]{:S(2)}) collective-permute-start(bf16[224,512]{1,0:T(8,128)(2,1)} %collective-permute-done.8.refs_8_), channel_id=1, source_target_pairs={{0,4},{4,8},{8,12},{12,14},{14,10},{10,6},{6,2},{2,0},{1,5},{5,9},... | collective-permute-start | bytes 688136 | tf_op jit(solution)/shard_map/ppermute | solution.py:129
  30.9 0.4 collective-permute-start.13
  31.4 3.9 %collective-permute-done.11.refs_1_ = bf16[224,512]{1,0:T(8,128)(2,1)} collective-permute-done((bf16[224,512]{1,0:T(8,128)(2,1)}, bf16[224,512]{1,0:T(8,128)(2,1)}, u32[]{:S(2)}, u32[]{:S(2)}) %collective-permute-start.11) | collective-permute-done | bytes 229408 | tf_op jit(solution)/shard_map/ppermute | solution.py:130
  35.3 2.0 %collective-permute-start.14 = (bf16[288,512]{1,0:T(8,128)(2,1)S(1)}, bf16[288,512]{1,0:T(8,128)(2,1)S(1)}, u32[]{:S(2)}, u32[]{:S(2)}) collective-permute-start(bf16[288,512]{1,0:T(8,128)(2,1)S(1)} %collective-permute-done.10.refs_0_), channel_id=1, source_target_pairs={{0,4},{4,8},{8,12},{12,14},{14,10},{10,6},{6,2},{2,0},{1,5},{5,9},... | collective-permute-start | bytes 884744 | tf_op jit(solution)/shard_map/ppermute | solution.py:135
  37.3 2.1 %pad_maximum_fusion = bf16[3072,512]{1,0:T(8,128)(2,1)S(1)} fusion(bf16[1536,512]{1,0:T(8,128)(2,1)} %collective-permute-done.2, bf16[1536,512]{1,0:T(8,128)(2,1)} %param.8), kind=kLoop, calls=%fused_computation.4 | loop fusion | flops 6291456 | bytes 6291456 | tf_op jit(solution)/shard_map/concatenate | solution.py:139
  39.4 1.2 %shard_map.73.before = f32[512,512]{1,0:T(8,128)S(1)} custom-call(s32[8]{0:T(128)S(1)} %get-tuple-element.20.slots, s32[8]{0:T(128)S(1)} %get-tuple-element.19.flags, bf16[6,512,512]{2,1,0:T(8,128)(2,1)S(1)} %bitcast.30, bf16[288,512]{1,0:T(8,128)(2,1)S(1)} %constant_dynamic-slice_fusion.1.refs_0_, bf16[224,512]{1,0:T(8,128)(2,1)S(1)} %constant_dynamic-slice_fusion.refs_1_, ...), custom_call_target="tpu_custom_call" | custom-call | flops 4026531840 | bytes 9437184 | tf_op jit(solution)/shard_map/pallas_call | solution.py:181
  40.7 0.8 %collective-permute-done.13.refs_3_ = bf16[288,512]{1,0:T(8,128)(2,1)S(1)} collective-permute-done((bf16[288,512]{1,0:T(8,128)(2,1)S(1)}, bf16[288,512]{1,0:T(8,128)(2,1)S(1)}, u32[]{:S(2)}, u32[]{:S(2)}) %collective-permute-start.13) | collective-permute-done | bytes 294944 | tf_op jit(solution)/shard_map/ppermute | solution.py:130
  41.5 2.5 %shard_map.74 = (f32[512,512]{1,0:T(8,128)S(1)}, s32[8,128]{1,0:T(8,128)S(1)}, bf16[512,512]{1,0:T(8,128)(2,1)}) custom-call(s32[8]{0:T(128)S(1)} %get-tuple-element.20.slots, s32[8]{0:T(128)S(1)} %get-tuple-element.19.flags, bf16[6,512,512]{2,1,0:T(8,128)(2,1)S(1)} %bitcast.32, f32[512,512]{1,0:T(8,128)S(1)} %shard_map.73.before, ...), custom_call_target="tpu_custom_call" | custom-call | flops 1610612736 | bytes 6291456 | tf_op jit(solution)/shard_map/pallas_call | solution.py:189
  44.0 1.4 %collective-permute-done.15.refs_1_ = bf16[224,512]{1,0:T(8,128)(2,1)S(1)} collective-permute-done((bf16[224,512]{1,0:T(8,128)(2,1)}, bf16[224,512]{1,0:T(8,128)(2,1)S(1)}, u32[]{:S(2)}, u32[]{:S(2)}) %collective-permute-start.15) | collective-permute-done | bytes 229408 | tf_op jit(solution)/shard_map/ppermute | solution.py:136
  (24 shorter events, 0.3 us)
Async XLA Ops:
  0.0 1.2 %copy-start = (bf16[1024,512]{1,0:T(8,128)(2,1)S(1)}, bf16[1024,512]{1,0:T(8,128)(2,1)}, u32[]{:S(2)}) copy-start(bf16[1024,512]{1,0:T(8,128)(2,1)} %param.7) | copy-start | bytes 3145732
  0.0 37.3 %collective-permute-start.2 = (bf16[1536,512]{1,0:T(8,128)(2,1)}, bf16[1536,512]{1,0:T(8,128)(2,1)}, u32[]{:S(2)}, u32[]{:S(2)}) collective-permute-start(bf16[1536,512]{1,0:T(8,128)(2,1)} %param.8), channel_id=1, source_target_pairs={{0,1},{1,0},{2,3},{3,2},{4,5},{5,4},{6,7},{7,6},{8,9},{9,8},{10,11... | collective-permute-start | bytes 4718600 | tf_op jit(solution)/shard_map/ppermute | solution.py:138
  1.2 11.7 %collective-permute-start.3 = (bf16[288,512]{1,0:T(8,128)(2,1)S(1)}, bf16[288,512]{1,0:T(8,128)(2,1)S(1)}, u32[]{:S(2)}, u32[]{:S(2)}) collective-permute-start(bf16[288,512]{1,0:T(8,128)(2,1)S(1)} %constant_dynamic-slice_fusion.1.refs_0_), channel_id=1, source_target_pairs={{0,4},{4,8},{8,12},{12,14},{14,10},{10,6},{6,2},{2,0},{1,5},{5,9},... | collective-permute-start | bytes 884744 | tf_op jit(solution)/shard_map/ppermute | solution.py:129
  4.3 8.6 %collective-permute-start.4 = (bf16[224,512]{1,0:T(8,128)(2,1)S(1)}, bf16[224,512]{1,0:T(8,128)(2,1)S(1)}, u32[]{:S(2)}, u32[]{:S(2)}) collective-permute-start(bf16[224,512]{1,0:T(8,128)(2,1)S(1)} %constant_dynamic-slice_fusion.refs_1_), channel_id=1, source_target_pairs={{4,0},{8,4},{12,8},{14,12},{10,14},{6,10},{2,6},{0,2},{5,1},{9,5},... | collective-permute-start | bytes 688136 | tf_op jit(solution)/shard_map/ppermute | solution.py:130
  4.4 12.6 %collective-permute-start = (bf16[224,512]{1,0:T(8,128)(2,1)S(1)}, bf16[224,512]{1,0:T(8,128)(2,1)S(1)}, u32[]{:S(2)}, u32[]{:S(2)}) collective-permute-start(bf16[224,512]{1,0:T(8,128)(2,1)S(1)} %constant_dynamic-slice_fusion.refs_1_), channel_id=1, source_target_pairs={{0,4},{4,8},{8,12},{12,14},{14,10},{10,6},{6,2},{2,0},{1,5},{5,9},... | collective-permute-start | bytes 688136 | tf_op jit(solution)/shard_map/ppermute | solution.py:129
  6.4 14.0 %collective-permute-start.5 = (bf16[288,512]{1,0:T(8,128)(2,1)S(1)}, bf16[288,512]{1,0:T(8,128)(2,1)S(1)}, u32[]{:S(2)}, u32[]{:S(2)}) collective-permute-start(bf16[288,512]{1,0:T(8,128)(2,1)S(1)} %constant_dynamic-slice_fusion.1.refs_0_), channel_id=1, source_target_pairs={{4,0},{8,4},{12,8},{14,12},{10,14},{6,10},{2,6},{0,2},{5,1},{9,5},... | collective-permute-start | bytes 884744 | tf_op jit(solution)/shard_map/ppermute | solution.py:130
  12.9 9.9 %collective-permute-start.7 = (bf16[224,512]{1,0:T(8,128)(2,1)S(1)}, bf16[224,512]{1,0:T(8,128)(2,1)}, u32[]{:S(2)}, u32[]{:S(2)}) collective-permute-start(bf16[224,512]{1,0:T(8,128)(2,1)S(1)} %collective-permute-done.4.refs_3_), channel_id=1, source_target_pairs={{4,0},{8,4},{12,8},{14,12},{10,14},{6,10},{2,6},{0,2},{5,1},{9,5},... | collective-permute-start | bytes 688136 | tf_op jit(solution)/shard_map/ppermute | solution.py:130
  13.0 10.4 %collective-permute-start.6 = (bf16[288,512]{1,0:T(8,128)(2,1)S(1)}, bf16[288,512]{1,0:T(8,128)(2,1)S(1)}, u32[]{:S(2)}, u32[]{:S(2)}) collective-permute-start(bf16[288,512]{1,0:T(8,128)(2,1)S(1)} %collective-permute-done.3.refs_2_), channel_id=1, source_target_pairs={{0,4},{4,8},{8,12},{12,14},{14,10},{10,6},{6,2},{2,0},{1,5},{5,9},... | collective-permute-start | bytes 884744 | tf_op jit(solution)/shard_map/ppermute | solution.py:129
  17.0 1.3 %collective-permute-start.1 = (s32[3,1]{0,1:T(1,128)}, s32[3,1]{0,1:T(1,128)S(1)}, u32[]{:S(2)}, u32[]{:S(2)}) collective-permute-start(s32[3,1]{0,1:T(1,128)} %param.10), channel_id=1, source_target_pairs={{0,1},{1,0},{2,3},{3,2},{4,5},{5,4},{6,7},{7,6},{8,9},{9,8},{10,11... | collective-permute-start | bytes 44 | tf_op jit(solution)/shard_map/ppermute | solution.py:142
  18.2 11.0 %collective-permute-start.8 = (bf16[224,512]{1,0:T(8,128)(2,1)S(1)}, bf16[224,512]{1,0:T(8,128)(2,1)}, u32[]{:S(2)}, u32[]{:S(2)}) collective-permute-start(bf16[224,512]{1,0:T(8,128)(2,1)S(1)} %collective-permute-done.refs_4_), channel_id=1, source_target_pairs={{0,4},{4,8},{8,12},{12,14},{14,10},{10,6},{6,2},{2,0},{1,5},{5,9},... | collective-permute-start | bytes 688136 | tf_op jit(solution)/shard_map/ppermute | solution.py:129
  20.4 10.5 %collective-permute-start.9 = (bf16[288,512]{1,0:T(8,128)(2,1)S(1)}, bf16[288,512]{1,0:T(8,128)(2,1)S(1)}, u32[]{:S(2)}, u32[]{:S(2)}) collective-permute-start(bf16[288,512]{1,0:T(8,128)(2,1)S(1)} %collective-permute-done.5.refs_5_), channel_id=1, source_target_pairs={{4,0},{8,4},{12,8},{14,12},{10,14},{6,10},{2,6},{0,2},{5,1},{9,5},... | collective-permute-start | bytes 884744 | tf_op jit(solution)/shard_map/ppermute | solution.py:130
  22.8 12.5 %collective-permute-start.11 = (bf16[224,512]{1,0:T(8,128)(2,1)}, bf16[224,512]{1,0:T(8,128)(2,1)}, u32[]{:S(2)}, u32[]{:S(2)}) collective-permute-start(bf16[224,512]{1,0:T(8,128)(2,1)} %collective-permute-done.7.refs_7_), channel_id=1, source_target_pairs={{4,0},{8,4},{12,8},{14,12},{10,14},{6,10},{2,6},{0,2},{5,1},{9,5},... | collective-permute-start | bytes 688136 | tf_op jit(solution)/shard_map/ppermute | solution.py:130
  23.3 12.0 %collective-permute-start.10 = (bf16[288,512]{1,0:T(8,128)(2,1)S(1)}, bf16[288,512]{1,0:T(8,128)(2,1)S(1)}, u32[]{:S(2)}, u32[]{:S(2)}) collective-permute-start(bf16[288,512]{1,0:T(8,128)(2,1)S(1)} %collective-permute-done.6.refs_6_), channel_id=1, source_target_pairs={{0,4},{4,8},{8,12},{12,14},{14,10},{10,6},{6,2},{2,0},{1,5},{5,9},... | collective-permute-start | bytes 884744 | tf_op jit(solution)/shard_map/ppermute | solution.py:129
  29.3 11.4 %collective-permute-start.12 = (bf16[224,512]{1,0:T(8,128)(2,1)}, bf16[224,512]{1,0:T(8,128)(2,1)S(1)}, u32[]{:S(2)}, u32[]{:S(2)}) collective-permute-start(bf16[224,512]{1,0:T(8,128)(2,1)} %collective-permute-done.8.refs_8_), channel_id=1, source_target_pairs={{0,4},{4,8},{8,12},{12,14},{14,10},{10,6},{6,2},{2,0},{1,5},{5,9},... | collective-permute-start | bytes 688136 | tf_op jit(solution)/shard_map/ppermute | solution.py:129
  30.9 10.6 %collective-permute-start.13 = (bf16[288,512]{1,0:T(8,128)(2,1)S(1)}, bf16[288,512]{1,0:T(8,128)(2,1)S(1)}, u32[]{:S(2)}, u32[]{:S(2)}) collective-permute-start(bf16[288,512]{1,0:T(8,128)(2,1)S(1)} %collective-permute-done.9.refs_9_), channel_id=1, source_target_pairs={{4,0},{8,4},{12,8},{14,12},{10,14},{6,10},{2,6},{0,2},{5,1},{9,5},... | collective-permute-start | bytes 884744 | tf_op jit(solution)/shard_map/ppermute | solution.py:130
  35.3 10.1 %collective-permute-start.15 = (bf16[224,512]{1,0:T(8,128)(2,1)}, bf16[224,512]{1,0:T(8,128)(2,1)S(1)}, u32[]{:S(2)}, u32[]{:S(2)}) collective-permute-start(bf16[224,512]{1,0:T(8,128)(2,1)} %collective-permute-done.11.refs_1_), channel_id=1, source_target_pairs={{4,0},{8,4},{12,8},{14,12},{10,14},{6,10},{2,6},{0,2},{5,1},{9,5},... | collective-permute-start | bytes 688136 | tf_op jit(solution)/shard_map/ppermute | solution.py:136
  35.3 10.1 %collective-permute-start.14 = (bf16[288,512]{1,0:T(8,128)(2,1)S(1)}, bf16[288,512]{1,0:T(8,128)(2,1)S(1)}, u32[]{:S(2)}, u32[]{:S(2)}) collective-permute-start(bf16[288,512]{1,0:T(8,128)(2,1)S(1)} %collective-permute-done.10.refs_0_), channel_id=1, source_target_pairs={{0,4},{4,8},{8,12},{12,14},{14,10},{10,6},{6,2},{2,0},{1,5},{5,9},... | collective-permute-start | bytes 884744 | tf_op jit(solution)/shard_map/ppermute | solution.py:135

commit v7 on v6

--- a/solution.py
+++ b/solution.py
@@ -109,7 +109,7 @@
     column = lax.axis_index("grid")
     half = (size * 9 // 16) // 16 * 16
 
-    order = list(range(0, grid_size, 2)) + list(range(1, grid_size, 2))[::-1]
+    order = [0] + list(range(1, grid_size, 2)) + list(range(2, grid_size, 2))[::-1]
     onward = [(order[i], order[(i + 1) % grid_size]) for i in range(grid_size)]
     backward = [(b, a) for a, b in onward]
     position_of = [order.index(g) for g in range(grid_size)]

time: 45.7 us -> 46.2 us (1.011); the launches traced: 45.5 us -> 46.5 us
  Pallas kernels: 3.76 us -> 4.87 us
    pallas_call x1, Pallas kernels: 0.06 us -> 1.18 us  [gather_columns(): pl.pallas_call(late_kernel, out_shape=result, in_specs=[vmem] * (3 + len(...]
    ppermute x6, waiting for transfers between devices: 9.05 us -> 8.33 us  [gather_columns(): left[1 - h] = lax.ppermute(left[1 - h], 'grid', backward)]
    ppermute x6, starting transfers between devices: 12.9 us -> 12.2 us  [gather_columns(): right[h] = lax.ppermute(right[h], 'grid', onward)]
    pallas_call x1, Pallas kernels: 2.49 us -> 1.89 us  [gather_columns(): pl.pallas_call(functools.partial(middle_kernel, placed(far), steps + 1),...]
    ppermute x1, waiting for transfers between devices: 1.37 us -> 1.97 us  [gather_columns(): last[steps + 1, 1] = lax.ppermute(left[1], 'grid', backward)]
    pallas_call x1, Pallas kernels: 1.21 us -> 1.79 us  [gather_columns(): pl.pallas_call(functools.partial(early_kernel, placed(near)), out_shape=w...]
    ppermute x6, starting transfers between devices: 0.89 us -> 1.41 us  [gather_columns(): left[1 - h] = lax.ppermute(left[1 - h], 'grid', backward)]
where the time goes in v7:
time: 46.2 us; the launch traced here: 46.5 us
  starting transfers between devices  16.1 us (35%)
  waiting for transfers between devices  12.7 us (27%)
  local copies, waits for them, and re-layouts  7.24 us (16%)
  Pallas kernels  4.87 us (11%)
  other arithmetic  3.54 us (8%)
  between operations  2.04 us (4%)
    ppermute x6, starting transfers between devices, gather_columns(): right[h] = lax.ppermute(right[h], 'grid', onward)  12.2 us
    ppermute x6, waiting for transfers between devices, gather_columns(): left[1 - h] = lax.ppermute(left[1 - h], 'grid', backward)  8.33 us
    concatenate x1, other arithmetic, gather_columns(): jnp.concatenate([inner_tiles, swapped], axis=0).reshape(-1, size, size)  2.09 us
    ppermute x1, starting transfers between devices, gather_columns(): last[steps + 1, 0] = lax.ppermute(right[0], 'grid', onward)  1.97 us
    ppermute x1, waiting for transfers between devices, gather_columns(): last[steps + 1, 1] = lax.ppermute(left[1], 'grid', backward)  1.97 us
    pallas_call x1, Pallas kernels, gather_columns(): pl.pallas_call(functools.partial(middle_kernel, placed(far), steps + 1),...  1.89 us
    pallas_call x1, Pallas kernels, gather_columns(): pl.pallas_call(functools.partial(early_kernel, placed(near)), out_shape=w...  1.79 us
    ppermute x6, starting transfers between devices, gather_columns(): left[1 - h] = lax.ppermute(left[1 - h], 'grid', backward)  1.41 us
  transfers between devices with their start and end apart: 16, of which 8 were waited for; matrix products, arithmetic and copies ran while one was open for 22% of the time, Pallas kernels for 8%

profile of v7, /device:TPU:0, one launch (start us, length us, event | category | flops | bytes accessed | tf_op | source)
XLA Modules:
  0.0 46.5 jit_solution(16519915550244475319)
XLA Ops:
  0.0 0.5 collective-permute-start.2
  0.5 0.8 %copy-done = bf16[1024,512]{1,0:T(8,128)(2,1)S(1)} copy-done((bf16[1024,512]{1,0:T(8,128)(2,1)S(1)}, bf16[1024,512]{1,0:T(8,128)(2,1)}, u32[]{:S(2)}) %copy-start) | copy-done | bytes 1048600
  1.2 3.0 %collective-permute-start.3 = (bf16[288,512]{1,0:T(8,128)(2,1)S(1)}, bf16[288,512]{1,0:T(8,128)(2,1)S(1)}, u32[]{:S(2)}, u32[]{:S(2)}) collective-permute-start(bf16[288,512]{1,0:T(8,128)(2,1)S(1)} %constant_dynamic-slice_fusion.1.refs_0_), channel_id=1, source_target_pairs={{0,2},{2,6},{6,10},{10,14},{14,12},{12,8},{8,4},{4,0},{1,3},{3,7},... | collective-permute-start | bytes 884744 | tf_op jit(solution)/shard_map/ppermute | solution.py:129
  4.4 1.9 %collective-permute-start = (bf16[224,512]{1,0:T(8,128)(2,1)S(1)}, bf16[224,512]{1,0:T(8,128)(2,1)S(1)}, u32[]{:S(2)}, u32[]{:S(2)}) collective-permute-start(bf16[224,512]{1,0:T(8,128)(2,1)S(1)} %constant_dynamic-slice_fusion.refs_1_), channel_id=1, source_target_pairs={{0,2},{2,6},{6,10},{10,14},{14,12},{12,8},{8,4},{4,0},{1,3},{3,7},... | collective-permute-start | bytes 688136 | tf_op jit(solution)/shard_map/ppermute | solution.py:129
  6.5 1.2 %dynamic_slice.17 = s32[1]{0:T(128)} dynamic-slice(s32[8]{0:T(128)} %constant.68.clone, s32[]{:T(128)S(6)} %select_n.115), dynamic_slice_sizes={1} | dynamic-slice | bytes 12 | tf_op jit(solution)/shard_map/dynamic_slice | solution.py:145
  7.7 0.7 %fusion.5 = s32[8]{0:T(128)S(1)} fusion(s32[]{:T(128)} %bitcast), kind=kLoop, calls=%fused_computation.32 | loop fusion | flops 120 | bytes 36 | tf_op jit(solution)/shard_map/select_n | solution.py:146
  8.4 1.3 %gather_fusion = s32[8]{0:T(128)S(1)} fusion(s32[8]{0:T(128)} %constant.69.clone, s32[1024]{0:T(1024)S(1)} %pad_clamp_fusion.3), kind=kCustom, calls=%fused_computation | custom fusion | bytes 96 | tf_op jit(solution)/shard_map/gather | solution.py:146
  9.7 1.3 %gather_fusion.1 = s32[8]{0:T(128)S(1)} fusion(s32[8]{0:T(128)} %param.11, s32[1024]{0:T(1024)S(1)} %pad_clamp_fusion.2), kind=kCustom, calls=%fused_computation.1 | custom fusion | bytes 96 | tf_op jit(solution)/shard_map/gather | solution.py:149
  11.0 1.9 %collective-permute-done.4.refs_3_ = bf16[224,512]{1,0:T(8,128)(2,1)S(1)} collective-permute-done((bf16[224,512]{1,0:T(8,128)(2,1)S(1)}, bf16[224,512]{1,0:T(8,128)(2,1)S(1)}, u32[]{:S(2)}, u32[]{:S(2)}) %collective-permute-start.4) | collective-permute-done | bytes 229408 | tf_op jit(solution)/shard_map/ppermute | solution.py:130
  13.0 1.8 %collective-permute-start.6 = (bf16[288,512]{1,0:T(8,128)(2,1)S(1)}, bf16[288,512]{1,0:T(8,128)(2,1)S(1)}, u32[]{:S(2)}, u32[]{:S(2)}) collective-permute-start(bf16[288,512]{1,0:T(8,128)(2,1)S(1)} %collective-permute-done.3.refs_2_), channel_id=1, source_target_pairs={{0,2},{2,6},{6,10},{10,14},{14,12},{12,8},{8,4},{4,0},{1,3},{3,7},... | collective-permute-start | bytes 884744 | tf_op jit(solution)/shard_map/ppermute | solution.py:129
  14.9 0.7 %fusion.2 = s32[8]{0:T(128)S(1)} fusion(s32[2,8]{1,0:T(2,128)} %param.9, s32[]{:T(128)S(6)} %select_n.122), kind=kLoop, calls=%fused_computation.29 | loop fusion | bytes 68 | tf_op jit(solution)/shard_map/jit(dynamic_index_in_dim)/squeeze | solution.py:153
  15.6 0.6 %gather_fusion.2 = s32[8]{0:T(128)S(1)} fusion(s32[8]{0:T(128)S(1)} %fusion.2, s32[1024]{0:T(1024)S(1)} %get-tuple-element.24), kind=kCustom, calls=%fused_computation.2 | custom fusion | bytes 96 | tf_op jit(solution)/shard_map/gather | solution.py:154
  16.2 0.8 %collective-permute-done.refs_4_ = bf16[224,512]{1,0:T(8,128)(2,1)S(1)} collective-permute-done((bf16[224,512]{1,0:T(8,128)(2,1)S(1)}, bf16[224,512]{1,0:T(8,128)(2,1)S(1)}, u32[]{:S(2)}, u32[]{:S(2)}) %collective-permute-start) | collective-permute-done | bytes 229408 | tf_op jit(solution)/shard_map/ppermute | solution.py:129
  17.1 1.3 %collective-permute-done.1 = s32[3,1]{0,1:T(1,128)S(1)} collective-permute-done((s32[3,1]{0,1:T(1,128)}, s32[3,1]{0,1:T(1,128)S(1)}, u32[]{:S(2)}, u32[]{:S(2)}) %collective-permute-start.1) | collective-permute-done | bytes 44 | tf_op jit(solution)/shard_map/ppermute | solution.py:142
  18.3 2.0 %collective-permute-start.8 = (bf16[224,512]{1,0:T(8,128)(2,1)S(1)}, bf16[224,512]{1,0:T(8,128)(2,1)}, u32[]{:S(2)}, u32[]{:S(2)}) collective-permute-start(bf16[224,512]{1,0:T(8,128)(2,1)S(1)} %collective-permute-done.refs_4_), channel_id=1, source_target_pairs={{0,2},{2,6},{6,10},{10,14},{14,12},{12,8},{8,4},{4,0},{1,3},{3,7},... | collective-permute-start | bytes 688136 | tf_op jit(solution)/shard_map/ppermute | solution.py:129
  20.4 2.3 %collective-permute-done.7.refs_7_ = bf16[224,512]{1,0:T(8,128)(2,1)} collective-permute-done((bf16[224,512]{1,0:T(8,128)(2,1)S(1)}, bf16[224,512]{1,0:T(8,128)(2,1)}, u32[]{:S(2)}, u32[]{:S(2)}) %collective-permute-start.7) | collective-permute-done | bytes 229408 | tf_op jit(solution)/shard_map/ppermute | solution.py:130
  22.7 0.4 collective-permute-start.11
  23.1 0.3 collective-permute-done.6.refs_6_
  23.4 1.9 %collective-permute-start.10 = (bf16[288,512]{1,0:T(8,128)(2,1)S(1)}, bf16[288,512]{1,0:T(8,128)(2,1)S(1)}, u32[]{:S(2)}, u32[]{:S(2)}) collective-permute-start(bf16[288,512]{1,0:T(8,128)(2,1)S(1)} %collective-permute-done.6.refs_6_), channel_id=1, source_target_pairs={{0,2},{2,6},{6,10},{10,14},{14,12},{12,8},{8,4},{4,0},{1,3},{3,7},... | collective-permute-start | bytes 884744 | tf_op jit(solution)/shard_map/ppermute | solution.py:129
  25.3 0.7 %add_bitcast_fusion = s32[6]{0:T(128)S(1)} fusion(s32[3,1]{0,1:T(1,128)S(1)} %collective-permute-done.1, s32[3,1]{0,1:T(1,128)} %param.10), kind=kLoop, calls=%fused_computation.36 | loop fusion | flops 6 | bytes 48 | tf_op jit(solution)/shard_map/squeeze | solution.py:141
  26.0 0.6 %gather_fusion.3 = s32[8]{0:T(128)S(1)} fusion(s32[6]{0:T(128)S(1)} %add_bitcast_fusion, s32[1024]{0:T(1024)S(1)} %get-tuple-element.23), kind=kCustom, calls=%fused_computation.3 | custom fusion | bytes 96 | tf_op jit(solution)/shard_map/gather | solution.py:160
  26.7 0.6 %slice.3 = s32[1]{0:T(128)} slice(s32[8]{0:T(128)S(1)} %get-tuple-element.20.slots), slice={[4:5]} | slice | bytes 8 | tf_op jit(solution)/shard_map/slice | solution.py:198
  29.2 1.6 %collective-permute-start.12 = (bf16[224,512]{1,0:T(8,128)(2,1)}, bf16[224,512]{1,0:T(8,128)(2,1)S(1)}, u32[]{:S(2)}, u32[]{:S(2)}) collective-permute-start(bf16[224,512]{1,0:T(8,128)(2,1)} %collective-permute-done.8.refs_8_), channel_id=1, source_target_pairs={{0,2},{2,6},{6,10},{10,14},{14,12},{12,8},{8,4},{4,0},{1,3},{3,7},... | collective-permute-start | bytes 688136 | tf_op jit(solution)/shard_map/ppermute | solution.py:129
  30.8 0.5 collective-permute-start.13
  31.3 3.9 %collective-permute-done.11.refs_1_ = bf16[224,512]{1,0:T(8,128)(2,1)} collective-permute-done((bf16[224,512]{1,0:T(8,128)(2,1)}, bf16[224,512]{1,0:T(8,128)(2,1)}, u32[]{:S(2)}, u32[]{:S(2)}) %collective-permute-start.11) | collective-permute-done | bytes 229408 | tf_op jit(solution)/shard_map/ppermute | solution.py:130
  35.3 2.0 %collective-permute-start.14 = (bf16[288,512]{1,0:T(8,128)(2,1)S(1)}, bf16[288,512]{1,0:T(8,128)(2,1)S(1)}, u32[]{:S(2)}, u32[]{:S(2)}) collective-permute-start(bf16[288,512]{1,0:T(8,128)(2,1)S(1)} %collective-permute-done.10.refs_0_), channel_id=1, source_target_pairs={{0,2},{2,6},{6,10},{10,14},{14,12},{12,8},{8,4},{4,0},{1,3},{3,7},... | collective-permute-start | bytes 884744 | tf_op jit(solution)/shard_map/ppermute | solution.py:135
  37.2 2.1 %pad_maximum_fusion = bf16[3072,512]{1,0:T(8,128)(2,1)S(1)} fusion(bf16[1536,512]{1,0:T(8,128)(2,1)} %collective-permute-done.2, bf16[1536,512]{1,0:T(8,128)(2,1)} %param.8), kind=kLoop, calls=%fused_computation.4 | loop fusion | flops 6291456 | bytes 6291456 | tf_op jit(solution)/shard_map/concatenate | solution.py:139
  39.3 1.8 %shard_map.73.before = f32[512,512]{1,0:T(8,128)S(1)} custom-call(s32[8]{0:T(128)S(1)} %get-tuple-element.20.slots, s32[8]{0:T(128)S(1)} %get-tuple-element.19.flags, bf16[6,512,512]{2,1,0:T(8,128)(2,1)S(1)} %bitcast.30, bf16[288,512]{1,0:T(8,128)(2,1)S(1)} %constant_dynamic-slice_fusion.1.refs_0_, bf16[224,512]{1,0:T(8,128)(2,1)S(1)} %constant_dynamic-slice_fusion.refs_1_, ...), custom_call_target="tpu_custom_call" | custom-call | flops 4026531840 | bytes 9437184 | tf_op jit(solution)/shard_map/pallas_call | solution.py:181
  41.2 0.2 collective-permute-done.13.refs_3_
  41.4 1.9 %shard_map.74 = (f32[512,512]{1,0:T(8,128)S(1)}, s32[8,128]{1,0:T(8,128)S(1)}, bf16[512,512]{1,0:T(8,128)(2,1)}) custom-call(s32[8]{0:T(128)S(1)} %get-tuple-element.20.slots, s32[8]{0:T(128)S(1)} %get-tuple-element.19.flags, bf16[6,512,512]{2,1,0:T(8,128)(2,1)S(1)} %bitcast.32, f32[512,512]{1,0:T(8,128)S(1)} %shard_map.73.before, ...), custom_call_target="tpu_custom_call" | custom-call | flops 1610612736 | bytes 6291456 | tf_op jit(solution)/shard_map/pallas_call | solution.py:189
  43.3 2.0 %collective-permute-done.15.refs_1_ = bf16[224,512]{1,0:T(8,128)(2,1)S(1)} collective-permute-done((bf16[224,512]{1,0:T(8,128)(2,1)}, bf16[224,512]{1,0:T(8,128)(2,1)S(1)}, u32[]{:S(2)}, u32[]{:S(2)}) %collective-permute-start.15) | collective-permute-done | bytes 229408 | tf_op jit(solution)/shard_map/ppermute | solution.py:136
  45.3 1.2 %shard_map.75 = bf16[512,512]{1,0:T(8,128)(2,1)} custom-call(s32[8,128]{1,0:T(8,128)S(1)} %get-tuple-element.16.flag, bf16[512,512]{1,0:T(8,128)(2,1)S(1)} %dynamic-slice_bitcast_fusion.tile, f32[512,512]{1,0:T(8,128)S(1)} %get-tuple-element.17.before, bf16[288,512]{1,0:T(8,128)(2,1)S(1)} %collective-permute-done.14.refs_0_, ...), custom_call_target="tpu_custom_call", output_to_operand_aliasing={{}: (5, {})} | custom-call | tf_op jit(solution)/shard_map/pallas_call | solution.py:199
  (24 shorter events, 0.8 us)
Async XLA Ops:
  0.0 1.2 %copy-start = (bf16[1024,512]{1,0:T(8,128)(2,1)S(1)}, bf16[1024,512]{1,0:T(8,128)(2,1)}, u32[]{:S(2)}) copy-start(bf16[1024,512]{1,0:T(8,128)(2,1)} %param.7) | copy-start | bytes 3145732
  0.0 37.2 %collective-permute-start.2 = (bf16[1536,512]{1,0:T(8,128)(2,1)}, bf16[1536,512]{1,0:T(8,128)(2,1)}, u32[]{:S(2)}, u32[]{:S(2)}) collective-permute-start(bf16[1536,512]{1,0:T(8,128)(2,1)} %param.8), channel_id=1, source_target_pairs={{0,1},{1,0},{2,3},{3,2},{4,5},{5,4},{6,7},{7,6},{8,9},{9,8},{10,11... | collective-permute-start | bytes 4718600 | tf_op jit(solution)/shard_map/ppermute | solution.py:138
  1.2 11.8 %collective-permute-start.3 = (bf16[288,512]{1,0:T(8,128)(2,1)S(1)}, bf16[288,512]{1,0:T(8,128)(2,1)S(1)}, u32[]{:S(2)}, u32[]{:S(2)}) collective-permute-start(bf16[288,512]{1,0:T(8,128)(2,1)S(1)} %constant_dynamic-slice_fusion.1.refs_0_), channel_id=1, source_target_pairs={{0,2},{2,6},{6,10},{10,14},{14,12},{12,8},{8,4},{4,0},{1,3},{3,7},... | collective-permute-start | bytes 884744 | tf_op jit(solution)/shard_map/ppermute | solution.py:129
  4.3 8.6 %collective-permute-start.4 = (bf16[224,512]{1,0:T(8,128)(2,1)S(1)}, bf16[224,512]{1,0:T(8,128)(2,1)S(1)}, u32[]{:S(2)}, u32[]{:S(2)}) collective-permute-start(bf16[224,512]{1,0:T(8,128)(2,1)S(1)} %constant_dynamic-slice_fusion.refs_1_), channel_id=1, source_target_pairs={{2,0},{6,2},{10,6},{14,10},{12,14},{8,12},{4,8},{0,4},{3,1},{7,3},... | collective-permute-start | bytes 688136 | tf_op jit(solution)/shard_map/ppermute | solution.py:130
  4.4 12.7 %collective-permute-start = (bf16[224,512]{1,0:T(8,128)(2,1)S(1)}, bf16[224,512]{1,0:T(8,128)(2,1)S(1)}, u32[]{:S(2)}, u32[]{:S(2)}) collective-permute-start(bf16[224,512]{1,0:T(8,128)(2,1)S(1)} %constant_dynamic-slice_fusion.refs_1_), channel_id=1, source_target_pairs={{0,2},{2,6},{6,10},{10,14},{14,12},{12,8},{8,4},{4,0},{1,3},{3,7},... | collective-permute-start | bytes 688136 | tf_op jit(solution)/shard_map/ppermute | solution.py:129
  6.3 14.0 %collective-permute-start.5 = (bf16[288,512]{1,0:T(8,128)(2,1)S(1)}, bf16[288,512]{1,0:T(8,128)(2,1)S(1)}, u32[]{:S(2)}, u32[]{:S(2)}) collective-permute-start(bf16[288,512]{1,0:T(8,128)(2,1)S(1)} %constant_dynamic-slice_fusion.1.refs_0_), channel_id=1, source_target_pairs={{2,0},{6,2},{10,6},{14,10},{12,14},{8,12},{4,8},{0,4},{3,1},{7,3},... | collective-permute-start | bytes 884744 | tf_op jit(solution)/shard_map/ppermute | solution.py:130
  12.8 9.9 %collective-permute-start.7 = (bf16[224,512]{1,0:T(8,128)(2,1)S(1)}, bf16[224,512]{1,0:T(8,128)(2,1)}, u32[]{:S(2)}, u32[]{:S(2)}) collective-permute-start(bf16[224,512]{1,0:T(8,128)(2,1)S(1)} %collective-permute-done.4.refs_3_), channel_id=1, source_target_pairs={{2,0},{6,2},{10,6},{14,10},{12,14},{8,12},{4,8},{0,4},{3,1},{7,3},... | collective-permute-start | bytes 688136 | tf_op jit(solution)/shard_map/ppermute | solution.py:130
  13.0 10.4 %collective-permute-start.6 = (bf16[288,512]{1,0:T(8,128)(2,1)S(1)}, bf16[288,512]{1,0:T(8,128)(2,1)S(1)}, u32[]{:S(2)}, u32[]{:S(2)}) collective-permute-start(bf16[288,512]{1,0:T(8,128)(2,1)S(1)} %collective-permute-done.3.refs_2_), channel_id=1, source_target_pairs={{0,2},{2,6},{6,10},{10,14},{14,12},{12,8},{8,4},{4,0},{1,3},{3,7},... | collective-permute-start | bytes 884744 | tf_op jit(solution)/shard_map/ppermute | solution.py:129
  17.1 1.3 %collective-permute-start.1 = (s32[3,1]{0,1:T(1,128)}, s32[3,1]{0,1:T(1,128)S(1)}, u32[]{:S(2)}, u32[]{:S(2)}) collective-permute-start(s32[3,1]{0,1:T(1,128)} %param.10), channel_id=1, source_target_pairs={{0,1},{1,0},{2,3},{3,2},{4,5},{5,4},{6,7},{7,6},{8,9},{9,8},{10,11... | collective-permute-start | bytes 44 | tf_op jit(solution)/shard_map/ppermute | solution.py:142
  18.3 10.9 %collective-permute-start.8 = (bf16[224,512]{1,0:T(8,128)(2,1)S(1)}, bf16[224,512]{1,0:T(8,128)(2,1)}, u32[]{:S(2)}, u32[]{:S(2)}) collective-permute-start(bf16[224,512]{1,0:T(8,128)(2,1)S(1)} %collective-permute-done.refs_4_), channel_id=1, source_target_pairs={{0,2},{2,6},{6,10},{10,14},{14,12},{12,8},{8,4},{4,0},{1,3},{3,7},... | collective-permute-start | bytes 688136 | tf_op jit(solution)/shard_map/ppermute | solution.py:129
  20.3 10.5 %collective-permute-start.9 = (bf16[288,512]{1,0:T(8,128)(2,1)S(1)}, bf16[288,512]{1,0:T(8,128)(2,1)S(1)}, u32[]{:S(2)}, u32[]{:S(2)}) collective-permute-start(bf16[288,512]{1,0:T(8,128)(2,1)S(1)} %collective-permute-done.5.refs_5_), channel_id=1, source_target_pairs={{2,0},{6,2},{10,6},{14,10},{12,14},{8,12},{4,8},{0,4},{3,1},{7,3},... | collective-permute-start | bytes 884744 | tf_op jit(solution)/shard_map/ppermute | solution.py:130
  22.7 12.5 %collective-permute-start.11 = (bf16[224,512]{1,0:T(8,128)(2,1)}, bf16[224,512]{1,0:T(8,128)(2,1)}, u32[]{:S(2)}, u32[]{:S(2)}) collective-permute-start(bf16[224,512]{1,0:T(8,128)(2,1)} %collective-permute-done.7.refs_7_), channel_id=1, source_target_pairs={{2,0},{6,2},{10,6},{14,10},{12,14},{8,12},{4,8},{0,4},{3,1},{7,3},... | collective-permute-start | bytes 688136 | tf_op jit(solution)/shard_map/ppermute | solution.py:130
  23.4 11.9 %collective-permute-start.10 = (bf16[288,512]{1,0:T(8,128)(2,1)S(1)}, bf16[288,512]{1,0:T(8,128)(2,1)S(1)}, u32[]{:S(2)}, u32[]{:S(2)}) collective-permute-start(bf16[288,512]{1,0:T(8,128)(2,1)S(1)} %collective-permute-done.6.refs_6_), channel_id=1, source_target_pairs={{0,2},{2,6},{6,10},{10,14},{14,12},{12,8},{8,4},{4,0},{1,3},{3,7},... | collective-permute-start | bytes 884744 | tf_op jit(solution)/shard_map/ppermute | solution.py:129
  29.2 12.0 %collective-permute-start.12 = (bf16[224,512]{1,0:T(8,128)(2,1)}, bf16[224,512]{1,0:T(8,128)(2,1)S(1)}, u32[]{:S(2)}, u32[]{:S(2)}) collective-permute-start(bf16[224,512]{1,0:T(8,128)(2,1)} %collective-permute-done.8.refs_8_), channel_id=1, source_target_pairs={{0,2},{2,6},{6,10},{10,14},{14,12},{12,8},{8,4},{4,0},{1,3},{3,7},... | collective-permute-start | bytes 688136 | tf_op jit(solution)/shard_map/ppermute | solution.py:129
  30.8 10.6 %collective-permute-start.13 = (bf16[288,512]{1,0:T(8,128)(2,1)S(1)}, bf16[288,512]{1,0:T(8,128)(2,1)S(1)}, u32[]{:S(2)}, u32[]{:S(2)}) collective-permute-start(bf16[288,512]{1,0:T(8,128)(2,1)S(1)} %collective-permute-done.9.refs_9_), channel_id=1, source_target_pairs={{2,0},{6,2},{10,6},{14,10},{12,14},{8,12},{4,8},{0,4},{3,1},{7,3},... | collective-permute-start | bytes 884744 | tf_op jit(solution)/shard_map/ppermute | solution.py:130
  35.2 10.1 %collective-permute-start.15 = (bf16[224,512]{1,0:T(8,128)(2,1)}, bf16[224,512]{1,0:T(8,128)(2,1)S(1)}, u32[]{:S(2)}, u32[]{:S(2)}) collective-permute-start(bf16[224,512]{1,0:T(8,128)(2,1)} %collective-permute-done.11.refs_1_), channel_id=1, source_target_pairs={{2,0},{6,2},{10,6},{14,10},{12,14},{8,12},{4,8},{0,4},{3,1},{7,3},... | collective-permute-start | bytes 688136 | tf_op jit(solution)/shard_map/ppermute | solution.py:136
  35.3 10.0 %collective-permute-start.14 = (bf16[288,512]{1,0:T(8,128)(2,1)S(1)}, bf16[288,512]{1,0:T(8,128)(2,1)S(1)}, u32[]{:S(2)}, u32[]{:S(2)}) collective-permute-start(bf16[288,512]{1,0:T(8,128)(2,1)S(1)} %collective-permute-done.10.refs_0_), channel_id=1, source_target_pairs={{0,2},{2,6},{6,10},{10,14},{14,12},{12,8},{8,4},{4,0},{1,3},{3,7},... | collective-permute-start | bytes 884744 | tf_op jit(solution)/shard_map/ppermute | solution.py:135

commit v8 on v7

--- a/solution.py
+++ b/solution.py
@@ -107,7 +107,7 @@
     halves = lax.axis_size("depth")
     depth_index = lax.axis_index("depth")
     column = lax.axis_index("grid")
-    half = (size * 9 // 16) // 16 * 16
+    half = (size * 19 // 32) // 16 * 16
 
     order = [0] + list(range(1, grid_size, 2)) + list(range(2, grid_size, 2))[::-1]
     onward = [(order[i], order[(i + 1) % grid_size]) for i in range(grid_size)]

time: 46.2 us -> 45.8 us (level); the launches traced: 46.5 us -> 45.5 us
  Pallas kernels: 4.87 us -> 3.84 us
    ppermute x6, waiting for transfers between devices: 1.14 us -> 5.96 us  [gather_columns(): right[h] = lax.ppermute(right[h], 'grid', onward)]
    ppermute x6, waiting for transfers between devices: 8.33 us -> 4.8 us  [gather_columns(): left[1 - h] = lax.ppermute(left[1 - h], 'grid', backward)]
    ppermute x1, waiting for transfers between devices: 1.97 us -> 0.76 us  [gather_columns(): last[steps + 1, 1] = lax.ppermute(left[1], 'grid', backward)]
    pallas_call x1, Pallas kernels: 1.18 us -> 0.06 us  [gather_columns(): pl.pallas_call(late_kernel, out_shape=result, in_specs=[vmem] * (3 + len(...]
    pallas_call x1, Pallas kernels: 1.89 us -> 2.49 us  [gather_columns(): pl.pallas_call(functools.partial(middle_kernel, placed(far), steps + 1),...]
    ppermute x6, starting transfers between devices: 1.41 us -> 0.84 us  [gather_columns(): left[1 - h] = lax.ppermute(left[1 - h], 'grid', backward)]
    ppermute x6, starting transfers between devices: 12.2 us -> 12.7 us  [gather_columns(): right[h] = lax.ppermute(right[h], 'grid', onward)]
    pallas_call x1, Pallas kernels: 1.79 us -> 1.3 us  [gather_columns(): pl.pallas_call(functools.partial(early_kernel, placed(near)), out_shape=w...]
  transfers between devices with their start and end apart: 16 -> 16, of which waited for: 8 -> 7; matrix products, arithmetic and copies ran while one was open for 22% -> 22% of each run, Pallas kernels for 8% -> 8%
where the time goes in v8:
time: 45.8 us; the launch traced here: 45.5 us
  starting transfers between devices  16 us (35%)
  waiting for transfers between devices  12.8 us (28%)
  local copies, waits for them, and re-layouts  7.23 us (16%)
  Pallas kernels  3.84 us (8%)
  other arithmetic  3.54 us (8%)
  between operations  2.05 us (4%)
    ppermute x6, starting transfers between devices, gather_columns(): right[h] = lax.ppermute(right[h], 'grid', onward)  12.7 us
    ppermute x6, waiting for transfers between devices, gather_columns(): right[h] = lax.ppermute(right[h], 'grid', onward)  5.96 us
    ppermute x6, waiting for transfers between devices, gather_columns(): left[1 - h] = lax.ppermute(left[1 - h], 'grid', backward)  4.8 us
    pallas_call x1, Pallas kernels, gather_columns(): pl.pallas_call(functools.partial(middle_kernel, placed(far), steps + 1),...  2.49 us
    concatenate x1, other arithmetic, gather_columns(): jnp.concatenate([inner_tiles, swapped], axis=0).reshape(-1, size, size)  2.09 us
    ppermute x1, starting transfers between devices, gather_columns(): last[steps + 1, 0] = lax.ppermute(right[0], 'grid', onward)  1.9 us
    gather x1, local copies, waits for them, and re-layouts, gather_columns(): jnp.asarray(order, jnp.int32)  1.3 us
    gather x1, local copies, waits for them, and re-layouts, gather_columns(): true_column = held_col[sources]  1.3 us
  transfers between devices with their start and end apart: 16, of which 7 were waited for; matrix products, arithmetic and copies ran while one was open for 22% of the time, Pallas kernels for 8%

profile of v8, /device:TPU:0, one launch (start us, length us, event | category | flops | bytes accessed | tf_op | source)
XLA Modules:
  0.0 45.5 jit_solution(11273575351958148395)
XLA Ops:
  0.0 0.5 collective-permute-start.2
  0.5 0.8 %copy-done = bf16[1024,512]{1,0:T(8,128)(2,1)S(1)} copy-done((bf16[1024,512]{1,0:T(8,128)(2,1)S(1)}, bf16[1024,512]{1,0:T(8,128)(2,1)}, u32[]{:S(2)}) %copy-start) | copy-done | bytes 1048600
  1.3 3.0 %collective-permute-start.3 = (bf16[304,512]{1,0:T(8,128)(2,1)S(1)}, bf16[304,512]{1,0:T(8,128)(2,1)S(1)}, u32[]{:S(2)}, u32[]{:S(2)}) collective-permute-start(bf16[304,512]{1,0:T(8,128)(2,1)S(1)} %constant_dynamic-slice_fusion.1.refs_0_), channel_id=1, source_target_pairs={{0,2},{2,6},{6,10},{10,14},{14,12},{12,8},{8,4},{4,0},{1,3},{3,7},... | collective-permute-start | bytes 933896 | tf_op jit(solution)/shard_map/ppermute | solution.py:129
  4.3 0.2 collective-permute-start.4
  4.4 1.9 %collective-permute-start = (bf16[208,512]{1,0:T(8,128)(2,1)S(1)}, bf16[208,512]{1,0:T(8,128)(2,1)}, u32[]{:S(2)}, u32[]{:S(2)}) collective-permute-start(bf16[208,512]{1,0:T(8,128)(2,1)S(1)} %constant_dynamic-slice_fusion.refs_1_), channel_id=1, source_target_pairs={{0,2},{2,6},{6,10},{10,14},{14,12},{12,8},{8,4},{4,0},{1,3},{3,7},... | collective-permute-start | bytes 638984 | tf_op jit(solution)/shard_map/ppermute | solution.py:129
  6.5 1.2 %dynamic_slice.17 = s32[1]{0:T(128)} dynamic-slice(s32[8]{0:T(128)} %constant.68.clone, s32[]{:T(128)S(6)} %select_n.115), dynamic_slice_sizes={1} | dynamic-slice | bytes 12 | tf_op jit(solution)/shard_map/dynamic_slice | solution.py:145
  7.7 0.7 %fusion.5 = s32[8]{0:T(128)S(1)} fusion(s32[]{:T(128)} %bitcast), kind=kLoop, calls=%fused_computation.32 | loop fusion | flops 120 | bytes 36 | tf_op jit(solution)/shard_map/select_n | solution.py:146
  8.4 1.3 %gather_fusion = s32[8]{0:T(128)S(1)} fusion(s32[8]{0:T(128)} %constant.69.clone, s32[1024]{0:T(1024)S(1)} %pad_clamp_fusion.3), kind=kCustom, calls=%fused_computation | custom fusion | bytes 96 | tf_op jit(solution)/shard_map/gather | solution.py:146
  9.7 1.3 %gather_fusion.1 = s32[8]{0:T(128)S(1)} fusion(s32[8]{0:T(128)} %param.11, s32[1024]{0:T(1024)S(1)} %pad_clamp_fusion.2), kind=kCustom, calls=%fused_computation.1 | custom fusion | bytes 96 | tf_op jit(solution)/shard_map/gather | solution.py:149
  11.0 1.5 %collective-permute-done.3.refs_2_ = bf16[304,512]{1,0:T(8,128)(2,1)S(1)} collective-permute-done((bf16[304,512]{1,0:T(8,128)(2,1)S(1)}, bf16[304,512]{1,0:T(8,128)(2,1)S(1)}, u32[]{:S(2)}, u32[]{:S(2)}) %collective-permute-start.3) | collective-permute-done | bytes 311328 | tf_op jit(solution)/shard_map/ppermute | solution.py:129
  12.5 2.0 %collective-permute-start.6 = (bf16[304,512]{1,0:T(8,128)(2,1)S(1)}, bf16[304,512]{1,0:T(8,128)(2,1)S(1)}, u32[]{:S(2)}, u32[]{:S(2)}) collective-permute-start(bf16[304,512]{1,0:T(8,128)(2,1)S(1)} %collective-permute-done.3.refs_2_), channel_id=1, source_target_pairs={{0,2},{2,6},{6,10},{10,14},{14,12},{12,8},{8,4},{4,0},{1,3},{3,7},... | collective-permute-start | bytes 933896 | tf_op jit(solution)/shard_map/ppermute | solution.py:129
  14.5 0.1 collective-permute-start.7
  14.7 0.7 %fusion.2 = s32[8]{0:T(128)S(1)} fusion(s32[2,8]{1,0:T(2,128)} %param.9, s32[]{:T(128)S(6)} %select_n.122), kind=kLoop, calls=%fused_computation.29 | loop fusion | bytes 68 | tf_op jit(solution)/shard_map/jit(dynamic_index_in_dim)/squeeze | solution.py:153
  15.4 0.6 %gather_fusion.2 = s32[8]{0:T(128)S(1)} fusion(s32[8]{0:T(128)S(1)} %fusion.2, s32[1024]{0:T(1024)S(1)} %get-tuple-element.24), kind=kCustom, calls=%fused_computation.2 | custom fusion | bytes 96 | tf_op jit(solution)/shard_map/gather | solution.py:154
  16.0 1.2 %collective-permute-done.refs_4_ = bf16[208,512]{1,0:T(8,128)(2,1)} collective-permute-done((bf16[208,512]{1,0:T(8,128)(2,1)S(1)}, bf16[208,512]{1,0:T(8,128)(2,1)}, u32[]{:S(2)}, u32[]{:S(2)}) %collective-permute-start) | collective-permute-done | bytes 213024 | tf_op jit(solution)/shard_map/ppermute | solution.py:129
  17.2 1.3 %collective-permute-done.1 = s32[3,1]{0,1:T(1,128)S(1)} collective-permute-done((s32[3,1]{0,1:T(1,128)}, s32[3,1]{0,1:T(1,128)S(1)}, u32[]{:S(2)}, u32[]{:S(2)}) %collective-permute-start.1) | collective-permute-done | bytes 44 | tf_op jit(solution)/shard_map/ppermute | solution.py:142
  18.4 2.0 %collective-permute-start.8 = (bf16[208,512]{1,0:T(8,128)(2,1)}, bf16[208,512]{1,0:T(8,128)(2,1)}, u32[]{:S(2)}, u32[]{:S(2)}) collective-permute-start(bf16[208,512]{1,0:T(8,128)(2,1)} %collective-permute-done.refs_4_), channel_id=1, source_target_pairs={{0,2},{2,6},{6,10},{10,14},{14,12},{12,8},{8,4},{4,0},{1,3},{3,7},... | collective-permute-start | bytes 638984 | tf_op jit(solution)/shard_map/ppermute | solution.py:129
  20.5 3.2 %collective-permute-done.6.refs_6_ = bf16[304,512]{1,0:T(8,128)(2,1)S(1)} collective-permute-done((bf16[304,512]{1,0:T(8,128)(2,1)S(1)}, bf16[304,512]{1,0:T(8,128)(2,1)S(1)}, u32[]{:S(2)}, u32[]{:S(2)}) %collective-permute-start.6) | collective-permute-done | bytes 311328 | tf_op jit(solution)/shard_map/ppermute | solution.py:129
  23.8 1.9 %collective-permute-start.10 = (bf16[304,512]{1,0:T(8,128)(2,1)S(1)}, bf16[304,512]{1,0:T(8,128)(2,1)S(1)}, u32[]{:S(2)}, u32[]{:S(2)}) collective-permute-start(bf16[304,512]{1,0:T(8,128)(2,1)S(1)} %collective-permute-done.6.refs_6_), channel_id=1, source_target_pairs={{0,2},{2,6},{6,10},{10,14},{14,12},{12,8},{8,4},{4,0},{1,3},{3,7},... | collective-permute-start | bytes 933896 | tf_op jit(solution)/shard_map/ppermute | solution.py:129
  25.7 0.7 %add_bitcast_fusion = s32[6]{0:T(128)S(1)} fusion(s32[3,1]{0,1:T(1,128)S(1)} %collective-permute-done.1, s32[3,1]{0,1:T(1,128)} %param.10), kind=kLoop, calls=%fused_computation.36 | loop fusion | flops 6 | bytes 48 | tf_op jit(solution)/shard_map/squeeze | solution.py:141
  26.4 0.6 %gather_fusion.3 = s32[8]{0:T(128)S(1)} fusion(s32[6]{0:T(128)S(1)} %add_bitcast_fusion, s32[1024]{0:T(1024)S(1)} %get-tuple-element.23), kind=kCustom, calls=%fused_computation.3 | custom fusion | bytes 96 | tf_op jit(solution)/shard_map/gather | solution.py:160
  27.0 0.2 collective-permute-start.11
  27.2 0.6 %slice.3 = s32[1]{0:T(128)} slice(s32[8]{0:T(128)S(1)} %get-tuple-element.20.slots), slice={[4:5]} | slice | bytes 8 | tf_op jit(solution)/shard_map/slice | solution.py:198
  29.8 2.0 %collective-permute-start.12 = (bf16[208,512]{1,0:T(8,128)(2,1)}, bf16[208,512]{1,0:T(8,128)(2,1)S(1)}, u32[]{:S(2)}, u32[]{:S(2)}) collective-permute-start(bf16[208,512]{1,0:T(8,128)(2,1)} %collective-permute-done.8.refs_8_), channel_id=1, source_target_pairs={{0,2},{2,6},{6,10},{10,14},{14,12},{12,8},{8,4},{4,0},{1,3},{3,7},... | collective-permute-start | bytes 638984 | tf_op jit(solution)/shard_map/ppermute | solution.py:129
  31.7 0.2 collective-permute-start.13
  31.9 3.7 %collective-permute-done.11.refs_1_ = bf16[208,512]{1,0:T(8,128)(2,1)} collective-permute-done((bf16[208,512]{1,0:T(8,128)(2,1)}, bf16[208,512]{1,0:T(8,128)(2,1)}, u32[]{:S(2)}, u32[]{:S(2)}) %collective-permute-start.11) | collective-permute-done | bytes 213024 | tf_op jit(solution)/shard_map/ppermute | solution.py:130
  35.7 1.9 %collective-permute-start.14 = (bf16[304,512]{1,0:T(8,128)(2,1)S(1)}, bf16[304,512]{1,0:T(8,128)(2,1)S(1)}, u32[]{:S(2)}, u32[]{:S(2)}) collective-permute-start(bf16[304,512]{1,0:T(8,128)(2,1)S(1)} %collective-permute-done.10.refs_0_), channel_id=1, source_target_pairs={{0,2},{2,6},{6,10},{10,14},{14,12},{12,8},{8,4},{4,0},{1,3},{3,7},... | collective-permute-start | bytes 933896 | tf_op jit(solution)/shard_map/ppermute | solution.py:135
  37.6 2.1 %pad_maximum_fusion = bf16[3072,512]{1,0:T(8,128)(2,1)S(1)} fusion(bf16[1536,512]{1,0:T(8,128)(2,1)} %collective-permute-done.2, bf16[1536,512]{1,0:T(8,128)(2,1)} %param.8), kind=kLoop, calls=%fused_computation.4 | loop fusion | flops 6291456 | bytes 6291456 | tf_op jit(solution)/shard_map/concatenate | solution.py:139
  39.7 1.3 %shard_map.73.before = f32[512,512]{1,0:T(8,128)S(1)} custom-call(s32[8]{0:T(128)S(1)} %get-tuple-element.20.slots, s32[8]{0:T(128)S(1)} %get-tuple-element.19.flags, bf16[6,512,512]{2,1,0:T(8,128)(2,1)S(1)} %bitcast.30, bf16[304,512]{1,0:T(8,128)(2,1)S(1)} %constant_dynamic-slice_fusion.1.refs_0_, bf16[208,512]{1,0:T(8,128)(2,1)S(1)} %constant_dynamic-slice_fusion.refs_1_, ...), custom_call_target="tpu_custom_call" | custom-call | flops 4026531840 | bytes 9437184 | tf_op jit(solution)/shard_map/pallas_call | solution.py:181
  41.1 1.1 %collective-permute-done.13.refs_3_ = bf16[304,512]{1,0:T(8,128)(2,1)S(1)} collective-permute-done((bf16[304,512]{1,0:T(8,128)(2,1)S(1)}, bf16[304,512]{1,0:T(8,128)(2,1)S(1)}, u32[]{:S(2)}, u32[]{:S(2)}) %collective-permute-start.13) | collective-permute-done | bytes 311328 | tf_op jit(solution)/shard_map/ppermute | solution.py:130
  42.2 2.5 %shard_map.74 = (f32[512,512]{1,0:T(8,128)S(1)}, s32[8,128]{1,0:T(8,128)S(1)}, bf16[512,512]{1,0:T(8,128)(2,1)}) custom-call(s32[8]{0:T(128)S(1)} %get-tuple-element.20.slots, s32[8]{0:T(128)S(1)} %get-tuple-element.19.flags, bf16[6,512,512]{2,1,0:T(8,128)(2,1)S(1)} %bitcast.32, f32[512,512]{1,0:T(8,128)S(1)} %shard_map.73.before, ...), custom_call_target="tpu_custom_call" | custom-call | flops 1610612736 | bytes 6291456 | tf_op jit(solution)/shard_map/pallas_call | solution.py:189
  44.7 0.8 %collective-permute-done.15.refs_1_ = bf16[208,512]{1,0:T(8,128)(2,1)S(1)} collective-permute-done((bf16[208,512]{1,0:T(8,128)(2,1)}, bf16[208,512]{1,0:T(8,128)(2,1)S(1)}, u32[]{:S(2)}, u32[]{:S(2)}) %collective-permute-start.15) | collective-permute-done | bytes 213024 | tf_op jit(solution)/shard_map/ppermute | solution.py:136
  (24 shorter events, 0.6 us)
Async XLA Ops:
  0.0 1.2 %copy-start = (bf16[1024,512]{1,0:T(8,128)(2,1)S(1)}, bf16[1024,512]{1,0:T(8,128)(2,1)}, u32[]{:S(2)}) copy-start(bf16[1024,512]{1,0:T(8,128)(2,1)} %param.7) | copy-start | bytes 3145732
  0.0 37.6 %collective-permute-start.2 = (bf16[1536,512]{1,0:T(8,128)(2,1)}, bf16[1536,512]{1,0:T(8,128)(2,1)}, u32[]{:S(2)}, u32[]{:S(2)}) collective-permute-start(bf16[1536,512]{1,0:T(8,128)(2,1)} %param.8), channel_id=1, source_target_pairs={{0,1},{1,0},{2,3},{3,2},{4,5},{5,4},{6,7},{7,6},{8,9},{9,8},{10,11... | collective-permute-start | bytes 4718600 | tf_op jit(solution)/shard_map/ppermute | solution.py:138
  1.3 11.3 %collective-permute-start.3 = (bf16[304,512]{1,0:T(8,128)(2,1)S(1)}, bf16[304,512]{1,0:T(8,128)(2,1)S(1)}, u32[]{:S(2)}, u32[]{:S(2)}) collective-permute-start(bf16[304,512]{1,0:T(8,128)(2,1)S(1)} %constant_dynamic-slice_fusion.1.refs_0_), channel_id=1, source_target_pairs={{0,2},{2,6},{6,10},{10,14},{14,12},{12,8},{8,4},{4,0},{1,3},{3,7},... | collective-permute-start | bytes 933896 | tf_op jit(solution)/shard_map/ppermute | solution.py:129
  4.3 10.3 %collective-permute-start.4 = (bf16[208,512]{1,0:T(8,128)(2,1)S(1)}, bf16[208,512]{1,0:T(8,128)(2,1)S(1)}, u32[]{:S(2)}, u32[]{:S(2)}) collective-permute-start(bf16[208,512]{1,0:T(8,128)(2,1)S(1)} %constant_dynamic-slice_fusion.refs_1_), channel_id=1, source_target_pairs={{2,0},{6,2},{10,6},{14,10},{12,14},{8,12},{4,8},{0,4},{3,1},{7,3},... | collective-permute-start | bytes 638984 | tf_op jit(solution)/shard_map/ppermute | solution.py:130
  4.4 12.8 %collective-permute-start = (bf16[208,512]{1,0:T(8,128)(2,1)S(1)}, bf16[208,512]{1,0:T(8,128)(2,1)}, u32[]{:S(2)}, u32[]{:S(2)}) collective-permute-start(bf16[208,512]{1,0:T(8,128)(2,1)S(1)} %constant_dynamic-slice_fusion.refs_1_), channel_id=1, source_target_pairs={{0,2},{2,6},{6,10},{10,14},{14,12},{12,8},{8,4},{4,0},{1,3},{3,7},... | collective-permute-start | bytes 638984 | tf_op jit(solution)/shard_map/ppermute | solution.py:129
  6.3 14.1 %collective-permute-start.5 = (bf16[304,512]{1,0:T(8,128)(2,1)S(1)}, bf16[304,512]{1,0:T(8,128)(2,1)S(1)}, u32[]{:S(2)}, u32[]{:S(2)}) collective-permute-start(bf16[304,512]{1,0:T(8,128)(2,1)S(1)} %constant_dynamic-slice_fusion.1.refs_0_), channel_id=1, source_target_pairs={{2,0},{6,2},{10,6},{14,10},{12,14},{8,12},{4,8},{0,4},{3,1},{7,3},... | collective-permute-start | bytes 933896 | tf_op jit(solution)/shard_map/ppermute | solution.py:130
  12.5 11.2 %collective-permute-start.6 = (bf16[304,512]{1,0:T(8,128)(2,1)S(1)}, bf16[304,512]{1,0:T(8,128)(2,1)S(1)}, u32[]{:S(2)}, u32[]{:S(2)}) collective-permute-start(bf16[304,512]{1,0:T(8,128)(2,1)S(1)} %collective-permute-done.3.refs_2_), channel_id=1, source_target_pairs={{0,2},{2,6},{6,10},{10,14},{14,12},{12,8},{8,4},{4,0},{1,3},{3,7},... | collective-permute-start | bytes 933896 | tf_op jit(solution)/shard_map/ppermute | solution.py:129
  14.5 12.5 %collective-permute-start.7 = (bf16[208,512]{1,0:T(8,128)(2,1)S(1)}, bf16[208,512]{1,0:T(8,128)(2,1)}, u32[]{:S(2)}, u32[]{:S(2)}) collective-permute-start(bf16[208,512]{1,0:T(8,128)(2,1)S(1)} %collective-permute-done.4.refs_3_), channel_id=1, source_target_pairs={{2,0},{6,2},{10,6},{14,10},{12,14},{8,12},{4,8},{0,4},{3,1},{7,3},... | collective-permute-start | bytes 638984 | tf_op jit(solution)/shard_map/ppermute | solution.py:130
  17.2 1.3 %collective-permute-start.1 = (s32[3,1]{0,1:T(1,128)}, s32[3,1]{0,1:T(1,128)S(1)}, u32[]{:S(2)}, u32[]{:S(2)}) collective-permute-start(s32[3,1]{0,1:T(1,128)} %param.10), channel_id=1, source_target_pairs={{0,1},{1,0},{2,3},{3,2},{4,5},{5,4},{6,7},{7,6},{8,9},{9,8},{10,11... | collective-permute-start | bytes 44 | tf_op jit(solution)/shard_map/ppermute | solution.py:142
  18.4 11.3 %collective-permute-start.8 = (bf16[208,512]{1,0:T(8,128)(2,1)}, bf16[208,512]{1,0:T(8,128)(2,1)}, u32[]{:S(2)}, u32[]{:S(2)}) collective-permute-start(bf16[208,512]{1,0:T(8,128)(2,1)} %collective-permute-done.refs_4_), channel_id=1, source_target_pairs={{0,2},{2,6},{6,10},{10,14},{14,12},{12,8},{8,4},{4,0},{1,3},{3,7},... | collective-permute-start | bytes 638984 | tf_op jit(solution)/shard_map/ppermute | solution.py:129
  20.4 11.3 %collective-permute-start.9 = (bf16[304,512]{1,0:T(8,128)(2,1)S(1)}, bf16[304,512]{1,0:T(8,128)(2,1)S(1)}, u32[]{:S(2)}, u32[]{:S(2)}) collective-permute-start(bf16[304,512]{1,0:T(8,128)(2,1)S(1)} %collective-permute-done.5.refs_5_), channel_id=1, source_target_pairs={{2,0},{6,2},{10,6},{14,10},{12,14},{8,12},{4,8},{0,4},{3,1},{7,3},... | collective-permute-start | bytes 933896 | tf_op jit(solution)/shard_map/ppermute | solution.py:130
  23.8 12.0 %collective-permute-start.10 = (bf16[304,512]{1,0:T(8,128)(2,1)S(1)}, bf16[304,512]{1,0:T(8,128)(2,1)S(1)}, u32[]{:S(2)}, u32[]{:S(2)}) collective-permute-start(bf16[304,512]{1,0:T(8,128)(2,1)S(1)} %collective-permute-done.6.refs_6_), channel_id=1, source_target_pairs={{0,2},{2,6},{6,10},{10,14},{14,12},{12,8},{8,4},{4,0},{1,3},{3,7},... | collective-permute-start | bytes 933896 | tf_op jit(solution)/shard_map/ppermute | solution.py:129
  27.0 8.6 %collective-permute-start.11 = (bf16[208,512]{1,0:T(8,128)(2,1)}, bf16[208,512]{1,0:T(8,128)(2,1)}, u32[]{:S(2)}, u32[]{:S(2)}) collective-permute-start(bf16[208,512]{1,0:T(8,128)(2,1)} %collective-permute-done.7.refs_7_), channel_id=1, source_target_pairs={{2,0},{6,2},{10,6},{14,10},{12,14},{8,12},{4,8},{0,4},{3,1},{7,3},... | collective-permute-start | bytes 638984 | tf_op jit(solution)/shard_map/ppermute | solution.py:130
  29.8 11.3 %collective-permute-start.12 = (bf16[208,512]{1,0:T(8,128)(2,1)}, bf16[208,512]{1,0:T(8,128)(2,1)S(1)}, u32[]{:S(2)}, u32[]{:S(2)}) collective-permute-start(bf16[208,512]{1,0:T(8,128)(2,1)} %collective-permute-done.8.refs_8_), channel_id=1, source_target_pairs={{0,2},{2,6},{6,10},{10,14},{14,12},{12,8},{8,4},{4,0},{1,3},{3,7},... | collective-permute-start | bytes 638984 | tf_op jit(solution)/shard_map/ppermute | solution.py:129
  31.7 10.4 %collective-permute-start.13 = (bf16[304,512]{1,0:T(8,128)(2,1)S(1)}, bf16[304,512]{1,0:T(8,128)(2,1)S(1)}, u32[]{:S(2)}, u32[]{:S(2)}) collective-permute-start(bf16[304,512]{1,0:T(8,128)(2,1)S(1)} %collective-permute-done.9.refs_9_), channel_id=1, source_target_pairs={{2,0},{6,2},{10,6},{14,10},{12,14},{8,12},{4,8},{0,4},{3,1},{7,3},... | collective-permute-start | bytes 933896 | tf_op jit(solution)/shard_map/ppermute | solution.py:130
  35.6 9.8 %collective-permute-start.15 = (bf16[208,512]{1,0:T(8,128)(2,1)}, bf16[208,512]{1,0:T(8,128)(2,1)S(1)}, u32[]{:S(2)}, u32[]{:S(2)}) collective-permute-start(bf16[208,512]{1,0:T(8,128)(2,1)} %collective-permute-done.11.refs_1_), channel_id=1, source_target_pairs={{2,0},{6,2},{10,6},{14,10},{12,14},{8,12},{4,8},{0,4},{3,1},{7,3},... | collective-permute-start | bytes 638984 | tf_op jit(solution)/shard_map/ppermute | solution.py:136
  35.7 9.7 %collective-permute-start.14 = (bf16[304,512]{1,0:T(8,128)(2,1)S(1)}, bf16[304,512]{1,0:T(8,128)(2,1)S(1)}, u32[]{:S(2)}, u32[]{:S(2)}) collective-permute-start(bf16[304,512]{1,0:T(8,128)(2,1)S(1)} %collective-permute-done.10.refs_0_), channel_id=1, source_target_pairs={{0,2},{2,6},{6,10},{10,14},{14,12},{12,8},{8,4},{4,0},{1,3},{3,7},... | collective-permute-start | bytes 933896 | tf_op jit(solution)/shard_map/ppermute | solution.py:135
